TPU v7x, 512 devices: a whole 4x4x16 slice. The times are simulated.
512 devices in a mesh: pool: 16 (over y, x_hi, core), batch: 32 (over z, x_lo).
Axes of the slice: x: 4 (x_hi: 2, x_lo: 2; x = x_hi * 2 + x_lo), y: 4, z: 16, core: 2. Of those that a mesh axis runs over, the one named last changes fastest.
Arguments:
- pooled_query_features: bfloat16 [65536, 768], P(('batch', 'pool'))
- item_features: bfloat16 [8192, 768], P(('pool', 'batch'))
- tower_weight: bfloat16 [768, 768], replicated, may hold values from -0.21875 to 0.21875
- item_counts: int32 [8192], P('pool'), may hold values from 1 to 4096
- positives: int32 [65536], P('batch'), may hold values from 0 to 8191
Outputs:
- mean_loss: float32 [], replicated
- weight_grad: float32 [768, 768], replicated
All inputs are finite; a program needn't handle non-finite values.
Results may differ from a plain program's by a relative error of at most 0.015.
Values may be sent and summed in bfloat16 or wider, within the bound.
No kernel may reach another device: no remote copies, remote signals or barrier semaphores. Data moves between devices by JAX's collectives and lax.ppermute only.
A program may use at most 64 MiB of HBM per device.

v0:
```python
import jax
import jax.numpy as jnp
from jax import lax
from jax.sharding import PartitionSpec as P


def tower(feature_matrix, tower_weight):
    proj = jnp.dot(feature_matrix, tower_weight, preferred_element_type=jnp.float32)
    radius = jnp.sqrt(jnp.sum(proj * proj, axis=1, keepdims=True) + 1e-06)
    return (proj / radius, radius)


def back_norm(unit, radius, incoming_gradient):
    inner = jnp.sum(unit * incoming_gradient, axis=1, keepdims=True)
    return (incoming_gradient - unit * inner) / radius


def weight_term(feature_matrix, incoming_gradient):
    return lax.dot_general(
        feature_matrix.astype(jnp.float32),
        incoming_gradient,
        (((0,), (0,)), ((), ())),
        precision=lax.Precision.HIGHEST,
    )


def body(pooled_query_features, item_features, tower_weight, item_counts, positives):
    eq, rq = tower(pooled_query_features, tower_weight)
    ei, ri = tower(item_features, tower_weight)
    query_block = lax.all_gather(eq.astype(jnp.bfloat16), "pool", axis=0, tiled=True)
    item_block = lax.all_gather(ei.astype(jnp.bfloat16), "batch", axis=0, tiled=True)
    n_cols = item_block.shape[0]
    rows_total = positives.shape[0] * lax.axis_size("batch")
    inv_norm = 1.0 / jnp.sqrt(jnp.float32(rows_total))
    scores = 100.0 * lax.dot_general(
        query_block, item_block, (((1,), (1,)), ((), ())), preferred_element_type=jnp.float32
    )
    scores = scores - jnp.log(item_counts.astype(jnp.float32))[None, :]
    col_ids = lax.axis_index("pool") * n_cols + lax.iota(jnp.int32, n_cols)
    hit = col_ids[None, :] == positives[:, None]
    pos_local = jnp.sum(jnp.where(hit, scores, 0.0), axis=1)
    top = lax.pmax(jnp.max(scores, axis=1), "pool")
    total, pos_score = lax.psum(
        (jnp.sum(jnp.exp(scores - top[:, None]), axis=1), pos_local), "pool"
    )
    lse = top + jnp.log(total)
    grad = ((jnp.exp(scores - lse[:, None]) - hit.astype(jnp.float32)) * inv_norm).astype(
        jnp.bfloat16
    )
    own_rows = pooled_query_features.shape[0]
    loss_rows = lax.dynamic_slice_in_dim(
        lse - pos_score, lax.axis_index("pool") * own_rows, own_rows, 0
    )
    loss_part = jnp.sum(loss_rows) / jnp.float32(rows_total)
    item_terms = 100.0 * lax.dot_general(
        grad, query_block, (((0,), (0,)), ((), ())), preferred_element_type=jnp.float32
    )
    query_terms = 100.0 * jnp.dot(grad, item_block, preferred_element_type=jnp.float32)
    dq = lax.psum_scatter(
        query_terms.astype(jnp.bfloat16), "pool", scatter_dimension=0, tiled=True
    ).astype(jnp.float32)
    di = lax.psum_scatter(
        item_terms.astype(jnp.bfloat16), "batch", scatter_dimension=0, tiled=True
    ).astype(jnp.float32)
    dzq = back_norm(eq, rq, dq)
    dzi = back_norm(ei, ri, di)
    weight_part = weight_term(pooled_query_features, dzq) + weight_term(item_features, dzi)
    weight_grad, mean_loss = lax.psum((weight_part, loss_part), ("pool", "batch"))
    return (mean_loss, weight_grad)


def solution(mesh):
    return jax.shard_map(
        body,
        mesh=mesh,
        in_specs=(
            P(("batch", "pool"), None),
            P(("pool", "batch"), None),
            P(),
            P("pool"),
            P("batch"),
        ),
        out_specs=(P(), P()),
        check_vma=False,
    )
```

profile of v0, /device:TPU:1, one launch (start us, length us, event | category | flops | bytes accessed | tf_op | source)
XLA Modules:
  0.0 929.5 jit_solution(2485420876446959509)
XLA Ops:
  7.2 0.0 copy-start
  7.2 0.0 all-gather.2.cloned.1.call-start
  7.2 1.2 copy-done
  8.4 1.3 multiply_reduce_fusion
  9.8 0.0 copy-start.1
  9.8 0.7 copy-done.1
  10.5 0.8 fusion.19
  11.3 0.0 all-gather.2.cloned.1.call-update
  11.3 0.0 reduce-scatter.5.cloned.1.call-start
  11.4 1.1 multiply_reduce_fusion.1
  12.5 0.0 copy-start.2
  12.6 0.7 convert_log_fusion
  13.3 0.1 fusion.18
  13.3 61.2 %all_gather.7 = bf16[512,768]{1,0:T(8,128)(2,1)S(1)} all-gather(bf16[16,768]{1,0:T(8,128)(2,1)S(1)} %fusion.18), channel_id=1, replica_groups=mesh['pool'=16,'batch'=32] {'batch'}, dimensions={0}, use_global_device_ids=true | all-gather | bytes 811008 | tf_op jit(solution)/shard_map/all_gather | solution.py:31
  74.6 0.0 copy-start.3
  74.6 12.1 %all-gather.2.cloned.1.call-done = bf16[2048,768]{1,0:T(8,128)(2,1)} async-done(((bf16[128,768]{1,0:T(8,128)(2,1)}), bf16[2048,768]{1,0:T(8,128)(2,1)}) %all-gather.2.cloned.1.call-update) | async-done | bytes 3145744 | tf_op jit(solution)/shard_map/all_gather | solution.py:30
  86.6 5.6 fusion.22
  92.3 34.4 %pmax.7 = f32[2048]{0:T(1024)S(1)} all-reduce(f32[2048]{0:T(1024)S(1)} %get-tuple-element.12), channel_id=1, replica_groups=mesh['pool'=16,'batch'=32] {'pool'}, use_global_device_ids=true, to_apply=%region_3.4 | all-reduce | flops 2048 | bytes 16384 | tf_op jit(solution)/shard_map/pmax | solution.py:42
  126.7 0.0 copy-done.3
  126.7 3.2 exponential_reduce_fusion
  129.9 59.9 %all-reduce = (f32[2048]{0:T(1024)}, f32[2048]{0:T(1024)S(1)}) all-reduce(f32[2048]{0:T(1024)S(1)} %get-tuple-element.5, f32[2048]{0:T(1024)S(1)} %get-tuple-element.4), channel_id=1, replica_groups=mesh['pool'=16,'batch'=32] {'pool'}, use_global_device_ids=true, to_apply=%region_7.8 | all-reduce | flops 4096 | bytes 32768 | tf_op jit(solution)/shard_map/psum | solution.py:43
  189.9 6.4 multiply_convert_fusion.1
  196.2 0.0 reduce-scatter.5.cloned.1.call-update
  196.2 0.0 reduce-scatter.3.cloned.1.call-start
  196.3 6.1 multiply_convert_fusion
  202.4 0.0 reduce-scatter.3.cloned.1.call-update
  202.4 0.0 all-reduce.3.cloned.1.call-start
  202.5 107.2 %reduce-scatter.5.cloned.1.call-done = bf16[16,768]{1,0:T(8,128)(2,1)} async-done(((bf16[512,768]{1,0:T(8,128)(2,1)}), bf16[16,768]{1,0:T(8,128)(2,1)}) %reduce-scatter.5.cloned.1.call-update) | async-done | bytes 24592 | tf_op jit(solution)/shard_map/reduce_scatter | solution.py:62
  309.7 0.0 copy-done.2
  309.7 0.9 fusion.10
  310.6 2.0 fusion.12
  312.7 122.3 %reduce-scatter.3.cloned.1.call-done = bf16[128,768]{1,0:T(8,128)(2,1)} async-done(((bf16[2048,768]{1,0:T(8,128)(2,1)}), bf16[128,768]{1,0:T(8,128)(2,1)}) %reduce-scatter.3.cloned.1.call-update) | async-done | bytes 196624 | tf_op jit(solution)/shard_map/reduce_scatter | solution.py:59
  435.0 1.3 fusion.4
  436.3 3.8 add_bitcast_fusion
  440.0 0.0 all-reduce.3.cloned.1.call-update
  440.1 1.4 fusion.17
  442.1 105.2 %psum.30 = f32[]{:T(128)} all-reduce(f32[]{:T(128)S(6)} %div.35), channel_id=1, replica_groups=mesh['pool'=16,'batch'=32] {'pool','batch'}, use_global_device_ids=true, to_apply=%region_9.10 | all-reduce | flops 1 | bytes 8 | tf_op jit(solution)/shard_map/psum | solution.py:68
  547.3 372.6 %all-reduce.3.cloned.1.call-done = f32[768,768]{0,1:T(8,128)} async-done(((f32[768,768]{0,1:T(8,128)}), f32[768,768]{0,1:T(8,128)}) %all-reduce.3.cloned.1.call-update) | async-done | bytes 2359312 | tf_op jit(solution)/shard_map/psum | solution.py:68
  919.9 3.0 copy.7
  (4 shorter events, 0.0 us)
Async XLA Ops:
  7.2 1.3 copy-start
  7.2 79.5 %all-gather.2.cloned.1.call-start = ((), (), s32[]{:S(2)}) async-start(), calls=%async_computation.2 | async-start | bytes 3342336 | tf_op jit(solution)/shard_map/all_gather | solution.py:30
  9.8 0.7 copy-start.1
  11.3 298.4 %reduce-scatter.5.cloned.1.call-start = ((), (), s32[]{:S(2)}) async-start(), calls=%async_computation.4 | async-start | bytes 811008 | tf_op jit(solution)/shard_map/reduce_scatter | solution.py:62
  12.5 297.2 %copy-start.2 = (f32[16,768]{1,0:T(8,128)}, f32[16,768]{1,0:T(8,128)S(1)}, u32[]{:S(2)}) copy-start(f32[16,768]{1,0:T(8,128)S(1)} %get-tuple-element.11) | copy-start | bytes 147460
  74.6 52.2 %copy-start.3 = (s32[2048]{0:T(1024)S(1)}, s32[2048]{0:T(1024)}, u32[]{:S(2)}) copy-start(s32[2048]{0:T(1024)} %param.9) | copy-start | bytes 24580
  196.2 238.7 %reduce-scatter.3.cloned.1.call-start = ((), (), s32[]{:S(2)}) async-start(), calls=%async_computation.3 | async-start | bytes 3342336 | tf_op jit(solution)/shard_map/reduce_scatter | solution.py:59
  202.4 717.5 %all-reduce.3.cloned.1.call-start = ((), (), s32[]{:S(2)}) async-start(), calls=%async_computation.5 | async-start | bytes 4718592 | tf_op jit(solution)/shard_map/psum | solution.py:68
Sparse Core Ops, SparseCore 0:
  11.9 74.6 all-gather.1
  196.4 113.3 reduce-scatter.4
  315.4 119.5 reduce-scatter.2
  441.5 478.2 all-reduce.2
where the time goes:
time: 931 us; the launch traced here: 929 us
  waiting for transfers between devices  614 us (66%)
  blocking collectives  261 us (28%)
  matrix products  26.4 us (3%)
  between operations  14.5 us (2%)
    psum x1, waiting for transfers between devices, body(): lax.psum((weight_part, loss_part), ('pool', 'batch'))  373 us
    reduce_scatter x1, waiting for transfers between devices, body(): lax.psum_scatter(query_terms.astype(jnp.bfloat16), 'pool', scatter_dimens...  122 us
    reduce_scatter x1, waiting for transfers between devices, body(): lax.psum_scatter(item_terms.astype(jnp.bfloat16), 'batch', scatter_dimens...  107 us
    psum x1, blocking collectives, body(): lax.psum((weight_part, loss_part), ('pool', 'batch'))  105 us
    all_gather x1, blocking collectives, body(): lax.all_gather(ei.astype(jnp.bfloat16), 'batch', axis=0, tiled=True)  61.2 us
    psum x1, blocking collectives, body(): lax.psum((jnp.sum(jnp.exp(scores - top[:, None]), axis=1), pos_local), 'p...  59.9 us
    pmax x1, blocking collectives, body(): top = lax.pmax(jnp.max(scores, axis=1), 'pool')  34.4 us
  transfers between devices with their start and end apart: 4, of which 4 were waited for; matrix products, arithmetic and copies ran while one was open for 1% of the time, Pallas kernels for 0%

commit v1 on v0

v1 whole, which is shorter than its diff:
```python
import jax
import jax.numpy as jnp
from jax import lax
from jax.sharding import Mesh, PartitionSpec as P

BF = jnp.bfloat16
F32 = jnp.float32
D = 768
YX = ("y", "xh")
ROWS = 65536
INV_NORM = 1.0 / ROWS**0.5


def swap(x, axis):
    return lax.ppermute(x, axis, [(0, 1), (1, 0)])


def pair(x, axis):
    other = swap(x, axis)
    first = lax.axis_index(axis) == 0
    return jnp.stack([jnp.where(first, x, other), jnp.where(first, other, x)])


def exchange(x, axes):
    return lax.all_to_all(x, axes, 0, 0, tiled=True)


def gather(x, axes, n):
    return exchange(jnp.broadcast_to(x[None], (n,) + x.shape), axes)


def tower(features, weight):
    proj = jnp.dot(features, weight, preferred_element_type=F32)
    radius = jnp.sqrt(jnp.sum(proj * proj, axis=1, keepdims=True) + 1e-06)
    return (proj / radius).astype(BF), radius


def back_norm(unit, radius, incoming):
    unit = unit.astype(F32)
    inner = jnp.sum(unit * incoming, axis=1, keepdims=True)
    return ((incoming - unit * inner) / radius).astype(BF)


def dot(a, b, dims):
    return lax.dot_general(a, b, (dims, ((), ())), preferred_element_type=F32)


def split3(x):
    hi = x.astype(BF)
    mid = (x - hi.astype(F32)).astype(BF)
    low = (x - hi.astype(F32) - mid.astype(F32)).astype(BF)
    return jnp.stack([hi, mid, low])


def body(xq_own, xi_own, weight, counts, positives):
    core = lax.axis_index("c")
    xi = gather(pair(xi_own, "xl"), "z", 16).reshape(512, D)
    half = gather(xq_own, YX, 8).reshape(1024, D)
    xq = jnp.concatenate([half, swap(half, "c")], axis=0)
    targets = positives.reshape(8, 2, 128).transpose(1, 0, 2).reshape(2, 1024)
    targets = jnp.where(core == 0, targets, targets[::-1]).reshape(2048)

    eq, rq = tower(xq, weight)
    ei, ri = tower(xi, weight)
    scores = 100.0 * dot(eq, ei, ((1,), (1,))) - jnp.log(counts.astype(F32))[None, :]
    block = (lax.axis_index("y") * 2 + lax.axis_index("xh")) * 2 + core
    hit = (block * 512 + lax.iota(jnp.int32, 512))[None, :] == targets[:, None]
    top = jnp.max(scores, axis=1)
    lse = top + jnp.log(jnp.sum(jnp.exp(scores - top[:, None]), axis=1))
    pos = jnp.sum(jnp.where(hit, scores, 0.0))

    lse = lse.reshape(2, 1024)
    lse = jnp.where(core == 0, lse, lse[::-1])
    mine = jnp.concatenate([lse.reshape(16, 128), jnp.full((8, 128), pos, F32)])
    both = pair(mine, "c")
    lo = jnp.maximum(both[0, :16], both[1, :16])
    merged = lo + jnp.log(jnp.exp(both[0, :16] - lo) + jnp.exp(both[1, :16] - lo))
    merged = jnp.concatenate([merged, both[0, 16:] + both[1, 16:]])
    parts = gather(merged, YX, 8)
    tops = jnp.max(parts[:, :16], axis=0)
    lse = tops + jnp.log(jnp.sum(jnp.exp(parts[:, :16] - tops[None]), axis=0))
    loss = (jnp.sum(lse) - jnp.sum(parts[:, 16, 0])) / ROWS
    lse = lse.reshape(2, 1024)
    lse = jnp.where(core == 0, lse, lse[::-1]).reshape(2048)

    grad = ((jnp.exp(scores - lse[:, None]) - hit.astype(F32)) * INV_NORM).astype(BF)
    dzq = back_norm(eq, rq, 100.0 * dot(grad, ei, ((1,), (0,))))
    dzi = back_norm(ei, ri, 100.0 * dot(grad, eq, ((0,), (0,))))
    part = dot(xq, dzq, ((0,), (0,))) + dot(xi, dzi, ((0,), (0,)))

    part = part.astype(BF).reshape(2, 384, D)
    keep = jnp.where(core == 0, part[0], part[1])
    send = jnp.where(core == 0, part[1], part[0])
    s = (keep.astype(F32) + swap(send, "c").astype(F32)).astype(BF)
    s = jnp.sum(exchange(s.reshape(8, 48, D), YX).astype(F32), axis=0).astype(BF)
    s = s.reshape(32, 9, 128)
    tail = jnp.zeros((32, 1, 128), BF).at[:, 0, :3].set(split3(loss)[None])
    s = exchange(jnp.concatenate([s, tail], axis=1), ("z", "xl"))
    s = jnp.sum(s.astype(F32), axis=0)
    mean_loss = jnp.sum(s[9, :3])
    s = gather(s[:9].astype(BF), ("z", "xl"), 32).reshape(48, D)
    s = gather(s, YX, 8).reshape(384, D)
    return mean_loss, pair(s, "c").reshape(D, D).astype(F32)


def solution(mesh):
    fine = Mesh(mesh.devices.reshape(4, 2, 2, 16, 2), ("y", "xh", "c", "z", "xl"))
    pool, batch = ("y", "xh", "c"), ("z", "xl")
    return jax.shard_map(
        body,
        mesh=fine,
        in_specs=(P(batch + pool, None), P(pool + batch, None), P(), P(pool), P(batch)),
        out_specs=(P(), P()),
        check_vma=False,
    )
```

time: 931 us -> 225 us (0.24)
  waiting for transfers between devices: 614 us -> 57.8 us
  blocking collectives: 261 us -> 63 us
  starting transfers between devices: 0.16 us -> 49.1 us
  between operations: 14.5 us -> 2.48 us
  local copies, waits for them, and re-layouts: 5 us -> 15.2 us
    psum x1 -> x0, waiting for transfers between devices: 373 us -> none  [body(): lax.psum((weight_part, loss_part), ('pool', 'batch'))]
    reduce_scatter x2 -> x0, waiting for transfers between devices: 230 us -> none  [the longest x1 122 us: body(): lax.psum_scatter(query_terms.astype(jnp.bfloat16), 'pool', scatter_dimens...]
    psum x2 -> x0, blocking collectives: 165 us -> none  [the longest x1 105 us: body(): lax.psum((weight_part, loss_part), ('pool', 'batch'))]
    all_to_all x0 -> x4, blocking collectives: none -> 63 us  [exchange(): return lax.all_to_all(x, axes, 0, 0, tiled=True)]
    all_gather x1 -> x0, blocking collectives: 61.2 us -> none  [body(): lax.all_gather(ei.astype(jnp.bfloat16), 'batch', axis=0, tiled=True)]
    all_to_all x0 -> x3, waiting for transfers between devices: none -> 54.4 us  [exchange(): return lax.all_to_all(x, axes, 0, 0, tiled=True)]
    pmax x1 -> x0, blocking collectives: 34.4 us -> none  [body(): top = lax.pmax(jnp.max(scores, axis=1), 'pool')]
    all_to_all x0 -> x3, starting transfers between devices: none -> 26.1 us  [exchange(): return lax.all_to_all(x, axes, 0, 0, tiled=True)]
  transfers between devices with their start and end apart: 4 -> 8, of which waited for: 4 -> 6; matrix products, arithmetic and copies ran while one was open for 1% -> 5% of each run, Pallas kernels for 0% -> 0%
where the time goes in v1:
time: 225 us; the launch traced here: 224 us
  blocking collectives  63 us (28%)
  waiting for transfers between devices  57.8 us (26%)
  starting transfers between devices  49.1 us (22%)
  matrix products  20.7 us (9%)
  other arithmetic  15.4 us (7%)
  local copies, waits for them, and re-layouts  15.2 us (7%)
  between operations  2.48 us (1%)
    all_to_all x4, blocking collectives, exchange(): return lax.all_to_all(x, axes, 0, 0, tiled=True)  63 us
    all_to_all x3, waiting for transfers between devices, exchange(): return lax.all_to_all(x, axes, 0, 0, tiled=True)  54.4 us
    all_to_all x3, starting transfers between devices, exchange(): return lax.all_to_all(x, axes, 0, 0, tiled=True)  26.1 us
    ppermute x5, starting transfers between devices, swap(): return lax.ppermute(x, axis, [(0, 1), (1, 0)])  23 us
    dot_general x5, matrix products, dot(): return lax.dot_general(a, b, (dims, ((), ())), preferred_element_type=F32)  15.6 us
    dot_general x2, matrix products, tower(): proj = jnp.dot(features, weight, preferred_element_type=F32)  5.06 us
  transfers between devices with their start and end apart: 8, of which 6 were waited for; matrix products, arithmetic and copies ran while one was open for 5% of the time, Pallas kernels for 0%

profile of v1, /device:TPU:1, one launch (start us, length us, event | category | flops | bytes accessed | tf_op | source)
XLA Modules:
  0.0 223.7 jit_solution(1946981934044783582)
XLA Ops:
  0.6 0.0 copy-start
  0.7 2.3 %broadcast_in_dim.16 = bf16[8,128,768]{2,1,0:T(8,128)(2,1)} broadcast(bf16[128,768]{1,0:T(8,128)(2,1)} %param.7), dimensions={1,2} | broadcast | bytes 1769472 | tf_op jit(solution)/shard_map/broadcast_in_dim | solution.py:29
  2.9 7.6 %all-to-all-start = ((bf16[8,128,768]{2,1,0:T(8,128)(2,1)}), bf16[8,128,768]{2,1,0:T(8,128)(2,1)S(1)}, u32[]{:S(2)}, u32[]{:S(2)}) async-start(bf16[8,128,768]{2,1,0:T(8,128)(2,1)} %broadcast_in_dim.16), calls=%async_computation | async-start | bytes 3145728 | tf_op jit(solution)/shard_map/all_to_all | solution.py:25
  10.5 2.2 collective-permute-start.1
  12.8 17.4 %all-to-all-done = bf16[8,128,768]{2,1,0:T(8,128)(2,1)S(1)} async-done(((bf16[8,128,768]{2,1,0:T(8,128)(2,1)}), bf16[8,128,768]{2,1,0:T(8,128)(2,1)S(1)}, u32[]{:S(2)}, u32[]{:S(2)}) %all-to-all-start) | async-done | bytes 1572896 | tf_op jit(solution)/shard_map/all_to_all | solution.py:25
  30.2 6.3 %collective-permute-start = (bf16[1024,768]{1,0:T(8,128)(2,1)S(1)}, bf16[1024,768]{1,0:T(8,128)(2,1)}, u32[]{:S(2)}, u32[]{:S(2)}) collective-permute-start(bf16[1024,768]{1,0:T(8,128)(2,1)S(1)} %bitcast.58), channel_id=1, source_target_pairs={{0,32},{32,0},{1,33},{33,1},{2,34},{34,2},{3,35},{35,3},{4,36},{36... | collective-permute-start | bytes 4718600 | tf_op jit(solution)/shard_map/ppermute | solution.py:15
  36.5 0.0 collective-permute-done.1
  36.5 1.0 broadcast_in_dim.17
  37.5 14.9 %all-to-all-start.1 = ((bf16[16,2,16,768]{3,2,1,0:T(8,128)(2,1)}), bf16[16,2,16,768]{3,2,1,0:T(8,128)(2,1)S(1)}, u32[]{:S(2)}, u32[]{:S(2)}) async-start(bf16[16,2,16,768]{3,2,1,0:T(8,128)(2,1)} %broadcast_in_dim.17), calls=%async_computation.1 | async-start | bytes 1572864 | tf_op jit(solution)/shard_map/all_to_all | solution.py:25
  52.4 0.2 rev.10
  52.7 0.7 convert_log_fusion
  53.4 0.0 collective-permute-done
  53.4 4.2 %multiply_reduce_fusion = (f32[2048]{0:T(1024)S(1)}, f32[2048,768]{0,1:T(8,128)S(1)}) fusion(bf16[768,768]{1,0:T(8,128)(2,1)S(1)} %copy-done, bf16[1024,768]{1,0:T(8,128)(2,1)} %collective-permute-done, bf16[1024,768]{1,0:T(8,128)(2,1)S(1)} %bitcast.59), kind=kOutput, calls=%fused_computation.7 | convolution fusion | flops 2425354240 | bytes 10625024 | tf_op jit(solution)/shard_map/dot_general | solution.py:33
  57.6 0.6 copy-done.9
  58.2 2.5 %divide_convert_fusion = bf16[2048,768]{0,1:T(8,128)(2,1)} fusion(f32[2048,768]{0,1:T(8,128)S(1)} %get-tuple-element.27, f32[2048]{0:T(1024)S(1)} %add_sqrt_fusion), kind=kLoop, calls=%fused_computation.6 | loop fusion | flops 3145728 | bytes 9445376 | tf_op jit(solution)/shard_map/convert_element_type | solution.py:35
  60.8 28.2 %all-to-all-done.1 = bf16[16,2,16,768]{3,2,1,0:T(8,128)(2,1)S(1)} async-done(((bf16[16,2,16,768]{3,2,1,0:T(8,128)(2,1)}), bf16[16,2,16,768]{3,2,1,0:T(8,128)(2,1)S(1)}, u32[]{:S(2)}, u32[]{:S(2)}) %all-to-all-start.1) | async-done | bytes 786464 | tf_op jit(solution)/shard_map/all_to_all | solution.py:25
  89.0 0.9 multiply_reduce_fusion.1
  89.8 0.6 copy-done.14
  90.4 0.2 divide_convert_fusion.1
  90.6 0.2 copy-done.3
  90.9 1.8 fusion.30
  92.7 1.9 copy-done.1
  94.6 2.2 fusion.4
  96.8 0.6 log_add_fusion.2
  97.4 0.7 add.81
  98.1 2.4 %rev.9 = f32[2,1024]{1,0:T(2,128)} reverse(f32[2,1024]{1,0:T(2,128)S(1)} %add.81), dimensions={0} | reverse | bytes 16384 | tf_op jit(solution)/shard_map/rev | solution.py:73
  100.5 1.3 broadcast_select_fusion.1
  101.8 0.7 reshape.116
  102.5 0.6 concatenate.15
  103.1 4.9 %collective-permute-start.2 = (f32[24,128]{1,0:T(8,128)S(1)}, f32[24,128]{1,0:T(8,128)S(1)}, u32[]{:S(2)}, u32[]{:S(2)}) collective-permute-start(f32[24,128]{1,0:T(8,128)S(1)} %concatenate.15), channel_id=1, source_target_pairs={{0,32},{32,0},{1,33},{33,1},{2,34},{34,2},{3,35},{35,3},{4,36},{36... | collective-permute-start | bytes 36872 | tf_op jit(solution)/shard_map/ppermute | solution.py:15
  108.1 0.8 collective-permute-done.2
  108.9 0.6 select_bitcast_fusion.5
  109.6 9.3 %all_to_all.35 = f32[8,24,128]{2,1,0:T(8,128)S(1)} all-to-all(f32[8,24,128]{2,1,0:T(8,128)S(1)} %broadcast_in_dim.19), channel_id=1, replica_groups=mesh['y'=4,'xh'=2,'c'=2,'z'=16,'xl'=2] {'y','xh'}, dimensions={0} | all-to-all | bytes 196608 | tf_op jit(solution)/shard_map/all_to_all | solution.py:25
  118.9 0.6 copy-done.7
  119.5 1.2 fusion.29
  120.7 0.7 add.91
  121.4 2.3 %rev.11 = f32[2,1024]{1,0:T(2,128)} reverse(f32[2,1024]{1,0:T(2,128)S(1)} %add.91), dimensions={0} | reverse | bytes 16384 | tf_op jit(solution)/shard_map/rev | solution.py:84
  123.7 0.7 select_bitcast_fusion.6
  124.5 0.0 copy-start.6
  124.5 5.9 %fusion.11 = (f32[512]{0:T(512)S(1)}, f32[512,768]{1,0:T(8,128)S(1)}) fusion(bf16[512,768]{1,0:T(8,128)(2,1)} %copy-done.5, bf16[2048,768]{0,1:T(8,128)(2,1)} %divide_convert_fusion, f32[2048,512]{0,1:T(8,128)} %copy-done.1, f32[2048]{0:T(1024)S(1)} %bitcast.68, s32[2048]{0:T(1024)S(1)} %bitcast.64, s32[512]{0:T(512)} %copy-done.12), kind=kOutput, calls=%fused_computation.22 | convolution fusion | flops 1618476544 | bytes 9719808 | tf_op jit(solution)/shard_map/dot_general | solution.py:45
  130.4 2.7 %fusion = (f32[2048]{0:T(1024)S(1)}, f32[2048,768]{0,1:T(8,128)S(1)}) fusion(bf16[2048,768]{0,1:T(8,128)(2,1)S(1)} %copy-done.4, bf16[512,768]{1,0:T(8,128)(2,1)S(1)} %copy-done.6, f32[2048,512]{0,1:T(8,128)S(1)} %copy-done.2, f32[2048]{0:T(1024)S(1)} %bitcast.69, s32[2048]{0:T(1024)S(1)} %bitcast.65, s32[512]{0:T(512)S(1)} %copy-done.13), kind=kOutput, calls=%fused_computation.2 | convolution fusion | flops 1623193600 | bytes 14444544 | tf_op jit(solution)/shard_map/dot_general | solution.py:45
  133.1 1.0 fusion.17
  134.1 4.3 %add_convert_fusion = bf16[768,768]{1,0:T(8,128)(2,1)S(1)} fusion(f32[768,768]{1,0:T(8,128)S(1)} %fusion.17, bf16[2048,768]{0,1:T(8,128)(2,1)S(1)} %copy-done.4, f32[2048,768]{0,1:T(8,128)S(1)} %get-tuple-element.33, f32[2048]{0:T(1024)S(1)} %get-tuple-element.32, f32[2048]{0:T(1024)S(1)} %copy-done.10, bf16[1024,768]{1,0:T(8,128)(2,1)} %collective-permute-done, ...), kind=kOutput, calls=%fused_computation.18 | convolution fusion | flops 2432827392 | bytes 16138240 | tf_op jit(solution)/shard_map/dot_general | solution.py:45
  138.4 0.1 broadcast_select_fusion
  138.5 2.7 %collective-permute-start.3 = (bf16[384,768]{1,0:T(8,128)(2,1)S(1)}, bf16[384,768]{1,0:T(8,128)(2,1)S(1)}, u32[]{:S(2)}, u32[]{:S(2)}) collective-permute-start(bf16[384,768]{1,0:T(8,128)(2,1)S(1)} %broadcast_select_fusion), channel_id=1, source_target_pairs={{0,32},{32,0},{1,33},{33,1},{2,34},{34,2},{3,35},{35,3},{4,36},{36... | collective-permute-start | bytes 1769480 | tf_op jit(solution)/shard_map/ppermute | solution.py:15
  141.2 1.6 collective-permute-done.3
  142.8 1.0 add_convert_fusion.1
  143.9 3.5 %all-to-all-start.3 = ((bf16[8,48,768]{2,1,0:T(8,128)(2,1)}), bf16[8,48,768]{2,1,0:T(8,128)(2,1)S(1)}, u32[]{:S(2)}, u32[]{:S(2)}) async-start(bf16[8,48,768]{2,1,0:T(8,128)(2,1)} %bitcast.14), calls=%async_computation.3 | async-start | bytes 1179648 | tf_op jit(solution)/shard_map/all_to_all | solution.py:25
  147.4 1.5 slice_reduce_fusion.1
  150.2 0.1 select_maximum_fusion
  150.3 8.8 %all-to-all-done.3 = bf16[8,48,768]{2,1,0:T(8,128)(2,1)S(1)} async-done(((bf16[8,48,768]{2,1,0:T(8,128)(2,1)}), bf16[8,48,768]{2,1,0:T(8,128)(2,1)S(1)}, u32[]{:S(2)}, u32[]{:S(2)}) %all-to-all-start.3) | async-done | bytes 589856 | tf_op jit(solution)/shard_map/all_to_all | solution.py:25
  159.1 0.1 reduce_sum.118
  159.2 0.1 reshape.120
  159.3 0.1 pad_maximum_fusion.6
  159.4 21.1 %all_to_all.36 = bf16[32,10,128]{2,1,0:T(8,128)(2,1)S(1)} all-to-all(bf16[32,10,128]{2,1,0:T(8,128)(2,1)S(1)} %pad_maximum_fusion.6), channel_id=1, replica_groups=mesh['y'=4,'xh'=2,'c'=2,'z'=16,'xl'=2] {'z','xl'}, dimensions={0} | all-to-all | bytes 163840 | tf_op jit(solution)/shard_map/all_to_all | solution.py:25
  180.5 18.8 %all_to_all.37 = bf16[32,9,128]{2,1,0:T(8,128)(2,1)S(1)} all-to-all(bf16[32,9,128]{2,1,0:T(8,128)(2,1)S(1)} %broadcast_in_dim.20), channel_id=1, replica_groups=mesh['y'=4,'xh'=2,'c'=2,'z'=16,'xl'=2] {'z','xl'}, dimensions={0} | all-to-all | bytes 147456 | tf_op jit(solution)/shard_map/all_to_all | solution.py:25
  199.3 0.1 broadcast_in_dim.21
  199.5 13.9 %all_to_all.38 = bf16[8,48,768]{2,1,0:T(8,128)(2,1)S(1)} all-to-all(bf16[8,48,768]{2,1,0:T(8,128)(2,1)S(1)} %broadcast_in_dim.22), channel_id=1, replica_groups=mesh['y'=4,'xh'=2,'c'=2,'z'=16,'xl'=2] {'y','xh'}, dimensions={0} | all-to-all | bytes 1179648 | tf_op jit(solution)/shard_map/all_to_all | solution.py:25
  213.3 6.9 %collective-permute-start.4 = (bf16[384,768]{1,0:T(8,128)(2,1)S(1)}, bf16[384,768]{1,0:T(8,128)(2,1)S(1)}, u32[]{:S(2)}, u32[]{:S(2)}) collective-permute-start(bf16[384,768]{1,0:T(8,128)(2,1)S(1)} %bitcast.57), channel_id=1, source_target_pairs={{0,32},{32,0},{1,33},{33,1},{2,34},{34,2},{3,35},{35,3},{4,36},{36... | collective-permute-start | bytes 1769480 | tf_op jit(solution)/shard_map/ppermute | solution.py:15
  220.2 0.6 slice_reduce_fusion.2
  220.8 1.0 collective-permute-done.4
  221.8 0.1 select_bitcast_fusion.1
  221.9 0.1 pad_maximum_fusion.5
  222.1 1.7 bitcast_convert_fusion
  (44 shorter events, 0.3 us)
Async XLA Ops:
  0.6 52.8 %copy-start = (bf16[768,768]{1,0:T(8,128)(2,1)S(1)}, bf16[768,768]{1,0:T(8,128)(2,1)}, u32[]{:S(2)}) copy-start(bf16[768,768]{1,0:T(8,128)(2,1)} %param.9) | copy-start | bytes 3538948
  0.6 9.9 %copy-start.11 = (bf16[16,768]{1,0:T(8,128)(2,1)S(1)}, bf16[16,768]{1,0:T(8,128)(2,1)}, u32[]{:S(2)}) copy-start(bf16[16,768]{1,0:T(8,128)(2,1)} %param.8) | copy-start | bytes 73732
  2.9 49.5 %copy-start.8 = (s32[2048]{0:T(1024)S(1)}, s32[2048]{0:T(1024)}, u32[]{:S(2)}) copy-start(s32[2048]{0:T(1024)} %param.11) | copy-start | bytes 24580
  2.9 27.2 %all-to-all-start = ((bf16[8,128,768]{2,1,0:T(8,128)(2,1)}), bf16[8,128,768]{2,1,0:T(8,128)(2,1)S(1)}, u32[]{:S(2)}, u32[]{:S(2)}) async-start(bf16[8,128,768]{2,1,0:T(8,128)(2,1)} %broadcast_in_dim.16), calls=%async_computation | async-start | bytes 3145728 | tf_op jit(solution)/shard_map/all_to_all | solution.py:25
  10.5 25.9 %collective-permute-start.1 = (bf16[16,768]{1,0:T(8,128)(2,1)S(1)}, bf16[16,768]{1,0:T(8,128)(2,1)S(1)}, u32[]{:S(2)}, u32[]{:S(2)}) collective-permute-start(bf16[16,768]{1,0:T(8,128)(2,1)S(1)} %copy-done.11), channel_id=1, source_target_pairs={{0,1},{1,0},{2,3},{3,2},{4,5},{5,4},{6,7},{7,6},{8,9},{9,8},{10,11... | collective-permute-start | bytes 73736 | tf_op jit(solution)/shard_map/ppermute | solution.py:15
  30.2 23.2 %collective-permute-start = (bf16[1024,768]{1,0:T(8,128)(2,1)S(1)}, bf16[1024,768]{1,0:T(8,128)(2,1)}, u32[]{:S(2)}, u32[]{:S(2)}) collective-permute-start(bf16[1024,768]{1,0:T(8,128)(2,1)S(1)} %bitcast.58), channel_id=1, source_target_pairs={{0,32},{32,0},{1,33},{33,1},{2,34},{34,2},{3,35},{35,3},{4,36},{36... | collective-permute-start | bytes 4718600 | tf_op jit(solution)/shard_map/ppermute | solution.py:15
  37.5 51.5 %all-to-all-start.1 = ((bf16[16,2,16,768]{3,2,1,0:T(8,128)(2,1)}), bf16[16,2,16,768]{3,2,1,0:T(8,128)(2,1)S(1)}, u32[]{:S(2)}, u32[]{:S(2)}) async-start(bf16[16,2,16,768]{3,2,1,0:T(8,128)(2,1)} %broadcast_in_dim.17), calls=%async_computation.1 | async-start | bytes 1572864 | tf_op jit(solution)/shard_map/all_to_all | solution.py:25
  52.7 40.0 %copy-start.12 = (s32[512]{0:T(512)}, s32[512]{0:T(512)S(1)}, u32[]{:S(2)}) copy-start(s32[512]{0:T(512)S(1)} %iota_add_fusion) | copy-start | bytes 6148
  57.6 0.6 copy-start.9
  89.0 1.9 copy-start.3
  89.8 0.6 copy-start.14
  90.9 1.8 copy-start.5
  92.7 1.9 copy-start.1
  103.1 5.7 %collective-permute-start.2 = (f32[24,128]{1,0:T(8,128)S(1)}, f32[24,128]{1,0:T(8,128)S(1)}, u32[]{:S(2)}, u32[]{:S(2)}) collective-permute-start(f32[24,128]{1,0:T(8,128)S(1)} %concatenate.15), channel_id=1, source_target_pairs={{0,32},{32,0},{1,33},{33,1},{2,34},{34,2},{3,35},{35,3},{4,36},{36... | collective-permute-start | bytes 36872 | tf_op jit(solution)/shard_map/ppermute | solution.py:15
  118.9 0.6 copy-start.7
  124.5 5.9 %copy-start.2 = (f32[2048,512]{0,1:T(8,128)S(1)}, f32[2048,512]{0,1:T(8,128)}, u32[]{:S(2)}) copy-start(f32[2048,512]{0,1:T(8,128)} %copy-done.1) | copy-start | bytes 12582916
  124.5 5.9 %copy-start.4 = (bf16[2048,768]{0,1:T(8,128)(2,1)S(1)}, bf16[2048,768]{0,1:T(8,128)(2,1)}, u32[]{:S(2)}) copy-start(bf16[2048,768]{0,1:T(8,128)(2,1)} %divide_convert_fusion) | copy-start | bytes 9437188
  124.5 5.9 %copy-start.6 = (bf16[512,768]{1,0:T(8,128)(2,1)S(1)}, bf16[512,768]{1,0:T(8,128)(2,1)}, u32[]{:S(2)}) copy-start(bf16[512,768]{1,0:T(8,128)(2,1)} %copy-done.5) | copy-start | bytes 2359300
  124.5 5.9 %copy-start.13 = (s32[512]{0:T(512)S(1)}, s32[512]{0:T(512)}, u32[]{:S(2)}) copy-start(s32[512]{0:T(512)} %copy-done.12) | copy-start | bytes 6148
  130.4 2.7 %copy-start.15 = (f32[512]{0:T(512)S(1)}, f32[512]{0:T(512)}, u32[]{:S(2)}) copy-start(f32[512]{0:T(512)} %copy-done.14) | copy-start | bytes 6148
  133.1 1.0 copy-start.10
  138.5 4.3 %collective-permute-start.3 = (bf16[384,768]{1,0:T(8,128)(2,1)S(1)}, bf16[384,768]{1,0:T(8,128)(2,1)S(1)}, u32[]{:S(2)}, u32[]{:S(2)}) collective-permute-start(bf16[384,768]{1,0:T(8,128)(2,1)S(1)} %broadcast_select_fusion), channel_id=1, source_target_pairs={{0,32},{32,0},{1,33},{33,1},{2,34},{34,2},{3,35},{35,3},{4,36},{36... | collective-permute-start | bytes 1769480 | tf_op jit(solution)/shard_map/ppermute | solution.py:15
  143.9 15.2 %all-to-all-start.3 = ((bf16[8,48,768]{2,1,0:T(8,128)(2,1)}), bf16[8,48,768]{2,1,0:T(8,128)(2,1)S(1)}, u32[]{:S(2)}, u32[]{:S(2)}) async-start(bf16[8,48,768]{2,1,0:T(8,128)(2,1)} %bitcast.14), calls=%async_computation.3 | async-start | bytes 1179648 | tf_op jit(solution)/shard_map/all_to_all | solution.py:25
  213.3 8.5 %collective-permute-start.4 = (bf16[384,768]{1,0:T(8,128)(2,1)S(1)}, bf16[384,768]{1,0:T(8,128)(2,1)S(1)}, u32[]{:S(2)}, u32[]{:S(2)}) collective-permute-start(bf16[384,768]{1,0:T(8,128)(2,1)S(1)} %bitcast.57), channel_id=1, source_target_pairs={{0,32},{32,0},{1,33},{33,1},{2,34},{34,2},{3,35},{35,3},{4,36},{36... | collective-permute-start | bytes 1769480 | tf_op jit(solution)/shard_map/ppermute | solution.py:15

commit v2 on v1

v2 whole, which is shorter than its diff:
```python
import functools

import jax
import jax.numpy as jnp
from jax import lax
from jax.experimental import pallas as pl
from jax.experimental.pallas import tpu as pltpu
from jax.sharding import Mesh, PartitionSpec as P

BF = jnp.bfloat16
F32 = jnp.float32
D = 768
YX = ("y", "xh")
YXX = ("y", "xh", "xl")
POOL = ("y", "xh", "c")
ROWS = 65536
QB = 2048
IB = 512
HALF = 1024
CH = 512
INV_NORM = 1.0 / ROWS**0.5


def swap(x, axis):
    return lax.ppermute(x, axis, [(0, 1), (1, 0)])


def flip(x, k):
    return lax.ppermute(x, "z", [(i, i ^ k) for i in range(16)])


def exchange(x, axes):
    return lax.all_to_all(x, axes, 0, 0, tiled=True)


def gather(x, axes, n):
    return exchange(jnp.broadcast_to(x[None], (n,) + x.shape), axes)


def dot(a, b, dims):
    return lax.dot_general(a, b, (dims, ((), ())), preferred_element_type=F32)


def split3(x):
    hi = x.astype(BF)
    mid = (x - hi.astype(F32)).astype(BF)
    low = (x - hi.astype(F32) - mid.astype(F32)).astype(BF)
    return jnp.stack([hi, mid, low])


def unit_rows(x, weight):
    proj = dot(x, weight, ((1,), (0,)))
    inv = 1.0 / jnp.sqrt(jnp.sum(proj * proj, axis=1, keepdims=True) + 1e-06)
    return (proj * inv).astype(BF), inv


def tower_kernel(x_ref, w_ref, after_ref, e_ref, inv_ref):
    e_ref[...], inv_ref[...] = unit_rows(x_ref[...], w_ref[...])


def tower(x, weight, after, step):
    n = x.shape[0]
    return pl.pallas_call(
        tower_kernel,
        grid=(n // step,),
        in_specs=[
            pl.BlockSpec((step, D), lambda i: (i, 0)),
            pl.BlockSpec((D, D), lambda i: (0, 0)),
            pl.BlockSpec((16, 128), lambda i: (0, 0)),
        ],
        out_specs=[
            pl.BlockSpec((step, D), lambda i: (i, 0)),
            pl.BlockSpec((step, 1), lambda i: (i, 0)),
        ],
        out_shape=[jax.ShapeDtypeStruct((n, D), BF), jax.ShapeDtypeStruct((n, 1), F32)],
        compiler_params=pltpu.CompilerParams(vmem_limit_bytes=16 << 20),
        cost_estimate=pl.CostEstimate(flops=2 * n * D * D, bytes_accessed=4 * n * D, transcendentals=n),
        name="tower",
    )(x, weight, after)


def score_kernel(own_ref, other_ref, xi_ref, w_ref, logc_ref, ids_ref, tgt_ref,
                 ei_ref, invi_ref, exp_ref, top_ref, stat_ref):
    i = pl.program_id(0)

    @pl.when(i == 0)
    def _():
        ei_ref[...], invi_ref[...] = unit_rows(xi_ref[...], w_ref[...])
        stat_ref[2] = jnp.zeros_like(stat_ref[2])

    def run(eq):
        scores = 100.0 * dot(ei_ref[...], eq, ((1,), (1,))) - logc_ref[...]
        top = jnp.max(scores, axis=0, keepdims=True)
        e = jnp.exp(scores - top)
        exp_ref[...] = e
        top_ref[...] = top
        lse = top + jnp.log(jnp.sum(e, axis=0, keepdims=True))
        hit = ids_ref[...] == tgt_ref[...]
        pos = jnp.sum(jnp.where(hit, scores, 0.0), axis=0, keepdims=True)
        lanes = pl.ds(pl.multiple_of((i % 2) * CH, CH), CH)
        stat_ref[i // 2, :, lanes] = lse
        stat_ref[2, :, lanes] = stat_ref[2, :, lanes] + pos

    @pl.when(i < 2)
    def _():
        run(own_ref[...])

    @pl.when(i >= 2)
    def _():
        run(other_ref[...])


def score(own, other, xi, weight, logc, ids, targets):
    whole = lambda *s: pl.BlockSpec(s, lambda i: (0,) * len(s))
    return pl.pallas_call(
        score_kernel,
        grid=(QB // CH,),
        in_specs=[
            pl.BlockSpec((CH, D), lambda i: (jnp.minimum(i, 1), 0)),
            pl.BlockSpec((CH, D), lambda i: (jnp.maximum(i - 2, 0), 0)),
            whole(IB, D),
            whole(D, D),
            whole(IB, 1),
            whole(IB, 1),
            pl.BlockSpec((1, CH), lambda i: (0, i)),
        ],
        out_specs=[
            whole(IB, D),
            whole(IB, 1),
            pl.BlockSpec((IB, CH), lambda i: (0, i)),
            pl.BlockSpec((1, CH), lambda i: (0, i)),
            whole(3, 1, HALF),
        ],
        out_shape=[
            jax.ShapeDtypeStruct((IB, D), BF),
            jax.ShapeDtypeStruct((IB, 1), F32),
            jax.ShapeDtypeStruct((IB, QB), F32),
            jax.ShapeDtypeStruct((1, QB), F32),
            jax.ShapeDtypeStruct((3, 1, HALF), F32),
        ],
        compiler_params=pltpu.CompilerParams(vmem_limit_bytes=24 << 20),
        cost_estimate=pl.CostEstimate(
            flops=2 * IB * D * (D + QB), bytes_accessed=10 << 20, transcendentals=IB * QB
        ),
        name="score",
    )(own, other, xi, weight, logc, ids, targets)


def grad_kernel(core_ref, parts_ref, exp_ref, top_ref, eqa_ref, eqb_ref, inva_ref, invb_ref, xqa_ref, xqb_ref,
                ei_ref, invi_ref, xi_ref, ids_ref, tgt_ref,
                send_ref, keep_ref, loss_ref, lse_ref, di_ref, acc_ref):
    i = pl.program_id(0)
    core = core_ref[0]

    @pl.when(i == 0)
    def _():
        total = jnp.zeros((1, HALF), F32)
        for h in range(2):
            vals = []
            for d in range(8):
                vals.append(parts_ref[2 * d + core, h])
                vals.append(parts_ref[2 * d + 1 - core, 1 - h])
            top = functools.reduce(jnp.maximum, vals)
            lse = top + jnp.log(sum(jnp.exp(v - top) for v in vals))
            lse_ref[h] = lse
            total = total + lse
        for d in range(16):
            total = total - parts_ref[d, 2]
        loss_ref[...] = jnp.broadcast_to(jnp.sum(total, axis=1, keepdims=True), (8, 128))
        di_ref[...] = jnp.zeros_like(di_ref)
        acc_ref[...] = jnp.zeros_like(acc_ref)

    def run(eq_ref, inv_ref, xq_ref):
        lanes = pl.ds(pl.multiple_of((i % 2) * CH, CH), CH)
        scale = jnp.exp(top_ref[...] - lse_ref[i // 2, :, lanes])
        hit = ids_ref[...] == tgt_ref[...]
        grad = ((exp_ref[...] * scale - jnp.where(hit, 1.0, 0.0)) * INV_NORM).astype(BF)
        eq = eq_ref[...]
        di_ref[...] += dot(grad, eq, ((1,), (0,)))
        dq = 100.0 * dot(grad, ei_ref[...], ((0,), (0,)))
        eq = eq.astype(F32)
        inner = jnp.sum(eq * dq, axis=1, keepdims=True)
        dz = ((dq - eq * inner) * inv_ref[...]).astype(BF)
        acc_ref[...] += dot(xq_ref[...], dz, ((0,), (0,)))

    @pl.when(i < 2)
    def _():
        run(eqa_ref, inva_ref, xqa_ref)

    @pl.when(i >= 2)
    def _():
        run(eqb_ref, invb_ref, xqb_ref)

    @pl.when(i == QB // CH - 1)
    def _():
        di = 100.0 * di_ref[...]
        ei = ei_ref[...].astype(F32)
        inner = jnp.sum(ei * di, axis=1, keepdims=True)
        dz = ((di - ei * inner) * invi_ref[...]).astype(BF)
        acc_ref[...] += dot(xi_ref[...], dz, ((0,), (0,)))
        mine = pl.ds(pl.multiple_of(core * (D // 2), D // 2), D // 2)
        theirs = pl.ds(pl.multiple_of((1 - core) * (D // 2), D // 2), D // 2)
        keep_ref[...] = acc_ref[mine, :].astype(BF)
        send_ref[...] = acc_ref[theirs, :].astype(BF)


def grads(core, parts, e, top, eqa, eqb, inva, invb, xqa, xqb, ei, invi, xi, ids, targets):
    whole = lambda *s: pl.BlockSpec(s, lambda i: (0,) * len(s))
    first = lambda c: pl.BlockSpec((CH, c), lambda i: (jnp.minimum(i, 1), 0))
    second = lambda c: pl.BlockSpec((CH, c), lambda i: (jnp.maximum(i - 2, 0), 0))
    return pl.pallas_call(
        grad_kernel,
        grid=(QB // CH,),
        in_specs=[
            pl.BlockSpec(memory_space=pltpu.SMEM),
            whole(16, 3, 1, HALF),
            pl.BlockSpec((IB, CH), lambda i: (0, i)),
            pl.BlockSpec((1, CH), lambda i: (0, i)),
            first(D),
            second(D),
            first(1),
            second(1),
            first(D),
            second(D),
            whole(IB, D),
            whole(IB, 1),
            whole(IB, D),
            whole(IB, 1),
            pl.BlockSpec((1, CH), lambda i: (0, i)),
        ],
        out_specs=[whole(D // 2, D), whole(D // 2, D), whole(8, 128)],
        out_shape=[
            jax.ShapeDtypeStruct((D // 2, D), BF),
            jax.ShapeDtypeStruct((D // 2, D), BF),
            jax.ShapeDtypeStruct((8, 128), F32),
        ],
        scratch_shapes=[
            pltpu.VMEM((2, 1, HALF), F32),
            pltpu.VMEM((IB, D), F32),
            pltpu.VMEM((D, D), F32),
        ],
        compiler_params=pltpu.CompilerParams(vmem_limit_bytes=32 << 20),
        cost_estimate=pl.CostEstimate(
            flops=2 * IB * D * 2 * QB + 2 * D * D * (QB + IB), bytes_accessed=14 << 20, transcendentals=QB
        ),
        name="grads",
    )(core, parts, e, top, eqa, eqb, inva, invb, xqa, xqb, ei, invi, xi, ids, targets)


def body(xq_own, xi_own, weight, counts, positives):
    core = lax.axis_index("c")
    z, xl = lax.axis_index("z"), lax.axis_index("xl")
    xqa = gather(xq_own, YX, 8).reshape(HALF, D)
    xi = xi_own
    for k in (8, 4, 2, 1):
        xi = jnp.concatenate([xi, flip(xi, k)])
    near = xi
    xi = jnp.concatenate([xi, swap(xi, "xl")])

    at = lax.iota(jnp.int32, IB)
    p = (at // 16) % 16
    bits = (p % 2) * 8 + (p // 2 % 2) * 4 + (p // 4 % 2) * 2 + p // 8
    ids = ((z ^ bits) * 2 + (xl ^ (at // 256))) * 16 + at % 16
    logs = jnp.log(counts.astype(F32))
    logc = jnp.sum(jnp.where(ids[:, None] == at[None, :], logs[None, :], 0.0), axis=1, keepdims=True)
    block = (lax.axis_index("y") * 2 + lax.axis_index("xh")) * 2 + core
    ids = (block * IB + ids)[:, None]
    targets = positives.reshape(8, 2, 128).transpose(1, 0, 2)
    targets = jnp.where(core == 0, targets, jnp.concatenate([targets[1:], targets[:1]])).reshape(1, QB)

    eqa, inva = tower(xqa, weight, near, 512)
    eqb, invb = swap(eqa, "c"), swap(inva, "c")
    xqb = swap(xqa, "c")
    ei, invi, e, top, stat = score(eqa, eqb, xi, weight, logc, ids, targets)
    parts = gather(stat, POOL, 16)
    send, keep, loss = grads(
        core.reshape(1), parts, e, top, eqa, eqb, inva, invb, xqa, xqb, ei, invi, xi, ids, targets
    )

    loss = (loss + swap(loss, "xl"))[0, 0] / ROWS
    s = (keep.astype(F32) + swap(send, "c").astype(F32)).astype(BF)
    s = jnp.sum(exchange(s.reshape(16, 24, D), YXX).astype(F32), axis=0).astype(BF)
    s = s.reshape(16, 9, 128)
    tail = jnp.zeros((16, 1, 128), BF).at[:, 0, :3].set(split3(loss)[None])
    s = exchange(jnp.concatenate([s, tail], axis=1), "z")
    s = jnp.sum(s.astype(F32), axis=0)
    mean_loss = jnp.sum(s[9, :3])
    s = gather(s[:9].astype(BF), "z", 16).reshape(24, D)
    s = gather(s, YXX, 16).reshape(D // 2, D)
    other = swap(s, "c")
    first, second = jnp.where(core == 0, s, other), jnp.where(core == 0, other, s)
    return mean_loss, jnp.concatenate([first, second]).astype(F32)


def solution(mesh):
    fine = Mesh(mesh.devices.reshape(4, 2, 2, 16, 2), ("y", "xh", "c", "z", "xl"))
    batch = ("z", "xl")
    return jax.shard_map(
        body,
        mesh=fine,
        in_specs=(P(batch + POOL, None), P(POOL + batch, None), P(), P(POOL), P(batch)),
        out_specs=(P(), P()),
        check_vma=False,
    )
```

time: 225 us -> 207 us (0.920)
  starting transfers between devices: 49.1 us -> 70.9 us
  Pallas kernels: 0 us -> 21.4 us
  matrix products: 20.7 us -> 0 us
  waiting for transfers between devices: 57.8 us -> 39.8 us
  blocking collectives: 63 us -> 50.6 us
  other arithmetic: 15.4 us -> 4.24 us
    all_to_all x3, waiting for transfers between devices: 54.4 us -> 6.23 us  [exchange(): return lax.all_to_all(x, axes, 0, 0, tiled=True)]
    ppermute x0 -> x4, starting transfers between devices: none -> 24.8 us  [flip(): return lax.ppermute(x, 'z', [(i, i ^ k) for i in range(16)])]
    pallas_call x0 -> x3, Pallas kernels: none -> 21.4 us  [the longest x1 12.1 us: grads(): pl.pallas_call(grad_kernel, grid=(QB // CH,), in_specs=[pl.BlockSpec(memo...]
    dot_general x7 -> x0, matrix products: 20.7 us -> none  [the longest x5 15.6 us: dot(): return lax.dot_general(a, b, (dims, ((), ())), preferred_element_type=F32)]
    ppermute x5 -> x7, waiting for transfers between devices: 3.43 us -> 18.9 us  [swap(): return lax.ppermute(x, axis, [(0, 1), (1, 0)])]
    ppermute x0 -> x4, waiting for transfers between devices: none -> 14.8 us  [flip(): return lax.ppermute(x, 'z', [(i, i ^ k) for i in range(16)])]
    all_to_all x4 -> x3, blocking collectives: 63 us -> 50.6 us  [exchange(): return lax.all_to_all(x, axes, 0, 0, tiled=True)]
    unnamed x34 -> x32, local copies, waits for them, and re-layouts: 4.03 us -> 12.3 us
  transfers between devices with their start and end apart: 8 -> 14, of which waited for: 6 -> 11; matrix products, arithmetic and copies ran while one was open for 5% -> 2% of each run, Pallas kernels for 0% -> 3%
where the time goes in v2:
time: 207 us; the launch traced here: 206 us
  starting transfers between devices  70.9 us (34%)
  blocking collectives  50.6 us (24%)
  waiting for transfers between devices  39.8 us (19%)
  Pallas kernels  21.4 us (10%)
  local copies, waits for them, and re-layouts  17.2 us (8%)
  other arithmetic  4.24 us (2%)
    all_to_all x3, blocking collectives, exchange(): return lax.all_to_all(x, axes, 0, 0, tiled=True)  50.6 us
    ppermute x7, starting transfers between devices, swap(): return lax.ppermute(x, axis, [(0, 1), (1, 0)])  26.4 us
    ppermute x4, starting transfers between devices, flip(): return lax.ppermute(x, 'z', [(i, i ^ k) for i in range(16)])  24.8 us
    all_to_all x3, starting transfers between devices, exchange(): return lax.all_to_all(x, axes, 0, 0, tiled=True)  19.7 us
    ppermute x7, waiting for transfers between devices, swap(): return lax.ppermute(x, axis, [(0, 1), (1, 0)])  18.9 us
    ppermute x4, waiting for transfers between devices, flip(): return lax.ppermute(x, 'z', [(i, i ^ k) for i in range(16)])  14.8 us
    unnamed x32, local copies, waits for them, and re-layouts  12.3 us
    pallas_call x1, Pallas kernels, grads(): pl.pallas_call(grad_kernel, grid=(QB // CH,), in_specs=[pl.BlockSpec(memo...  12.1 us
  transfers between devices with their start and end apart: 14, of which 11 were waited for; matrix products, arithmetic and copies ran while one was open for 2% of the time, Pallas kernels for 3%

profile of v2, /device:TPU:1, one launch (start us, length us, event | category | flops | bytes accessed | tf_op | source)
XLA Modules:
  0.0 205.8 jit_solution(13279766238420418983)
XLA Ops:
  0.6 2.2 %broadcast_in_dim.26 = bf16[8,128,768]{2,1,0:T(8,128)(2,1)} broadcast(bf16[128,768]{1,0:T(8,128)(2,1)} %param.7), dimensions={1,2} | broadcast | bytes 1769472 | tf_op jit(solution)/shard_map/broadcast_in_dim | solution.py:37
  2.8 7.6 %all-to-all-start = ((bf16[8,128,768]{2,1,0:T(8,128)(2,1)}), bf16[8,128,768]{2,1,0:T(8,128)(2,1)S(1)}, u32[]{:S(2)}, u32[]{:S(2)}) async-start(bf16[8,128,768]{2,1,0:T(8,128)(2,1)} %broadcast_in_dim.26), calls=%async_computation | async-start | bytes 3145728 | tf_op jit(solution)/shard_map/all_to_all | solution.py:33
  10.4 0.0 copy-done.10
  10.4 15.4 %collective-permute-start = (bf16[16,768]{1,0:T(8,128)(2,1)S(1)}, bf16[16,768]{1,0:T(8,128)(2,1)S(1)}, u32[]{:S(2)}, u32[]{:S(2)}) collective-permute-start(bf16[16,768]{1,0:T(8,128)(2,1)S(1)} %copy-done.10), channel_id=1, source_target_pairs={{0,16},{2,18},{4,20},{6,22},{8,24},{10,26},{12,28},{14,30},{16,0},... | collective-permute-start | bytes 73736 | tf_op jit(solution)/shard_map/ppermute | solution.py:29
  25.9 1.3 collective-permute-done
  27.2 5.3 %collective-permute-start.1 = (bf16[32,768]{1,0:T(8,128)(2,1)S(1)}, bf16[32,768]{1,0:T(8,128)(2,1)S(1)}, u32[]{:S(2)}, u32[]{:S(2)}) collective-permute-start(bf16[32,768]{1,0:T(8,128)(2,1)S(1)} %pad_maximum_fusion.3), channel_id=1, source_target_pairs={{0,8},{2,10},{4,12},{6,14},{8,0},{10,2},{12,4},{14,6},{16,24},{18,... | collective-permute-start | bytes 147464 | tf_op jit(solution)/shard_map/ppermute | solution.py:29
  32.5 4.4 %collective-permute-done.1 = bf16[32,768]{1,0:T(8,128)(2,1)S(1)} collective-permute-done((bf16[32,768]{1,0:T(8,128)(2,1)S(1)}, bf16[32,768]{1,0:T(8,128)(2,1)S(1)}, u32[]{:S(2)}, u32[]{:S(2)}) %collective-permute-start.1) | collective-permute-done | bytes 49184 | tf_op jit(solution)/shard_map/ppermute | solution.py:29
  37.0 2.1 %collective-permute-start.2 = (bf16[64,768]{1,0:T(8,128)(2,1)S(1)}, bf16[64,768]{1,0:T(8,128)(2,1)S(1)}, u32[]{:S(2)}, u32[]{:S(2)}) collective-permute-start(bf16[64,768]{1,0:T(8,128)(2,1)S(1)} %pad_maximum_fusion.1), channel_id=1, source_target_pairs={{0,4},{2,6},{4,0},{6,2},{8,12},{10,14},{12,8},{14,10},{16,20},{18,... | collective-permute-start | bytes 294920 | tf_op jit(solution)/shard_map/ppermute | solution.py:29
  39.1 4.6 %collective-permute-done.2 = bf16[64,768]{1,0:T(8,128)(2,1)S(1)} collective-permute-done((bf16[64,768]{1,0:T(8,128)(2,1)S(1)}, bf16[64,768]{1,0:T(8,128)(2,1)S(1)}, u32[]{:S(2)}, u32[]{:S(2)}) %collective-permute-start.2) | collective-permute-done | bytes 98336 | tf_op jit(solution)/shard_map/ppermute | solution.py:29
  43.7 1.9 collective-permute-start.3
  45.7 4.4 %collective-permute-done.3 = bf16[128,768]{1,0:T(8,128)(2,1)S(1)} collective-permute-done((bf16[128,768]{1,0:T(8,128)(2,1)S(1)}, bf16[128,768]{1,0:T(8,128)(2,1)S(1)}, u32[]{:S(2)}, u32[]{:S(2)}) %collective-permute-start.3) | collective-permute-done | bytes 196640 | tf_op jit(solution)/shard_map/ppermute | solution.py:29
  50.2 0.0 all-to-all-done
  50.2 0.0 copy-start
  50.2 1.3 copy-done
  51.5 2.8 %tower.1 = (bf16[1024,768]{1,0:T(8,128)(2,1)}, f32[1024,1]{1,0:T(8,128)S(1)}) custom-call(bf16[1024,768]{1,0:T(8,128)(2,1)S(1)} %bitcast.18, bf16[768,768]{1,0:T(8,128)(2,1)S(1)} %copy-done, bf16[256,768]{1,0:T(8,128)(2,1)S(1)} %get-tuple-element.37.after_ref), custom_call_target="tpu_custom_call" | custom-call | flops 1207959552 | bytes 3145728 | tf_op jit(solution)/shard_map/tower/pallas_call | solution.py:63
  54.2 0.8 copy-done.2
  55.1 7.1 %collective-permute-start.4 = (bf16[1024,768]{1,0:T(8,128)(2,1)}, bf16[1024,768]{1,0:T(8,128)(2,1)}, u32[]{:S(2)}, u32[]{:S(2)}) collective-permute-start(bf16[1024,768]{1,0:T(8,128)(2,1)} %get-tuple-element.24.own_ref.eqa_ref), channel_id=1, source_target_pairs={{0,32},{32,0},{1,33},{33,1},{2,34},{34,2},{3,35},{35,3},{4,36},{36... | collective-permute-start | bytes 4718600 | tf_op jit(solution)/shard_map/ppermute | solution.py:25
  62.2 1.9 collective-permute-start.7
  64.1 0.0 copy-done.11
  64.2 0.0 copy-done.12
  64.2 2.2 %collective-permute-start.5 = (bf16[256,768]{1,0:T(8,128)(2,1)S(1)}, bf16[256,768]{1,0:T(8,128)(2,1)}, u32[]{:S(2)}, u32[]{:S(2)}) collective-permute-start(bf16[256,768]{1,0:T(8,128)(2,1)S(1)} %get-tuple-element.37.after_ref), channel_id=1, source_target_pairs={{0,1},{1,0},{2,3},{3,2},{4,5},{5,4},{6,7},{7,6},{8,9},{9,8},{10,11... | collective-permute-start | bytes 1179656 | tf_op jit(solution)/shard_map/ppermute | solution.py:25
  66.5 0.3 select_reduce_fusion
  66.7 0.2 copy.13.logc_ref
  66.9 0.4 fusion.16.ids_ref
  67.3 9.1 %collective-permute-done.5 = bf16[256,768]{1,0:T(8,128)(2,1)} collective-permute-done((bf16[256,768]{1,0:T(8,128)(2,1)S(1)}, bf16[256,768]{1,0:T(8,128)(2,1)}, u32[]{:S(2)}, u32[]{:S(2)}) %collective-permute-start.5) | collective-permute-done | bytes 393248 | tf_op jit(solution)/shard_map/ppermute | solution.py:25
  76.4 1.0 constant_dynamic-update-slice_fusion.5.xi_ref
  77.4 0.0 collective-permute-done.4.other_ref.eqb_ref
  77.4 0.0 copy-start.1
  77.4 1.3 copy-done.1
  78.7 6.5 %score.1 = (bf16[512,768]{1,0:T(8,128)(2,1)S(1)}, f32[512,1]{1,0:T(8,128)S(1)}, f32[512,2048]{1,0:T(8,128)S(1)}, f32[1,2048]{1,0:T(1,128)S(1)}, f32[3,1,1024]{2,1,0:T(1,128)S(1)}) custom-call(bf16[1024,768]{1,0:T(8,128)(2,1)} %get-tuple-element.24.own_ref.eqa_ref, bf16[1024,768]{1,0:T(8,128)(2,1)} %collective-permute-done.4.other_ref.eqb_ref, ...), custom_call_target="tpu_custom_call" | custom-call | flops 2214592512 | bytes 10485760 | tf_op jit(solution)/shard_map/score/pallas_call | solution.py:115
  85.2 1.9 copy-done.4
  87.1 0.9 copy-done.6
  88.1 0.7 copy-done.8
  88.8 0.8 broadcast_in_dim.31
  89.6 8.5 %all-to-all-start.1 = ((f32[16,3,1,1024]{3,2,1,0:T(1,128)}), f32[16,3,1,1024]{3,2,1,0:T(1,128)S(1)}, u32[]{:S(2)}, u32[]{:S(2)}) async-start(f32[16,3,1,1024]{3,2,1,0:T(1,128)} %broadcast_in_dim.31), calls=%async_computation.1 | async-start | bytes 393216 | tf_op jit(solution)/shard_map/all_to_all | solution.py:33
  98.1 2.0 collective-permute-start.6
  100.1 2.0 collective-permute-done.6.invb_ref
  102.1 0.0 collective-permute-done.7.xqb_ref
  102.1 4.2 %all-to-all-done.1.parts_ref = f32[16,3,1,1024]{3,2,1,0:T(1,128)S(1)} async-done(((f32[16,3,1,1024]{3,2,1,0:T(1,128)}), f32[16,3,1,1024]{3,2,1,0:T(1,128)S(1)}, u32[]{:S(2)}, u32[]{:S(2)}) %all-to-all-start.1) | async-done | bytes 196640 | tf_op jit(solution)/shard_map/all_to_all | solution.py:33
  106.3 1.0 copy-done.3
  107.3 2.2 %copy-done.5 = f32[512,2048]{1,0:T(8,128)S(1)} copy-done((f32[512,2048]{1,0:T(8,128)S(1)}, f32[512,2048]{1,0:T(8,128)}, u32[]{:S(2)}) %copy-start.5) | copy-done | bytes 4194328
  109.5 1.1 copy-done.7
  110.7 0.9 copy-done.9
  111.6 12.1 %grads.1 = (bf16[384,768]{1,0:T(8,128)(2,1)S(1)}, bf16[384,768]{1,0:T(8,128)(2,1)S(1)}, f32[8,128]{1,0:T(8,128)S(1)}) custom-call(s32[1]{0:T(128)} %bitcast.core_ref, f32[16,3,1,1024]{3,2,1,0:T(1,128)S(1)} %all-to-all-done.1.parts_ref, f32[512,2048]{1,0:T(8,128)S(1)} %copy-done.5, f32[1,2048]{1,0:T(1,128)S(1)} %get-tuple-element.27.top_ref, ...), custom_call_target="tpu_custom_call" | custom-call | flops 6241124352 | bytes 14680064 | tf_op jit(solution)/shard_map/grads/pallas_call | solution.py:211
  123.8 2.7 %collective-permute-start.8 = (bf16[384,768]{1,0:T(8,128)(2,1)S(1)}, bf16[384,768]{1,0:T(8,128)(2,1)S(1)}, u32[]{:S(2)}, u32[]{:S(2)}) collective-permute-start(bf16[384,768]{1,0:T(8,128)(2,1)S(1)} %get-tuple-element.32), channel_id=1, source_target_pairs={{0,32},{32,0},{1,33},{33,1},{2,34},{34,2},{3,35},{35,3},{4,36},{36... | collective-permute-start | bytes 1769480 | tf_op jit(solution)/shard_map/ppermute | solution.py:25
  126.5 1.6 collective-permute-done.8
  128.1 0.9 add_convert_fusion
  129.0 3.6 %all-to-all-start.2 = ((bf16[16,24,768]{2,1,0:T(8,128)(2,1)}), bf16[16,24,768]{2,1,0:T(8,128)(2,1)S(1)}, u32[]{:S(2)}, u32[]{:S(2)}) async-start(bf16[16,24,768]{2,1,0:T(8,128)(2,1)} %bitcast.7), calls=%async_computation.2 | async-start | bytes 1179648 | tf_op jit(solution)/shard_map/all_to_all | solution.py:33
  132.6 3.1 %collective-permute-start.9 = (f32[8,128]{1,0:T(8,128)S(1)}, f32[8,128]{1,0:T(8,128)S(1)}, u32[]{:S(2)}, u32[]{:S(2)}) collective-permute-start(f32[8,128]{1,0:T(8,128)S(1)} %get-tuple-element.33), channel_id=1, source_target_pairs={{0,1},{1,0},{2,3},{3,2},{4,5},{5,4},{6,7},{7,6},{8,9},{9,8},{10,11... | collective-permute-start | bytes 12296 | tf_op jit(solution)/shard_map/ppermute | solution.py:25
  135.8 5.2 %collective-permute-done.9 = f32[8,128]{1,0:T(8,128)S(1)} collective-permute-done((f32[8,128]{1,0:T(8,128)S(1)}, f32[8,128]{1,0:T(8,128)S(1)}, u32[]{:S(2)}, u32[]{:S(2)}) %collective-permute-start.9) | collective-permute-done | bytes 4128 | tf_op jit(solution)/shard_map/ppermute | solution.py:25
  141.0 0.5 slice.41
  142.1 0.1 select_maximum_fusion
  142.2 2.0 all-to-all-done.2
  144.3 0.1 reduce_sum.40
  144.4 0.1 reshape.415
  144.5 22.7 %all_to_all.30 = bf16[16,10,128]{2,1,0:T(8,128)(2,1)S(1)} all-to-all(bf16[16,10,128]{2,1,0:T(8,128)(2,1)S(1)} %pad_maximum_fusion.2), channel_id=1, replica_groups=mesh['y'=4,'xh'=2,'c'=2,'z'=16,'xl'=2] {'z'}, dimensions={0} | all-to-all | bytes 81920 | tf_op jit(solution)/shard_map/all_to_all | solution.py:33
  167.3 14.4 %all_to_all.31 = bf16[16,9,128]{2,1,0:T(8,128)(2,1)S(1)} all-to-all(bf16[16,9,128]{2,1,0:T(8,128)(2,1)S(1)} %broadcast_in_dim.32), channel_id=1, replica_groups=mesh['y'=4,'xh'=2,'c'=2,'z'=16,'xl'=2] {'z'}, dimensions={0} | all-to-all | bytes 73728 | tf_op jit(solution)/shard_map/all_to_all | solution.py:33
  181.7 0.1 broadcast_in_dim.58
  181.8 13.4 %all_to_all.32 = bf16[16,24,768]{2,1,0:T(8,128)(2,1)S(1)} all-to-all(bf16[16,24,768]{2,1,0:T(8,128)(2,1)S(1)} %broadcast_in_dim.59), channel_id=1, replica_groups=mesh['y'=4,'xh'=2,'c'=2,'z'=16,'xl'=2] {'y','xh','xl'}, dimensions={0} | all-to-all | bytes 1179648 | tf_op jit(solution)/shard_map/all_to_all | solution.py:33
  195.2 7.3 %collective-permute-start.10 = (bf16[384,768]{1,0:T(8,128)(2,1)S(1)}, bf16[384,768]{1,0:T(8,128)(2,1)S(1)}, u32[]{:S(2)}, u32[]{:S(2)}) collective-permute-start(bf16[384,768]{1,0:T(8,128)(2,1)S(1)} %bitcast.23), channel_id=1, source_target_pairs={{0,32},{32,0},{1,33},{33,1},{2,34},{34,2},{3,35},{35,3},{4,36},{36... | collective-permute-start | bytes 1769480 | tf_op jit(solution)/shard_map/ppermute | solution.py:25
  202.5 0.6 slice_reduce_fusion
  203.1 1.0 collective-permute-done.10
  204.1 0.1 broadcast_select_fusion.1
  204.2 1.6 maximum_convert_fusion
  (32 shorter events, 0.3 us)
Async XLA Ops:
  2.8 7.6 %copy-start.10 = (bf16[16,768]{1,0:T(8,128)(2,1)S(1)}, bf16[16,768]{1,0:T(8,128)(2,1)}, u32[]{:S(2)}) copy-start(bf16[16,768]{1,0:T(8,128)(2,1)} %param.8) | copy-start | bytes 73732
  2.8 47.4 %all-to-all-start = ((bf16[8,128,768]{2,1,0:T(8,128)(2,1)}), bf16[8,128,768]{2,1,0:T(8,128)(2,1)S(1)}, u32[]{:S(2)}, u32[]{:S(2)}) async-start(bf16[8,128,768]{2,1,0:T(8,128)(2,1)} %broadcast_in_dim.26), calls=%async_computation | async-start | bytes 3145728 | tf_op jit(solution)/shard_map/all_to_all | solution.py:33
  10.4 16.8 %collective-permute-start = (bf16[16,768]{1,0:T(8,128)(2,1)S(1)}, bf16[16,768]{1,0:T(8,128)(2,1)S(1)}, u32[]{:S(2)}, u32[]{:S(2)}) collective-permute-start(bf16[16,768]{1,0:T(8,128)(2,1)S(1)} %copy-done.10), channel_id=1, source_target_pairs={{0,16},{2,18},{4,20},{6,22},{8,24},{10,26},{12,28},{14,30},{16,0},... | collective-permute-start | bytes 73736 | tf_op jit(solution)/shard_map/ppermute | solution.py:29
  27.2 9.8 %collective-permute-start.1 = (bf16[32,768]{1,0:T(8,128)(2,1)S(1)}, bf16[32,768]{1,0:T(8,128)(2,1)S(1)}, u32[]{:S(2)}, u32[]{:S(2)}) collective-permute-start(bf16[32,768]{1,0:T(8,128)(2,1)S(1)} %pad_maximum_fusion.3), channel_id=1, source_target_pairs={{0,8},{2,10},{4,12},{6,14},{8,0},{10,2},{12,4},{14,6},{16,24},{18,... | collective-permute-start | bytes 147464 | tf_op jit(solution)/shard_map/ppermute | solution.py:29
  37.0 6.7 %collective-permute-start.2 = (bf16[64,768]{1,0:T(8,128)(2,1)S(1)}, bf16[64,768]{1,0:T(8,128)(2,1)S(1)}, u32[]{:S(2)}, u32[]{:S(2)}) collective-permute-start(bf16[64,768]{1,0:T(8,128)(2,1)S(1)} %pad_maximum_fusion.1), channel_id=1, source_target_pairs={{0,4},{2,6},{4,0},{6,2},{8,12},{10,14},{12,8},{14,10},{16,20},{18,... | collective-permute-start | bytes 294920 | tf_op jit(solution)/shard_map/ppermute | solution.py:29
  43.7 6.4 %collective-permute-start.3 = (bf16[128,768]{1,0:T(8,128)(2,1)S(1)}, bf16[128,768]{1,0:T(8,128)(2,1)S(1)}, u32[]{:S(2)}, u32[]{:S(2)}) collective-permute-start(bf16[128,768]{1,0:T(8,128)(2,1)S(1)} %pad_maximum_fusion), channel_id=1, source_target_pairs={{0,2},{2,0},{4,6},{6,4},{8,10},{10,8},{12,14},{14,12},{16,18},{18,... | collective-permute-start | bytes 589832 | tf_op jit(solution)/shard_map/ppermute | solution.py:29
  50.2 1.3 copy-start
  51.5 12.7 %copy-start.11 = (s32[2048]{0:T(1024)S(1)}, s32[2048]{0:T(1024)}, u32[]{:S(2)}) copy-start(s32[2048]{0:T(1024)} %param.11) | copy-start | bytes 24580
  51.5 12.7 %copy-start.12 = (s32[512]{0:T(512)S(1)}, s32[512]{0:T(512)}, u32[]{:S(2)}) copy-start(s32[512]{0:T(512)} %param.10) | copy-start | bytes 6148
  54.2 0.8 copy-start.2
  55.1 22.4 %collective-permute-start.4 = (bf16[1024,768]{1,0:T(8,128)(2,1)}, bf16[1024,768]{1,0:T(8,128)(2,1)}, u32[]{:S(2)}, u32[]{:S(2)}) collective-permute-start(bf16[1024,768]{1,0:T(8,128)(2,1)} %get-tuple-element.24.own_ref.eqa_ref), channel_id=1, source_target_pairs={{0,32},{32,0},{1,33},{33,1},{2,34},{34,2},{3,35},{35,3},{4,36},{36... | collective-permute-start | bytes 4718600 | tf_op jit(solution)/shard_map/ppermute | solution.py:25
  62.2 39.9 %collective-permute-start.7 = (bf16[1024,768]{1,0:T(8,128)(2,1)S(1)}, bf16[1024,768]{1,0:T(8,128)(2,1)}, u32[]{:S(2)}, u32[]{:S(2)}) collective-permute-start(bf16[1024,768]{1,0:T(8,128)(2,1)S(1)} %bitcast.19), channel_id=1, source_target_pairs={{0,32},{32,0},{1,33},{33,1},{2,34},{34,2},{3,35},{35,3},{4,36},{36... | collective-permute-start | bytes 4718600 | tf_op jit(solution)/shard_map/ppermute | solution.py:25
  64.2 12.2 %collective-permute-start.5 = (bf16[256,768]{1,0:T(8,128)(2,1)S(1)}, bf16[256,768]{1,0:T(8,128)(2,1)}, u32[]{:S(2)}, u32[]{:S(2)}) collective-permute-start(bf16[256,768]{1,0:T(8,128)(2,1)S(1)} %get-tuple-element.37.after_ref), channel_id=1, source_target_pairs={{0,1},{1,0},{2,3},{3,2},{4,5},{5,4},{6,7},{7,6},{8,9},{9,8},{10,11... | collective-permute-start | bytes 1179656 | tf_op jit(solution)/shard_map/ppermute | solution.py:25
  77.4 1.3 copy-start.1
  85.2 1.9 copy-start.4
  87.1 0.9 copy-start.6
  88.1 0.7 copy-start.8
  89.6 16.7 %all-to-all-start.1 = ((f32[16,3,1,1024]{3,2,1,0:T(1,128)}), f32[16,3,1,1024]{3,2,1,0:T(1,128)S(1)}, u32[]{:S(2)}, u32[]{:S(2)}) async-start(f32[16,3,1,1024]{3,2,1,0:T(1,128)} %broadcast_in_dim.31), calls=%async_computation.1 | async-start | bytes 393216 | tf_op jit(solution)/shard_map/all_to_all | solution.py:33
  98.1 4.0 %collective-permute-start.6 = (f32[1024,1]{1,0:T(8,128)}, f32[1024,1]{1,0:T(8,128)S(1)}, u32[]{:S(2)}, u32[]{:S(2)}) collective-permute-start(f32[1024,1]{1,0:T(8,128)} %copy-done.2), channel_id=1, source_target_pairs={{0,32},{32,0},{1,33},{33,1},{2,34},{34,2},{3,35},{35,3},{4,36},{36... | collective-permute-start | bytes 12296 | tf_op jit(solution)/shard_map/ppermute | solution.py:25
  106.3 1.0 copy-start.3
  107.3 2.2 %copy-start.5 = (f32[512,2048]{1,0:T(8,128)S(1)}, f32[512,2048]{1,0:T(8,128)}, u32[]{:S(2)}) copy-start(f32[512,2048]{1,0:T(8,128)} %copy-done.4) | copy-start | bytes 12582916
  109.5 1.1 copy-start.7
  110.7 0.9 copy-start.9
  123.8 4.3 %collective-permute-start.8 = (bf16[384,768]{1,0:T(8,128)(2,1)S(1)}, bf16[384,768]{1,0:T(8,128)(2,1)S(1)}, u32[]{:S(2)}, u32[]{:S(2)}) collective-permute-start(bf16[384,768]{1,0:T(8,128)(2,1)S(1)} %get-tuple-element.32), channel_id=1, source_target_pairs={{0,32},{32,0},{1,33},{33,1},{2,34},{34,2},{3,35},{35,3},{4,36},{36... | collective-permute-start | bytes 1769480 | tf_op jit(solution)/shard_map/ppermute | solution.py:25
  129.0 15.2 %all-to-all-start.2 = ((bf16[16,24,768]{2,1,0:T(8,128)(2,1)}), bf16[16,24,768]{2,1,0:T(8,128)(2,1)S(1)}, u32[]{:S(2)}, u32[]{:S(2)}) async-start(bf16[16,24,768]{2,1,0:T(8,128)(2,1)} %bitcast.7), calls=%async_computation.2 | async-start | bytes 1179648 | tf_op jit(solution)/shard_map/all_to_all | solution.py:33
  132.6 8.3 %collective-permute-start.9 = (f32[8,128]{1,0:T(8,128)S(1)}, f32[8,128]{1,0:T(8,128)S(1)}, u32[]{:S(2)}, u32[]{:S(2)}) collective-permute-start(f32[8,128]{1,0:T(8,128)S(1)} %get-tuple-element.33), channel_id=1, source_target_pairs={{0,1},{1,0},{2,3},{3,2},{4,5},{5,4},{6,7},{7,6},{8,9},{9,8},{10,11... | collective-permute-start | bytes 12296 | tf_op jit(solution)/shard_map/ppermute | solution.py:25
  195.2 8.9 %collective-permute-start.10 = (bf16[384,768]{1,0:T(8,128)(2,1)S(1)}, bf16[384,768]{1,0:T(8,128)(2,1)S(1)}, u32[]{:S(2)}, u32[]{:S(2)}) collective-permute-start(bf16[384,768]{1,0:T(8,128)(2,1)S(1)} %bitcast.23), channel_id=1, source_target_pairs={{0,32},{32,0},{1,33},{33,1},{2,34},{34,2},{3,35},{35,3},{4,36},{36... | collective-permute-start | bytes 1769480 | tf_op jit(solution)/shard_map/ppermute | solution.py:25

commit v3 on v2

v3 whole, which is shorter than its diff:
```python
import functools

import jax
import jax.numpy as jnp
from jax import lax
from jax.experimental import pallas as pl
from jax.experimental.pallas import tpu as pltpu
from jax.sharding import Mesh, PartitionSpec as P

BF = jnp.bfloat16
F32 = jnp.float32
D = 768
YX = ("y", "xh")
YXX = ("y", "xh", "xl")
POOL = ("y", "xh", "c")
ROWS = 65536
QB = 2048
IB = 512
HALF = 1024
CH = 512
INV_NORM = 1.0 / ROWS**0.5


def swap(x, axis):
    return lax.ppermute(x, axis, [(0, 1), (1, 0)])


def turn(x, k):
    return lax.ppermute(x, "y", [(i, (i + k) % 4) for i in range(4)])


def exchange(x, axes):
    return lax.all_to_all(x, axes, 0, 0, tiled=True)


def gather(x, axes, n):
    return exchange(jnp.broadcast_to(x[None], (n,) + x.shape), axes)


def dot(a, b, dims):
    return lax.dot_general(a, b, (dims, ((), ())), preferred_element_type=F32)


def split3(x):
    hi = x.astype(BF)
    mid = (x - hi.astype(F32)).astype(BF)
    low = (x - hi.astype(F32) - mid.astype(F32)).astype(BF)
    return jnp.stack([hi, mid, low])


def unit_rows(x, weight):
    proj = dot(x, weight, ((1,), (0,)))
    inv = 1.0 / jnp.sqrt(jnp.sum(proj * proj, axis=1, keepdims=True) + 1e-06)
    return (proj * inv).astype(BF), inv


def score_tile(ei_ref, eq, logc_ref):
    return 100.0 * dot(ei_ref[...], eq, ((1,), (1,))) - logc_ref[...]


def whole(*s):
    return pl.BlockSpec(s, lambda i: (0,) * len(s))


def first(c):
    return pl.BlockSpec((CH, c), lambda i: (jnp.minimum(i, HALF // CH - 1), 0))


def second(c):
    return pl.BlockSpec((CH, c), lambda i: (jnp.maximum(i - HALF // CH, 0), 0))


def copies_kernel(xl_ref, mine_ref, other_ref, after_ref, out_ref):
    xl = xl_ref[0]
    out_ref[0, xl] = mine_ref[...]
    out_ref[0, 1 - xl] = other_ref[...]


def copies(xl, mine, other, after):
    n = mine.shape[0]
    return pl.pallas_call(
        copies_kernel,
        grid=(16,),
        in_specs=[
            pl.BlockSpec(memory_space=pltpu.SMEM),
            whole(n, D),
            whole(n, D),
            pl.BlockSpec(memory_space=pl.ANY),
        ],
        out_specs=pl.BlockSpec((1, 2, n, D), lambda i: (i, 0, 0, 0)),
        out_shape=jax.ShapeDtypeStruct((16, 2, n, D), BF),
        compiler_params=pltpu.CompilerParams(vmem_limit_bytes=4 << 20),
        cost_estimate=pl.CostEstimate(flops=0, bytes_accessed=32 * n * D * 2, transcendentals=0),
        name="copies",
    )(xl.reshape(1), mine, other, after)


def tower_kernel(x_ref, w_ref, e_ref, inv_ref):
    e_ref[...], inv_ref[...] = unit_rows(x_ref[...], w_ref[...])


def tower(x, weight):
    return pl.pallas_call(
        tower_kernel,
        grid=(HALF // CH,),
        in_specs=[pl.BlockSpec((CH, D), lambda i: (i, 0)), whole(D, D)],
        out_specs=[pl.BlockSpec((CH, D), lambda i: (i, 0)), pl.BlockSpec((CH, 1), lambda i: (i, 0))],
        out_shape=[pltpu.HBM((HALF, D), BF), pltpu.HBM((HALF, 1), F32)],
        compiler_params=pltpu.CompilerParams(vmem_limit_bytes=16 << 20),
        cost_estimate=pl.CostEstimate(flops=2 * HALF * D * D, bytes_accessed=4 * HALF * D, transcendentals=HALF),
        name="tower",
    )(x, weight)


def score_kernel(order_ref, eqa_ref, eqb_ref, w_ref, xi_ref, logc_ref, ids_ref, tgt_ref,
                 ei_ref, invi_ref, stat_ref):
    i = pl.program_id(0)

    @pl.when(i == 0)
    def _():
        ei_ref[...], invi_ref[...] = unit_rows(xi_ref[...], w_ref[...])
        stat_ref[...] = jnp.zeros_like(stat_ref)

    def run(eq):
        scores = score_tile(ei_ref, eq, logc_ref)
        top = jnp.max(scores, axis=0, keepdims=True)
        lse = top + jnp.log(jnp.sum(jnp.exp(scores - top), axis=0, keepdims=True))
        pos = jnp.sum(jnp.where(ids_ref[...] == tgt_ref[...], scores, 0.0), axis=0, keepdims=True)
        for k in range(CH // 128):
            part = slice(k * 128, (k + 1) * 128)
            stat_ref[pl.ds(order_ref[i * (CH // 128) + k], 1), :] = lse[:, part]
            stat_ref[16:17, :] = stat_ref[16:17, :] + pos[:, part]

    @pl.when(i < HALF // CH)
    def _():
        run(eqa_ref[...])

    @pl.when(i >= HALF // CH)
    def _():
        run(eqb_ref[...])


def score(order, eqa, eqb, weight, xi, logc, ids, targets):
    return pl.pallas_call(
        score_kernel,
        grid=(QB // CH,),
        in_specs=[
            pl.BlockSpec(memory_space=pltpu.SMEM),
            first(D),
            second(D),
            whole(D, D),
            whole(IB, D),
            whole(IB, 1),
            whole(IB, 1),
            pl.BlockSpec((1, CH), lambda i: (0, i)),
        ],
        out_specs=[whole(IB, D), whole(IB, 1), whole(24, 128)],
        out_shape=[
            jax.ShapeDtypeStruct((IB, D), BF),
            jax.ShapeDtypeStruct((IB, 1), F32),
            jax.ShapeDtypeStruct((24, 128), F32),
        ],
        compiler_params=pltpu.CompilerParams(vmem_limit_bytes=24 << 20),
        cost_estimate=pl.CostEstimate(
            flops=2 * IB * D * (D + QB), bytes_accessed=6 << 20, transcendentals=IB * QB
        ),
        name="score",
    )(order, eqa, eqb, weight, xi, logc, ids, targets)


def grad_kernel(core_ref, order_ref, parts_ref, eqa_ref, eqb_ref, inva_ref, invb_ref, xqa_ref, xqb_ref,
                ei_ref, invi_ref, xi_ref, logc_ref, ids_ref, tgt_ref,
                send_ref, keep_ref, loss_ref, lse_ref, di_ref, acc_ref):
    i = pl.program_id(0)
    core = core_ref[0]

    @pl.when(i == 0)
    def _():
        vals = [parts_ref[d, :16, :] for d in range(16)]
        top = functools.reduce(jnp.maximum, vals)
        lse = top + jnp.log(sum(jnp.exp(v - top) for v in vals))
        lse_ref[...] = lse
        pos = sum(parts_ref[d, 16:17, :] for d in range(16))
        total = jnp.sum(jnp.sum(lse, axis=0, keepdims=True) - pos, axis=1, keepdims=True)
        loss_ref[...] = jnp.broadcast_to(total, (8, 128))
        di_ref[...] = jnp.zeros_like(di_ref)
        acc_ref[...] = jnp.zeros_like(acc_ref)

    def run(eq_ref, inv_ref, xq_ref):
        eq = eq_ref[...]
        rows = [order_ref[i * (CH // 128) + k] for k in range(CH // 128)]
        lse = jnp.concatenate([lse_ref[pl.ds(r, 1), :] for r in rows], axis=1)
        prob = jnp.exp(score_tile(ei_ref, eq, logc_ref) - lse)
        hit = ids_ref[...] == tgt_ref[...]
        grad = ((prob - jnp.where(hit, 1.0, 0.0)) * INV_NORM).astype(BF)
        di_ref[...] += dot(grad, eq, ((1,), (0,)))
        dq = 100.0 * dot(grad, ei_ref[...], ((0,), (0,)))
        eq = eq.astype(F32)
        inner = jnp.sum(eq * dq, axis=1, keepdims=True)
        dz = ((dq - eq * inner) * inv_ref[...]).astype(BF)
        acc_ref[...] += dot(xq_ref[...], dz, ((0,), (0,)))

    @pl.when(i < HALF // CH)
    def _():
        run(eqa_ref, inva_ref, xqa_ref)

    @pl.when(i >= HALF // CH)
    def _():
        run(eqb_ref, invb_ref, xqb_ref)

    @pl.when(i == QB // CH - 1)
    def _():
        di = 100.0 * di_ref[...]
        ei = ei_ref[...].astype(F32)
        inner = jnp.sum(ei * di, axis=1, keepdims=True)
        dz = ((di - ei * inner) * invi_ref[...]).astype(BF)
        acc_ref[...] += dot(xi_ref[...], dz, ((0,), (0,)))
        mine = pl.ds(pl.multiple_of(core * (D // 2), D // 2), D // 2)
        theirs = pl.ds(pl.multiple_of((1 - core) * (D // 2), D // 2), D // 2)
        keep_ref[...] = acc_ref[mine, :].astype(BF)
        send_ref[...] = acc_ref[theirs, :].astype(BF)


def grads(core, order, parts, eqa, eqb, inva, invb, xqa, xqb, ei, invi, xi, logc, ids, targets):
    return pl.pallas_call(
        grad_kernel,
        grid=(QB // CH,),
        in_specs=[
            pl.BlockSpec(memory_space=pltpu.SMEM),
            pl.BlockSpec(memory_space=pltpu.SMEM),
            whole(16, 24, 128),
            first(D),
            second(D),
            first(1),
            second(1),
            first(D),
            second(D),
            whole(IB, D),
            whole(IB, 1),
            whole(IB, D),
            whole(IB, 1),
            whole(IB, 1),
            pl.BlockSpec((1, CH), lambda i: (0, i)),
        ],
        out_specs=[whole(D // 2, D), whole(D // 2, D), whole(8, 128)],
        out_shape=[
            jax.ShapeDtypeStruct((D // 2, D), BF),
            jax.ShapeDtypeStruct((D // 2, D), BF),
            jax.ShapeDtypeStruct((8, 128), F32),
        ],
        scratch_shapes=[
            pltpu.VMEM((16, 128), F32),
            pltpu.VMEM((IB, D), F32),
            pltpu.VMEM((D, D), F32),
        ],
        compiler_params=pltpu.CompilerParams(vmem_limit_bytes=32 << 20),
        cost_estimate=pl.CostEstimate(
            flops=2 * IB * D * 3 * QB + 2 * D * D * (QB + IB), bytes_accessed=9 << 20, transcendentals=IB * QB
        ),
        name="grads",
    )(core, order, parts, eqa, eqb, inva, invb, xqa, xqb, ei, invi, xi, logc, ids, targets)


def body(xq_own, xi_own, weight, counts, positives):
    core, y, xh = lax.axis_index("c"), lax.axis_index("y"), lax.axis_index("xh")
    xl = lax.axis_index("xl")
    far = swap(xi_own, "xl")
    side = swap(xq_own, "xh")
    two = jnp.concatenate([xq_own, side])
    xqa = jnp.concatenate([two, turn(two, 1), turn(two, 3), turn(two, 2)])
    xqb = swap(xqa, "c")
    xi = exchange(copies(xl, xi_own, far, side), "z").reshape(IB, D)

    q = lax.iota(jnp.int32, 16)
    step = (q // 2) % 4
    from_y = (y + jnp.where(step == 1, 3, jnp.where(step == 2, 1, jnp.where(step == 3, 2, 0)))) % 4
    order = from_y * 4 + (xh ^ (q % 2)) * 2 + (core ^ (q // 8))
    picks = order[:, None, None] == q[None, :, None]
    targets = jnp.sum(jnp.where(picks, positives.reshape(1, 16, 128), 0), axis=1).reshape(1, QB)
    block = (y * 2 + xh) * 2 + core
    ids = (block * IB + lax.iota(jnp.int32, IB))[:, None]
    logc = jnp.log(counts.astype(F32))[:, None]

    eqa, inva = tower(xqa, weight)
    eqb, invb = tower(xqb, weight)
    ei, invi, stat = score(order, eqa, eqb, weight, xi, logc, ids, targets)
    parts = gather(stat, POOL, 16)
    send, keep, loss = grads(
        core.reshape(1), order, parts, eqa, eqb, inva, invb, xqa, xqb, ei, invi, xi, logc, ids, targets
    )

    loss = (loss + swap(loss, "xl"))[0, 0] / ROWS
    s = (keep.astype(F32) + swap(send, "c").astype(F32)).astype(BF)
    s = jnp.sum(exchange(s.reshape(16, 24, D), YXX).astype(F32), axis=0).astype(BF)
    tail = jnp.zeros((7, 128), BF).at[0, :3].set(split3(loss))
    tail = jnp.broadcast_to(tail[None], (16, 7, 128))
    s = exchange(jnp.concatenate([s.reshape(16, 9, 128), tail], axis=1), "z")
    s = jnp.sum(s.astype(F32), axis=0)
    mean_loss = jnp.sum(s[9, :3])
    s = gather(s.astype(BF), "z", 16)[:, :9]
    s = gather(s.reshape(24, D), YXX, 16).reshape(D // 2, D)
    other = swap(s, "c")
    first, second = jnp.where(core == 0, s, other), jnp.where(core == 0, other, s)
    return mean_loss, jnp.concatenate([first, second]).astype(F32)


def solution(mesh):
    fine = Mesh(mesh.devices.reshape(4, 2, 2, 16, 2), ("y", "xh", "c", "z", "xl"))
    batch = ("z", "xl")
    return jax.shard_map(
        body,
        mesh=fine,
        in_specs=(P(batch + POOL, None), P(POOL + batch, None), P(), P(POOL), P(batch)),
        out_specs=(P(), P()),
        check_vma=False,
    )
```

time: 207 us -> 188 us (0.908)
  starting transfers between devices: 70.9 us -> 54.3 us
  waiting for transfers between devices: 39.8 us -> 24.2 us
  blocking collectives: 50.6 us -> 65.7 us
  local copies, waits for them, and re-layouts: 17.2 us -> 7.14 us
  Pallas kernels: 21.4 us -> 30 us
    all_to_all x3 -> x4, blocking collectives: 50.6 us -> 65.7 us  [exchange(): return lax.all_to_all(x, axes, 0, 0, tiled=True)]
    ppermute x4 -> x3, starting transfers between devices: 24.8 us -> 10.1 us  [turn(): return lax.ppermute(x, 'y', [(i, (i + k) % 4) for i in range(4)])]
    ppermute x7 -> x6, waiting for transfers between devices: 18.9 us -> 10.7 us  [swap(): return lax.ppermute(x, axis, [(0, 1), (1, 0)])]
    pallas_call x2 -> x4, Pallas kernels: 9.27 us -> 17 us  [the longest x2 6.93 us: tower(): pl.pallas_call(tower_kernel, grid=(HALF // CH,), in_specs=[pl.BlockSpec((...]
    unnamed x32 -> x27, local copies, waits for them, and re-layouts: 12.3 us -> 6.2 us
    all_to_all x3 -> x2, waiting for transfers between devices: 6.23 us -> 2.05 us  [exchange(): return lax.all_to_all(x, axes, 0, 0, tiled=True)]
    ppermute x4 -> x3, waiting for transfers between devices: 14.8 us -> 11.4 us  [turn(): return lax.ppermute(x, 'y', [(i, (i + k) % 4) for i in range(4)])]
    broadcast_in_dim x5 -> x4, local copies, waits for them, and re-layouts: 3.08 us -> 0.13 us  [gather(): return exchange(jnp.broadcast_to(x[None], (n,) + x.shape), axes)]
  transfers between devices with their start and end apart: 14 -> 11, of which waited for: 11 -> 8; matrix products, arithmetic and copies ran while one was open for 2% -> 1% of each run, Pallas kernels for 3% -> 4%
where the time goes in v3:
time: 188 us; the launch traced here: 187 us
  blocking collectives  65.7 us (35%)
  starting transfers between devices  54.3 us (29%)
  Pallas kernels  30 us (16%)
  waiting for transfers between devices  24.2 us (13%)
  local copies, waits for them, and re-layouts  7.14 us (4%)
  other arithmetic  3.7 us (2%)
    all_to_all x4, blocking collectives, exchange(): return lax.all_to_all(x, axes, 0, 0, tiled=True)  65.7 us
    ppermute x6, starting transfers between devices, swap(): return lax.ppermute(x, axis, [(0, 1), (1, 0)])  25.4 us
    all_to_all x2, starting transfers between devices, exchange(): return lax.all_to_all(x, axes, 0, 0, tiled=True)  18.8 us
    pallas_call x1, Pallas kernels, grads(): pl.pallas_call(grad_kernel, grid=(QB // CH,), in_specs=[pl.BlockSpec(memo...  13.1 us
    ppermute x3, waiting for transfers between devices, turn(): return lax.ppermute(x, 'y', [(i, (i + k) % 4) for i in range(4)])  11.4 us
    ppermute x6, waiting for transfers between devices, swap(): return lax.ppermute(x, axis, [(0, 1), (1, 0)])  10.7 us
    ppermute x3, starting transfers between devices, turn(): return lax.ppermute(x, 'y', [(i, (i + k) % 4) for i in range(4)])  10.1 us
    pallas_call x2, Pallas kernels, tower(): pl.pallas_call(tower_kernel, grid=(HALF // CH,), in_specs=[pl.BlockSpec((...  6.93 us
  transfers between devices with their start and end apart: 11, of which 8 were waited for; matrix products, arithmetic and copies ran while one was open for 1% of the time, Pallas kernels for 4%

profile of v3, /device:TPU:1, one launch (start us, length us, event | category | flops | bytes accessed | tf_op | source)
XLA Modules:
  0.0 186.7 jit_solution(10068775275617558135)
XLA Ops:
  0.6 5.5 %collective-permute-start = (bf16[128,768]{1,0:T(8,128)(2,1)}, bf16[128,768]{1,0:T(8,128)(2,1)S(1)}, u32[]{:S(2)}, u32[]{:S(2)}) collective-permute-start(bf16[128,768]{1,0:T(8,128)(2,1)} %param.7), channel_id=1, source_target_pairs={{0,64},{64,0},{1,65},{65,1},{2,66},{66,2},{3,67},{67,3},{4,68},{68... | collective-permute-start | bytes 589832 | tf_op jit(solution)/shard_map/ppermute | solution.py:25
  6.1 2.2 %collective-permute-start.5 = (bf16[16,768]{1,0:T(8,128)(2,1)}, bf16[16,768]{1,0:T(8,128)(2,1)S(1)}, u32[]{:S(2)}, u32[]{:S(2)}) collective-permute-start(bf16[16,768]{1,0:T(8,128)(2,1)} %mine_ref.1), channel_id=1, source_target_pairs={{0,1},{1,0},{2,3},{3,2},{4,5},{5,4},{6,7},{7,6},{8,9},{9,8},{10,11... | collective-permute-start | bytes 73736 | tf_op jit(solution)/shard_map/ppermute | solution.py:25
  8.3 2.9 %collective-permute-done.5.other_ref = bf16[16,768]{1,0:T(8,128)(2,1)S(1)} collective-permute-done((bf16[16,768]{1,0:T(8,128)(2,1)}, bf16[16,768]{1,0:T(8,128)(2,1)S(1)}, u32[]{:S(2)}, u32[]{:S(2)}) %collective-permute-start.5) | collective-permute-done | bytes 24608 | tf_op jit(solution)/shard_map/ppermute | solution.py:25
  11.2 0.0 collective-permute-done.after_ref
  11.2 0.0 copy-start
  11.2 0.7 copy-done
  12.0 0.0 copy-start.9
  12.0 5.0 %copies.1 = bf16[16,2,16,768]{3,2,1,0:T(8,128)(2,1)} custom-call(s32[1]{0:T(128)} %bitcast.1.xl_ref, bf16[16,768]{1,0:T(8,128)(2,1)S(1)} %copy-done, bf16[16,768]{1,0:T(8,128)(2,1)S(1)} %collective-permute-done.5.other_ref, bf16[128,768]{1,0:T(8,128)(2,1)S(1)} %collective-permute-done.after_ref), custom_call_target="tpu_custom_call" | custom-call | bytes 786432 | tf_op jit(solution)/shard_map/copies/pallas_call | solution.py:81
  17.0 15.2 %all-to-all-start = ((bf16[16,2,16,768]{3,2,1,0:T(8,128)(2,1)}), bf16[16,2,16,768]{3,2,1,0:T(8,128)(2,1)S(1)}, u32[]{:S(2)}, u32[]{:S(2)}) async-start(bf16[16,2,16,768]{3,2,1,0:T(8,128)(2,1)} %copies.1), calls=%async_computation | async-start | bytes 1572864 | tf_op jit(solution)/shard_map/all_to_all | solution.py:33
  32.2 0.0 copy-done.9
  32.2 0.0 copy-start.11
  32.2 0.0 copy-start.10
  32.3 3.2 %collective-permute-start.1 = (bf16[256,768]{1,0:T(8,128)(2,1)S(1)}, bf16[256,768]{1,0:T(8,128)(2,1)S(1)}, u32[]{:S(2)}, u32[]{:S(2)}) collective-permute-start(bf16[256,768]{1,0:T(8,128)(2,1)S(1)} %get-tuple-element.36), channel_id=1, source_target_pairs={{0,128},{128,256},{256,384},{384,0},{1,129},{129,257},{257,385},{3... | collective-permute-start | bytes 1179656 | tf_op jit(solution)/shard_map/ppermute | solution.py:29
  35.5 3.4 %collective-permute-start.2 = (bf16[256,768]{1,0:T(8,128)(2,1)S(1)}, bf16[256,768]{1,0:T(8,128)(2,1)S(1)}, u32[]{:S(2)}, u32[]{:S(2)}) collective-permute-start(bf16[256,768]{1,0:T(8,128)(2,1)S(1)} %get-tuple-element.36), channel_id=1, source_target_pairs={{0,384},{128,0},{256,128},{384,256},{1,385},{129,1},{257,129},{385... | collective-permute-start | bytes 1179656 | tf_op jit(solution)/shard_map/ppermute | solution.py:29
  38.9 3.5 %collective-permute-start.3 = (bf16[256,768]{1,0:T(8,128)(2,1)S(1)}, bf16[256,768]{1,0:T(8,128)(2,1)S(1)}, u32[]{:S(2)}, u32[]{:S(2)}) collective-permute-start(bf16[256,768]{1,0:T(8,128)(2,1)S(1)} %get-tuple-element.36), channel_id=1, source_target_pairs={{0,256},{128,384},{256,0},{384,128},{1,257},{129,385},{257,1},{385... | collective-permute-start | bytes 1179656 | tf_op jit(solution)/shard_map/ppermute | solution.py:29
  42.4 2.0 %collective-permute-done.1 = bf16[256,768]{1,0:T(8,128)(2,1)S(1)} collective-permute-done((bf16[256,768]{1,0:T(8,128)(2,1)S(1)}, bf16[256,768]{1,0:T(8,128)(2,1)S(1)}, u32[]{:S(2)}, u32[]{:S(2)}) %collective-permute-start.1) | collective-permute-done | bytes 393248 | tf_op jit(solution)/shard_map/ppermute | solution.py:29
  44.4 1.6 collective-permute-done.2
  46.0 7.9 %collective-permute-done.3 = bf16[256,768]{1,0:T(8,128)(2,1)S(1)} collective-permute-done((bf16[256,768]{1,0:T(8,128)(2,1)S(1)}, bf16[256,768]{1,0:T(8,128)(2,1)S(1)}, u32[]{:S(2)}, u32[]{:S(2)}) %collective-permute-start.3) | collective-permute-done | bytes 393248 | tf_op jit(solution)/shard_map/ppermute | solution.py:29
  53.9 4.6 %collective-permute-start.4 = (bf16[1024,768]{1,0:T(8,128)(2,1)S(1)}, bf16[1024,768]{1,0:T(8,128)(2,1)}, u32[]{:S(2)}, u32[]{:S(2)}) collective-permute-start(bf16[1024,768]{1,0:T(8,128)(2,1)S(1)} %constant_dynamic-update-slice_fusion.2.x_ref.xqa_ref), channel_id=1, source_target_pairs={{0,32},{32,0},{1,33},{33,1},{2,34},{34,2},{3,35},{35,3},{4,36},{36... | collective-permute-start | bytes 4718600 | tf_op jit(solution)/shard_map/ppermute | solution.py:25
  58.5 0.0 copy-done.11
  58.6 0.1 copy.9.logc_ref
  58.7 0.1 iota_compare_fusion
  58.8 0.0 copy-done.10
  58.8 0.1 select_reduce_fusion
  59.0 0.0 copy-start.1
  59.0 1.3 copy-done.1
  60.2 2.9 %tower.2 = (bf16[1024,768]{1,0:T(8,128)(2,1)}, f32[1024,1]{1,0:T(8,128)}) custom-call(bf16[1024,768]{1,0:T(8,128)(2,1)S(1)} %constant_dynamic-update-slice_fusion.2.x_ref.xqa_ref, bf16[768,768]{1,0:T(8,128)(2,1)S(1)} %copy-done.1), custom_call_target="tpu_custom_call" | custom-call | flops 1207959552 | bytes 3145728 | tf_op jit(solution)/shard_map/tower/pallas_call | solution.py:103
  63.1 0.0 collective-permute-done.4.x_ref.xqb_ref
  63.1 4.1 %tower.3 = (bf16[1024,768]{1,0:T(8,128)(2,1)}, f32[1024,1]{1,0:T(8,128)}) custom-call(bf16[1024,768]{1,0:T(8,128)(2,1)} %collective-permute-done.4.x_ref.xqb_ref, bf16[768,768]{1,0:T(8,128)(2,1)S(1)} %copy-done.1), custom_call_target="tpu_custom_call" | custom-call | flops 1207959552 | bytes 3145728 | tf_op jit(solution)/shard_map/tower/pallas_call | solution.py:103
  67.2 0.0 all-to-all-done
  67.2 0.0 copy-start.2
  67.2 1.3 copy-done.2
  68.5 0.0 copy-start.3
  68.5 1.4 copy-done.3
  69.9 0.0 copy-start.5
  69.9 1.4 copy-done.5
  71.3 0.0 copy-start.4
  71.3 5.0 %score.1 = (bf16[512,768]{1,0:T(8,128)(2,1)S(1)}, f32[512,1]{1,0:T(8,128)S(1)}, f32[24,128]{1,0:T(8,128)S(1)}) custom-call(s32[16]{0:T(128)S(1)} %fusion.3.order_ref, bf16[1024,768]{1,0:T(8,128)(2,1)S(1)} %copy-done.3, bf16[1024,768]{1,0:T(8,128)(2,1)S(1)} %copy-done.5, bf16[768,768]{1,0:T(8,128)(2,1)S(1)} %copy-done.2, bf16[512,768]{1,0:T(8,128)(2,1)S(1)} %bitcast.17, ...), custom_call_target="tpu_custom_call" | custom-call | flops 2214592512 | bytes 6291456 | tf_op jit(solution)/shard_map/score/pallas_call | solution.py:144
  76.4 18.7 %all_to_all.30.parts_ref = f32[16,24,128]{2,1,0:T(8,128)S(1)} all-to-all(f32[16,24,128]{2,1,0:T(8,128)S(1)} %broadcast_in_dim.68), channel_id=1, replica_groups=mesh['y'=4,'xh'=2,'c'=2,'z'=16,'xl'=2] {'y','xh','c'}, dimensions={0} | all-to-all | bytes 393216 | tf_op jit(solution)/shard_map/all_to_all | solution.py:33
  95.1 0.0 copy-done.4
  95.1 0.0 copy-done.6
  95.1 0.0 copy-done.7
  95.1 0.0 copy-done.8
  95.1 13.1 %grads.1 = (bf16[384,768]{1,0:T(8,128)(2,1)S(1)}, bf16[384,768]{1,0:T(8,128)(2,1)S(1)}, f32[8,128]{1,0:T(8,128)S(1)}) custom-call(s32[1]{0:T(128)} %bitcast.core_ref, s32[16]{0:T(128)S(1)} %fusion.3.order_ref, f32[16,24,128]{2,1,0:T(8,128)S(1)} %all_to_all.30.parts_ref, bf16[1024,768]{1,0:T(8,128)(2,1)S(1)} %copy-done.4, bf16[1024,768]{1,0:T(8,128)(2,1)S(1)} %copy-done.6, ...), custom_call_target="tpu_custom_call" | custom-call | flops 7851737088 | bytes 9437184 | tf_op jit(solution)/shard_map/grads/pallas_call | solution.py:225
  108.2 2.7 %collective-permute-start.6 = (bf16[384,768]{1,0:T(8,128)(2,1)S(1)}, bf16[384,768]{1,0:T(8,128)(2,1)S(1)}, u32[]{:S(2)}, u32[]{:S(2)}) collective-permute-start(bf16[384,768]{1,0:T(8,128)(2,1)S(1)} %get-tuple-element.32), channel_id=1, source_target_pairs={{0,32},{32,0},{1,33},{33,1},{2,34},{34,2},{3,35},{35,3},{4,36},{36... | collective-permute-start | bytes 1769480 | tf_op jit(solution)/shard_map/ppermute | solution.py:25
  110.9 1.6 collective-permute-done.6
  112.5 0.9 add_convert_fusion
  113.4 3.6 %all-to-all-start.2 = ((bf16[16,24,768]{2,1,0:T(8,128)(2,1)}), bf16[16,24,768]{2,1,0:T(8,128)(2,1)S(1)}, u32[]{:S(2)}, u32[]{:S(2)}) async-start(bf16[16,24,768]{2,1,0:T(8,128)(2,1)} %bitcast.6), calls=%async_computation.2 | async-start | bytes 1179648 | tf_op jit(solution)/shard_map/all_to_all | solution.py:33
  117.0 3.1 %collective-permute-start.7 = (f32[8,128]{1,0:T(8,128)S(1)}, f32[8,128]{1,0:T(8,128)S(1)}, u32[]{:S(2)}, u32[]{:S(2)}) collective-permute-start(f32[8,128]{1,0:T(8,128)S(1)} %get-tuple-element.33), channel_id=1, source_target_pairs={{0,1},{1,0},{2,3},{3,2},{4,5},{5,4},{6,7},{7,6},{8,9},{9,8},{10,11... | collective-permute-start | bytes 12296 | tf_op jit(solution)/shard_map/ppermute | solution.py:25
  120.2 5.2 %collective-permute-done.7 = f32[8,128]{1,0:T(8,128)S(1)} collective-permute-done((f32[8,128]{1,0:T(8,128)S(1)}, f32[8,128]{1,0:T(8,128)S(1)}, u32[]{:S(2)}, u32[]{:S(2)}) %collective-permute-start.7) | collective-permute-done | bytes 4128 | tf_op jit(solution)/shard_map/ppermute | solution.py:25
  125.4 0.5 slice.25
  126.5 0.1 maximum_bitcast_fusion
  126.6 2.0 %all-to-all-done.2 = bf16[16,24,768]{2,1,0:T(8,128)(2,1)S(1)} async-done(((bf16[16,24,768]{2,1,0:T(8,128)(2,1)}), bf16[16,24,768]{2,1,0:T(8,128)(2,1)S(1)}, u32[]{:S(2)}, u32[]{:S(2)}) %all-to-all-start.2) | async-done | bytes 589856 | tf_op jit(solution)/shard_map/all_to_all | solution.py:33
  128.7 0.1 reduce_sum.40
  128.8 0.1 reshape.167
  128.9 19.2 %all_to_all.31 = bf16[16,16,128]{2,1,0:T(8,128)(2,1)S(1)} all-to-all(bf16[16,16,128]{2,1,0:T(8,128)(2,1)S(1)} %pad_maximum_fusion), channel_id=1, replica_groups=mesh['y'=4,'xh'=2,'c'=2,'z'=16,'xl'=2] {'z'}, dimensions={0} | all-to-all | bytes 131072 | tf_op jit(solution)/shard_map/all_to_all | solution.py:33
  148.1 14.4 %all_to_all.32 = bf16[16,16,128]{2,1,0:T(8,128)(2,1)S(1)} all-to-all(bf16[16,16,128]{2,1,0:T(8,128)(2,1)S(1)} %broadcast_in_dim.71), channel_id=1, replica_groups=mesh['y'=4,'xh'=2,'c'=2,'z'=16,'xl'=2] {'z'}, dimensions={0} | all-to-all | bytes 131072 | tf_op jit(solution)/shard_map/all_to_all | solution.py:33
  162.5 0.1 broadcast_in_dim.72
  162.7 13.4 %all_to_all.33 = bf16[16,24,768]{2,1,0:T(8,128)(2,1)S(1)} all-to-all(bf16[16,24,768]{2,1,0:T(8,128)(2,1)S(1)} %broadcast_in_dim.73), channel_id=1, replica_groups=mesh['y'=4,'xh'=2,'c'=2,'z'=16,'xl'=2] {'y','xh','xl'}, dimensions={0} | all-to-all | bytes 1179648 | tf_op jit(solution)/shard_map/all_to_all | solution.py:33
  176.1 7.3 %collective-permute-start.8 = (bf16[384,768]{1,0:T(8,128)(2,1)S(1)}, bf16[384,768]{1,0:T(8,128)(2,1)S(1)}, u32[]{:S(2)}, u32[]{:S(2)}) collective-permute-start(bf16[384,768]{1,0:T(8,128)(2,1)S(1)} %bitcast.21), channel_id=1, source_target_pairs={{0,32},{32,0},{1,33},{33,1},{2,34},{34,2},{3,35},{35,3},{4,36},{36... | collective-permute-start | bytes 1769480 | tf_op jit(solution)/shard_map/ppermute | solution.py:25
  183.4 0.6 slice_reduce_fusion
  184.0 1.0 collective-permute-done.8
  185.0 0.1 broadcast_select_fusion.1
  185.1 1.6 maximum_convert_fusion
  (20 shorter events, 0.3 us)
Async XLA Ops:
  0.6 10.6 %collective-permute-start = (bf16[128,768]{1,0:T(8,128)(2,1)}, bf16[128,768]{1,0:T(8,128)(2,1)S(1)}, u32[]{:S(2)}, u32[]{:S(2)}) collective-permute-start(bf16[128,768]{1,0:T(8,128)(2,1)} %param.7), channel_id=1, source_target_pairs={{0,64},{64,0},{1,65},{65,1},{2,66},{66,2},{3,67},{67,3},{4,68},{68... | collective-permute-start | bytes 589832 | tf_op jit(solution)/shard_map/ppermute | solution.py:25
  6.1 5.1 %collective-permute-start.5 = (bf16[16,768]{1,0:T(8,128)(2,1)}, bf16[16,768]{1,0:T(8,128)(2,1)S(1)}, u32[]{:S(2)}, u32[]{:S(2)}) collective-permute-start(bf16[16,768]{1,0:T(8,128)(2,1)} %mine_ref.1), channel_id=1, source_target_pairs={{0,1},{1,0},{2,3},{3,2},{4,5},{5,4},{6,7},{7,6},{8,9},{9,8},{10,11... | collective-permute-start | bytes 73736 | tf_op jit(solution)/shard_map/ppermute | solution.py:25
  11.2 0.7 copy-start
  12.0 20.2 %copy-start.9 = (bf16[128,768]{1,0:T(8,128)(2,1)S(1)}, bf16[128,768]{1,0:T(8,128)(2,1)}, u32[]{:S(2)}) copy-start(bf16[128,768]{1,0:T(8,128)(2,1)} %param.7) | copy-start | bytes 589828
  17.0 50.2 %all-to-all-start = ((bf16[16,2,16,768]{3,2,1,0:T(8,128)(2,1)}), bf16[16,2,16,768]{3,2,1,0:T(8,128)(2,1)S(1)}, u32[]{:S(2)}, u32[]{:S(2)}) async-start(bf16[16,2,16,768]{3,2,1,0:T(8,128)(2,1)} %copies.1), calls=%async_computation | async-start | bytes 1572864 | tf_op jit(solution)/shard_map/all_to_all | solution.py:33
  32.2 26.3 %copy-start.11 = (s32[512]{0:T(512)S(1)}, s32[512]{0:T(512)}, u32[]{:S(2)}) copy-start(s32[512]{0:T(512)} %param.10) | copy-start | bytes 6148
  32.2 26.6 %copy-start.10 = (s32[2048]{0:T(1024)S(1)}, s32[2048]{0:T(1024)}, u32[]{:S(2)}) copy-start(s32[2048]{0:T(1024)} %param.11) | copy-start | bytes 24580
  32.3 12.1 %collective-permute-start.1 = (bf16[256,768]{1,0:T(8,128)(2,1)S(1)}, bf16[256,768]{1,0:T(8,128)(2,1)S(1)}, u32[]{:S(2)}, u32[]{:S(2)}) collective-permute-start(bf16[256,768]{1,0:T(8,128)(2,1)S(1)} %get-tuple-element.36), channel_id=1, source_target_pairs={{0,128},{128,256},{256,384},{384,0},{1,129},{129,257},{257,385},{3... | collective-permute-start | bytes 1179656 | tf_op jit(solution)/shard_map/ppermute | solution.py:29
  35.5 10.5 %collective-permute-start.2 = (bf16[256,768]{1,0:T(8,128)(2,1)S(1)}, bf16[256,768]{1,0:T(8,128)(2,1)S(1)}, u32[]{:S(2)}, u32[]{:S(2)}) collective-permute-start(bf16[256,768]{1,0:T(8,128)(2,1)S(1)} %get-tuple-element.36), channel_id=1, source_target_pairs={{0,384},{128,0},{256,128},{384,256},{1,385},{129,1},{257,129},{385... | collective-permute-start | bytes 1179656 | tf_op jit(solution)/shard_map/ppermute | solution.py:29
  38.9 15.0 %collective-permute-start.3 = (bf16[256,768]{1,0:T(8,128)(2,1)S(1)}, bf16[256,768]{1,0:T(8,128)(2,1)S(1)}, u32[]{:S(2)}, u32[]{:S(2)}) collective-permute-start(bf16[256,768]{1,0:T(8,128)(2,1)S(1)} %get-tuple-element.36), channel_id=1, source_target_pairs={{0,256},{128,384},{256,0},{384,128},{1,257},{129,385},{257,1},{385... | collective-permute-start | bytes 1179656 | tf_op jit(solution)/shard_map/ppermute | solution.py:29
  53.9 9.2 %collective-permute-start.4 = (bf16[1024,768]{1,0:T(8,128)(2,1)S(1)}, bf16[1024,768]{1,0:T(8,128)(2,1)}, u32[]{:S(2)}, u32[]{:S(2)}) collective-permute-start(bf16[1024,768]{1,0:T(8,128)(2,1)S(1)} %constant_dynamic-update-slice_fusion.2.x_ref.xqa_ref), channel_id=1, source_target_pairs={{0,32},{32,0},{1,33},{33,1},{2,34},{34,2},{3,35},{35,3},{4,36},{36... | collective-permute-start | bytes 4718600 | tf_op jit(solution)/shard_map/ppermute | solution.py:25
  59.0 1.3 copy-start.1
  67.2 1.3 copy-start.2
  68.5 1.4 copy-start.3
  69.9 1.4 copy-start.5
  71.3 23.8 %copy-start.4 = (bf16[1024,768]{1,0:T(8,128)(2,1)S(1)}, bf16[1024,768]{1,0:T(8,128)(2,1)}, u32[]{:S(2)}) copy-start(bf16[1024,768]{1,0:T(8,128)(2,1)} %get-tuple-element.24.eqa_ref) | copy-start | bytes 4718596
  71.3 23.8 %copy-start.6 = (bf16[1024,768]{1,0:T(8,128)(2,1)S(1)}, bf16[1024,768]{1,0:T(8,128)(2,1)}, u32[]{:S(2)}) copy-start(bf16[1024,768]{1,0:T(8,128)(2,1)} %get-tuple-element.25.eqb_ref) | copy-start | bytes 4718596
  71.3 23.8 %copy-start.7 = (f32[1024,1]{1,0:T(8,128)S(1)}, f32[1024,1]{1,0:T(8,128)}, u32[]{:S(2)}) copy-start(f32[1024,1]{1,0:T(8,128)} %get-tuple-element.27.inva_ref) | copy-start | bytes 12292
  71.3 23.8 %copy-start.8 = (f32[1024,1]{1,0:T(8,128)S(1)}, f32[1024,1]{1,0:T(8,128)}, u32[]{:S(2)}) copy-start(f32[1024,1]{1,0:T(8,128)} %get-tuple-element.28.invb_ref) | copy-start | bytes 12292
  108.2 4.3 %collective-permute-start.6 = (bf16[384,768]{1,0:T(8,128)(2,1)S(1)}, bf16[384,768]{1,0:T(8,128)(2,1)S(1)}, u32[]{:S(2)}, u32[]{:S(2)}) collective-permute-start(bf16[384,768]{1,0:T(8,128)(2,1)S(1)} %get-tuple-element.32), channel_id=1, source_target_pairs={{0,32},{32,0},{1,33},{33,1},{2,34},{34,2},{3,35},{35,3},{4,36},{36... | collective-permute-start | bytes 1769480 | tf_op jit(solution)/shard_map/ppermute | solution.py:25
  113.4 15.2 %all-to-all-start.2 = ((bf16[16,24,768]{2,1,0:T(8,128)(2,1)}), bf16[16,24,768]{2,1,0:T(8,128)(2,1)S(1)}, u32[]{:S(2)}, u32[]{:S(2)}) async-start(bf16[16,24,768]{2,1,0:T(8,128)(2,1)} %bitcast.6), calls=%async_computation.2 | async-start | bytes 1179648 | tf_op jit(solution)/shard_map/all_to_all | solution.py:33
  117.0 8.3 %collective-permute-start.7 = (f32[8,128]{1,0:T(8,128)S(1)}, f32[8,128]{1,0:T(8,128)S(1)}, u32[]{:S(2)}, u32[]{:S(2)}) collective-permute-start(f32[8,128]{1,0:T(8,128)S(1)} %get-tuple-element.33), channel_id=1, source_target_pairs={{0,1},{1,0},{2,3},{3,2},{4,5},{5,4},{6,7},{7,6},{8,9},{9,8},{10,11... | collective-permute-start | bytes 12296 | tf_op jit(solution)/shard_map/ppermute | solution.py:25
  176.1 8.9 %collective-permute-start.8 = (bf16[384,768]{1,0:T(8,128)(2,1)S(1)}, bf16[384,768]{1,0:T(8,128)(2,1)S(1)}, u32[]{:S(2)}, u32[]{:S(2)}) collective-permute-start(bf16[384,768]{1,0:T(8,128)(2,1)S(1)} %bitcast.21), channel_id=1, source_target_pairs={{0,32},{32,0},{1,33},{33,1},{2,34},{34,2},{3,35},{35,3},{4,36},{36... | collective-permute-start | bytes 1769480 | tf_op jit(solution)/shard_map/ppermute | solution.py:25

commit v4 on v3

--- a/solution.py
+++ b/solution.py
@@ -18,7 +18,10 @@
 IB = 512
 HALF = 1024
 CH = 512
+CG = 512
 INV_NORM = 1.0 / ROWS**0.5
+LOG2_NORM = -8.0
+LOG2E = 1.4426950408889634
 
 
 def swap(x, axis):
@@ -62,37 +65,31 @@
     return pl.BlockSpec(s, lambda i: (0,) * len(s))
 
 
-def first(c):
-    return pl.BlockSpec((CH, c), lambda i: (jnp.minimum(i, HALF // CH - 1), 0))
-
-
-def second(c):
-    return pl.BlockSpec((CH, c), lambda i: (jnp.maximum(i - HALF // CH, 0), 0))
-
-
-def copies_kernel(xl_ref, mine_ref, other_ref, after_ref, out_ref):
-    xl = xl_ref[0]
-    out_ref[0, xl] = mine_ref[...]
-    out_ref[0, 1 - xl] = other_ref[...]
-
-
-def copies(xl, mine, other, after):
-    n = mine.shape[0]
+def first(n, c):
+    return pl.BlockSpec((n, c), lambda i: (jnp.minimum(i, HALF // n - 1), 0))
+
+
+def second(n, c):
+    return pl.BlockSpec((n, c), lambda i: (jnp.maximum(i - HALF // n, 0), 0))
+
+
+def join_kernel(two_ref, a_ref, b_ref, c_ref, after_ref, out_ref):
+    n = two_ref.shape[0]
+    for k, ref in enumerate((two_ref, a_ref, b_ref, c_ref)):
+        out_ref[k * n:(k + 1) * n, :] = ref[...]
+
+
+def join(two, a, b, c, after):
+    n = two.shape[0]
     return pl.pallas_call(
-        copies_kernel,
-        grid=(16,),
-        in_specs=[
-            pl.BlockSpec(memory_space=pltpu.SMEM),
-            whole(n, D),
-            whole(n, D),
-            pl.BlockSpec(memory_space=pl.ANY),
-        ],
-        out_specs=pl.BlockSpec((1, 2, n, D), lambda i: (i, 0, 0, 0)),
-        out_shape=jax.ShapeDtypeStruct((16, 2, n, D), BF),
-        compiler_params=pltpu.CompilerParams(vmem_limit_bytes=4 << 20),
-        cost_estimate=pl.CostEstimate(flops=0, bytes_accessed=32 * n * D * 2, transcendentals=0),
-        name="copies",
-    )(xl.reshape(1), mine, other, after)
+        join_kernel,
+        in_specs=[pl.BlockSpec(memory_space=pltpu.VMEM)] * 4 + [pl.BlockSpec(memory_space=pl.ANY)],
+        out_specs=pl.BlockSpec(memory_space=pltpu.VMEM),
+        out_shape=jax.ShapeDtypeStruct((4 * n, D), BF),
+        compiler_params=pltpu.CompilerParams(vmem_limit_bytes=8 << 20),
+        cost_estimate=pl.CostEstimate(flops=0, bytes_accessed=16 * n * D, transcendentals=0),
+        name="join",
+    )(two, a, b, c, after)
 
 
 def tower_kernel(x_ref, w_ref, e_ref, inv_ref):
@@ -112,13 +109,15 @@
     )(x, weight)
 
 
-def score_kernel(order_ref, eqa_ref, eqb_ref, w_ref, xi_ref, logc_ref, ids_ref, tgt_ref,
+def score_kernel(order_ref, eqa_ref, eqb_ref, w_ref, near_ref, far_ref, logc_ref, ids_ref, tgt_ref,
                  ei_ref, invi_ref, stat_ref):
     i = pl.program_id(0)
 
     @pl.when(i == 0)
     def _():
-        ei_ref[...], invi_ref[...] = unit_rows(xi_ref[...], w_ref[...])
+        for k, ref in enumerate((near_ref, far_ref)):
+            part = slice(k * (IB // 2), (k + 1) * (IB // 2))
+            ei_ref[part, :], invi_ref[part, :] = unit_rows(ref[...], w_ref[...])
         stat_ref[...] = jnp.zeros_like(stat_ref)
 
     def run(eq):
@@ -140,16 +139,17 @@
         run(eqb_ref[...])
 
 
-def score(order, eqa, eqb, weight, xi, logc, ids, targets):
+def score(order, eqa, eqb, weight, near, far, logc, ids, targets):
     return pl.pallas_call(
         score_kernel,
         grid=(QB // CH,),
         in_specs=[
             pl.BlockSpec(memory_space=pltpu.SMEM),
-            first(D),
-            second(D),
+            first(CH, D),
+            second(CH, D),
             whole(D, D),
-            whole(IB, D),
+            whole(IB // 2, D),
+            whole(IB // 2, D),
             whole(IB, 1),
             whole(IB, 1),
             pl.BlockSpec((1, CH), lambda i: (0, i)),
@@ -165,11 +165,11 @@
             flops=2 * IB * D * (D + QB), bytes_accessed=6 << 20, transcendentals=IB * QB
         ),
         name="score",
-    )(order, eqa, eqb, weight, xi, logc, ids, targets)
+    )(order, eqa, eqb, weight, near, far, logc, ids, targets)
 
 
 def grad_kernel(core_ref, order_ref, parts_ref, eqa_ref, eqb_ref, inva_ref, invb_ref, xqa_ref, xqb_ref,
-                ei_ref, invi_ref, xi_ref, logc_ref, ids_ref, tgt_ref,
+                ei_ref, invi_ref, near_ref, far_ref, logc_ref, ids_ref, tgt_ref,
                 send_ref, keep_ref, loss_ref, lse_ref, di_ref, acc_ref):
     i = pl.program_id(0)
     core = core_ref[0]
@@ -188,59 +188,61 @@
 
     def run(eq_ref, inv_ref, xq_ref):
         eq = eq_ref[...]
-        rows = [order_ref[i * (CH // 128) + k] for k in range(CH // 128)]
+        rows = [order_ref[i * (CG // 128) + k] for k in range(CG // 128)]
         lse = jnp.concatenate([lse_ref[pl.ds(r, 1), :] for r in rows], axis=1)
-        prob = jnp.exp(score_tile(ei_ref, eq, logc_ref) - lse)
-        hit = ids_ref[...] == tgt_ref[...]
-        grad = ((prob - jnp.where(hit, 1.0, 0.0)) * INV_NORM).astype(BF)
+        power = dot(ei_ref[...], eq, ((1,), (1,))) * (100.0 * LOG2E) - logc_ref[...] * LOG2E
+        prob = jnp.exp2(power - (lse * LOG2E - LOG2_NORM))
+        grad = jnp.where(ids_ref[...] == tgt_ref[...], prob - INV_NORM, prob).astype(BF)
         di_ref[...] += dot(grad, eq, ((1,), (0,)))
-        dq = 100.0 * dot(grad, ei_ref[...], ((0,), (0,)))
+        dq = dot(grad, ei_ref[...], ((0,), (0,)))
         eq = eq.astype(F32)
         inner = jnp.sum(eq * dq, axis=1, keepdims=True)
-        dz = ((dq - eq * inner) * inv_ref[...]).astype(BF)
+        dz = ((dq - eq * inner) * (100.0 * inv_ref[...])).astype(BF)
         acc_ref[...] += dot(xq_ref[...], dz, ((0,), (0,)))
 
-    @pl.when(i < HALF // CH)
+    @pl.when(i < HALF // CG)
     def _():
         run(eqa_ref, inva_ref, xqa_ref)
 
-    @pl.when(i >= HALF // CH)
+    @pl.when(i >= HALF // CG)
     def _():
         run(eqb_ref, invb_ref, xqb_ref)
 
-    @pl.when(i == QB // CH - 1)
+    @pl.when(i == QB // CG - 1)
     def _():
         di = 100.0 * di_ref[...]
         ei = ei_ref[...].astype(F32)
         inner = jnp.sum(ei * di, axis=1, keepdims=True)
         dz = ((di - ei * inner) * invi_ref[...]).astype(BF)
-        acc_ref[...] += dot(xi_ref[...], dz, ((0,), (0,)))
+        for k, ref in enumerate((near_ref, far_ref)):
+            acc_ref[...] += dot(ref[...], dz[k * (IB // 2):(k + 1) * (IB // 2)], ((0,), (0,)))
         mine = pl.ds(pl.multiple_of(core * (D // 2), D // 2), D // 2)
         theirs = pl.ds(pl.multiple_of((1 - core) * (D // 2), D // 2), D // 2)
         keep_ref[...] = acc_ref[mine, :].astype(BF)
         send_ref[...] = acc_ref[theirs, :].astype(BF)
 
 
-def grads(core, order, parts, eqa, eqb, inva, invb, xqa, xqb, ei, invi, xi, logc, ids, targets):
+def grads(core, order, parts, eqa, eqb, inva, invb, xqa, xqb, ei, invi, near, far, logc, ids, targets):
     return pl.pallas_call(
         grad_kernel,
-        grid=(QB // CH,),
+        grid=(QB // CG,),
         in_specs=[
             pl.BlockSpec(memory_space=pltpu.SMEM),
             pl.BlockSpec(memory_space=pltpu.SMEM),
             whole(16, 24, 128),
-            first(D),
-            second(D),
-            first(1),
-            second(1),
-            first(D),
-            second(D),
+            first(CG, D),
+            second(CG, D),
+            first(CG, 1),
+            second(CG, 1),
+            first(CG, D),
+            second(CG, D),
             whole(IB, D),
             whole(IB, 1),
-            whole(IB, D),
-            whole(IB, 1),
-            whole(IB, 1),
-            pl.BlockSpec((1, CH), lambda i: (0, i)),
+            whole(IB // 2, D),
+            whole(IB // 2, D),
+            whole(IB, 1),
+            whole(IB, 1),
+            pl.BlockSpec((1, CG), lambda i: (0, i)),
         ],
         out_specs=[whole(D // 2, D), whole(D // 2, D), whole(8, 128)],
         out_shape=[
@@ -258,18 +260,17 @@
             flops=2 * IB * D * 3 * QB + 2 * D * D * (QB + IB), bytes_accessed=9 << 20, transcendentals=IB * QB
         ),
         name="grads",
-    )(core, order, parts, eqa, eqb, inva, invb, xqa, xqb, ei, invi, xi, logc, ids, targets)
+    )(core, order, parts, eqa, eqb, inva, invb, xqa, xqb, ei, invi, near, far, logc, ids, targets)
 
 
 def body(xq_own, xi_own, weight, counts, positives):
     core, y, xh = lax.axis_index("c"), lax.axis_index("y"), lax.axis_index("xh")
     xl = lax.axis_index("xl")
-    far = swap(xi_own, "xl")
-    side = swap(xq_own, "xh")
-    two = jnp.concatenate([xq_own, side])
-    xqa = jnp.concatenate([two, turn(two, 1), turn(two, 3), turn(two, 2)])
+    near = gather(xi_own, "z", 16).reshape(IB // 2, D)
+    far = swap(near, "xl")
+    two = jnp.concatenate([xq_own, swap(xq_own, "xh")])
+    xqa = join(two, turn(two, 1), turn(two, 3), turn(two, 2), near)
     xqb = swap(xqa, "c")
-    xi = exchange(copies(xl, xi_own, far, side), "z").reshape(IB, D)
 
     q = lax.iota(jnp.int32, 16)
     step = (q // 2) % 4
@@ -278,15 +279,18 @@
     picks = order[:, None, None] == q[None, :, None]
     targets = jnp.sum(jnp.where(picks, positives.reshape(1, 16, 128), 0), axis=1).reshape(1, QB)
     block = (y * 2 + xh) * 2 + core
-    ids = (block * IB + lax.iota(jnp.int32, IB))[:, None]
-    logc = jnp.log(counts.astype(F32))[:, None]
+    at = lax.iota(jnp.int32, IB)
+    ids = ((at // 16) % 16 * 2 + (xl ^ (at // 256))) * 16 + at % 16
+    logs = jnp.log(counts.astype(F32))
+    logc = jnp.sum(jnp.where(ids[:, None] == at[None, :], logs[None, :], 0.0), axis=1, keepdims=True)
+    ids = (block * IB + ids)[:, None]
 
     eqa, inva = tower(xqa, weight)
     eqb, invb = tower(xqb, weight)
-    ei, invi, stat = score(order, eqa, eqb, weight, xi, logc, ids, targets)
+    ei, invi, stat = score(order, eqa, eqb, weight, near, far, logc, ids, targets)
     parts = gather(stat, POOL, 16)
     send, keep, loss = grads(
-        core.reshape(1), order, parts, eqa, eqb, inva, invb, xqa, xqb, ei, invi, xi, logc, ids, targets
+        core.reshape(1), order, parts, eqa, eqb, inva, invb, xqa, xqb, ei, invi, near, far, logc, ids, targets
     )
 
     loss = (loss + swap(loss, "xl"))[0, 0] / ROWS

time: 188 us -> 185 us (0.984)
  Pallas kernels: 30 us -> 24.9 us
    pallas_call x2, Pallas kernels: 18.1 us -> 12.9 us  [the longest x1 12.8 us: grads(): pl.pallas_call(grad_kernel, grid=(QB // CG,), in_specs=[pl.BlockSpec(memo...]
    unnamed x27 -> x17, local copies, waits for them, and re-layouts: 6.2 us -> 3.65 us
  transfers between devices with their start and end apart: 11 -> 11, of which waited for: 8 -> 9; matrix products, arithmetic and copies ran while one was open for 1% -> 2% of each run, Pallas kernels for 4% -> 4%
where the time goes in v4:
time: 185 us; the launch traced here: 184 us
  blocking collectives  66.6 us (36%)
  starting transfers between devices  55 us (30%)
  waiting for transfers between devices  25.5 us (14%)
  Pallas kernels  24.9 us (13%)
  local copies, waits for them, and re-layouts  6.06 us (3%)
  other arithmetic  4.03 us (2%)
    all_to_all x4, blocking collectives, exchange(): return lax.all_to_all(x, axes, 0, 0, tiled=True)  66.6 us
    ppermute x6, starting transfers between devices, swap(): return lax.ppermute(x, axis, [(0, 1), (1, 0)])  25.6 us
    all_to_all x2, starting transfers between devices, exchange(): return lax.all_to_all(x, axes, 0, 0, tiled=True)  19.3 us
    pallas_call x1, Pallas kernels, grads(): pl.pallas_call(grad_kernel, grid=(QB // CG,), in_specs=[pl.BlockSpec(memo...  12.8 us
    ppermute x6, waiting for transfers between devices, swap(): return lax.ppermute(x, axis, [(0, 1), (1, 0)])  12 us
    ppermute x3, waiting for transfers between devices, turn(): return lax.ppermute(x, 'y', [(i, (i + k) % 4) for i in range(4)])  11.4 us
    ppermute x3, starting transfers between devices, turn(): return lax.ppermute(x, 'y', [(i, (i + k) % 4) for i in range(4)])  10.1 us
    pallas_call x2, Pallas kernels, tower(): pl.pallas_call(tower_kernel, grid=(HALF // CH,), in_specs=[pl.BlockSpec((...  7.01 us
  transfers between devices with their start and end apart: 11, of which 9 were waited for; matrix products, arithmetic and copies ran while one was open for 2% of the time, Pallas kernels for 4%

profile of v4, /device:TPU:1, one launch (start us, length us, event | category | flops | bytes accessed | tf_op | source)
XLA Modules:
  0.0 183.6 jit_solution(12148281750549508785)
XLA Ops:
  0.6 1.5 broadcast_in_dim.84
  2.1 15.7 %all-to-all-start = ((bf16[16,16,768]{2,1,0:T(8,128)(2,1)}), bf16[16,16,768]{2,1,0:T(8,128)(2,1)S(1)}, u32[]{:S(2)}, u32[]{:S(2)}) async-start(bf16[16,16,768]{2,1,0:T(8,128)(2,1)} %broadcast_in_dim.84), calls=%async_computation | async-start | bytes 786432 | tf_op jit(solution)/shard_map/all_to_all | solution.py:36
  17.9 4.7 %collective-permute-start = (bf16[128,768]{1,0:T(8,128)(2,1)}, bf16[128,768]{1,0:T(8,128)(2,1)S(1)}, u32[]{:S(2)}, u32[]{:S(2)}) collective-permute-start(bf16[128,768]{1,0:T(8,128)(2,1)} %param.7), channel_id=1, source_target_pairs={{0,64},{64,0},{1,65},{65,1},{2,66},{66,2},{3,67},{67,3},{4,68},{68... | collective-permute-start | bytes 589832 | tf_op jit(solution)/shard_map/ppermute | solution.py:28
  22.6 1.0 constant_dynamic-update-slice_fusion.1
  23.5 3.4 %collective-permute-done = bf16[128,768]{1,0:T(8,128)(2,1)S(1)} collective-permute-done((bf16[128,768]{1,0:T(8,128)(2,1)}, bf16[128,768]{1,0:T(8,128)(2,1)S(1)}, u32[]{:S(2)}, u32[]{:S(2)}) %collective-permute-start) | collective-permute-done | bytes 196640 | tf_op jit(solution)/shard_map/ppermute | solution.py:28
  27.0 3.2 %collective-permute-start.1 = (bf16[256,768]{1,0:T(8,128)(2,1)S(1)}, bf16[256,768]{1,0:T(8,128)(2,1)S(1)}, u32[]{:S(2)}, u32[]{:S(2)}) collective-permute-start(bf16[256,768]{1,0:T(8,128)(2,1)S(1)} %constant_dynamic-update-slice_fusion.two_ref), channel_id=1, source_target_pairs={{0,128},{128,256},{256,384},{384,0},{1,129},{129,257},{257,385},{3... | collective-permute-start | bytes 1179656 | tf_op jit(solution)/shard_map/ppermute | solution.py:32
  30.2 3.4 %collective-permute-start.2 = (bf16[256,768]{1,0:T(8,128)(2,1)S(1)}, bf16[256,768]{1,0:T(8,128)(2,1)S(1)}, u32[]{:S(2)}, u32[]{:S(2)}) collective-permute-start(bf16[256,768]{1,0:T(8,128)(2,1)S(1)} %constant_dynamic-update-slice_fusion.two_ref), channel_id=1, source_target_pairs={{0,384},{128,0},{256,128},{384,256},{1,385},{129,1},{257,129},{385... | collective-permute-start | bytes 1179656 | tf_op jit(solution)/shard_map/ppermute | solution.py:32
  33.5 3.5 %collective-permute-start.3 = (bf16[256,768]{1,0:T(8,128)(2,1)S(1)}, bf16[256,768]{1,0:T(8,128)(2,1)S(1)}, u32[]{:S(2)}, u32[]{:S(2)}) collective-permute-start(bf16[256,768]{1,0:T(8,128)(2,1)S(1)} %constant_dynamic-update-slice_fusion.two_ref), channel_id=1, source_target_pairs={{0,256},{128,384},{256,0},{384,128},{1,257},{129,385},{257,1},{385... | collective-permute-start | bytes 1179656 | tf_op jit(solution)/shard_map/ppermute | solution.py:32
  37.1 1.9 %collective-permute-done.1.a_ref = bf16[256,768]{1,0:T(8,128)(2,1)S(1)} collective-permute-done((bf16[256,768]{1,0:T(8,128)(2,1)S(1)}, bf16[256,768]{1,0:T(8,128)(2,1)S(1)}, u32[]{:S(2)}, u32[]{:S(2)}) %collective-permute-start.1) | collective-permute-done | bytes 393248 | tf_op jit(solution)/shard_map/ppermute | solution.py:32
  39.0 1.6 collective-permute-done.2.b_ref
  40.5 7.9 %collective-permute-done.3.c_ref = bf16[256,768]{1,0:T(8,128)(2,1)S(1)} collective-permute-done((bf16[256,768]{1,0:T(8,128)(2,1)S(1)}, bf16[256,768]{1,0:T(8,128)(2,1)S(1)}, u32[]{:S(2)}, u32[]{:S(2)}) %collective-permute-start.3) | collective-permute-done | bytes 393248 | tf_op jit(solution)/shard_map/ppermute | solution.py:32
  48.5 0.0 all-to-all-done
  48.5 0.0 copy-start.7
  48.5 0.0 copy-start.6
  48.5 0.1 join.1.x_ref.xqa_ref
  48.6 4.7 %collective-permute-start.4 = (bf16[1024,768]{1,0:T(8,128)(2,1)S(1)}, bf16[1024,768]{1,0:T(8,128)(2,1)}, u32[]{:S(2)}, u32[]{:S(2)}) collective-permute-start(bf16[1024,768]{1,0:T(8,128)(2,1)S(1)} %join.1.x_ref.xqa_ref), channel_id=1, source_target_pairs={{0,32},{32,0},{1,33},{33,1},{2,34},{34,2},{3,35},{35,3},{4,36},{36... | collective-permute-start | bytes 4718600 | tf_op jit(solution)/shard_map/ppermute | solution.py:28
  53.3 0.0 copy-done.7
  53.4 0.2 select_reduce_fusion
  53.6 0.1 iota_compare_fusion.1
  53.7 3.1 %collective-permute-start.5 = (bf16[256,768]{1,0:T(8,128)(2,1)S(1)}, bf16[256,768]{1,0:T(8,128)(2,1)S(1)}, u32[]{:S(2)}, u32[]{:S(2)}) collective-permute-start(bf16[256,768]{1,0:T(8,128)(2,1)S(1)} %bitcast.17), channel_id=1, source_target_pairs={{0,1},{1,0},{2,3},{3,2},{4,5},{5,4},{6,7},{7,6},{8,9},{9,8},{10,11... | collective-permute-start | bytes 1179656 | tf_op jit(solution)/shard_map/ppermute | solution.py:28
  56.8 0.0 copy-done.6
  56.8 0.1 select_reduce_fusion.1
  57.0 0.1 copy.12.logc_ref
  57.1 0.1 fusion.11.ids_ref
  57.2 0.0 copy-start
  57.2 1.3 copy-done
  58.5 2.9 %tower.2 = (bf16[1024,768]{1,0:T(8,128)(2,1)}, f32[1024,1]{1,0:T(8,128)}) custom-call(bf16[1024,768]{1,0:T(8,128)(2,1)S(1)} %join.1.x_ref.xqa_ref, bf16[768,768]{1,0:T(8,128)(2,1)S(1)} %copy-done), custom_call_target="tpu_custom_call" | custom-call | flops 1207959552 | bytes 3145728 | tf_op jit(solution)/shard_map/tower/pallas_call | solution.py:100
  61.4 0.0 copy-start.1
  61.4 0.0 collective-permute-done.4.x_ref.xqb_ref
  61.4 4.1 %tower.3 = (bf16[1024,768]{1,0:T(8,128)(2,1)}, f32[1024,1]{1,0:T(8,128)}) custom-call(bf16[1024,768]{1,0:T(8,128)(2,1)} %collective-permute-done.4.x_ref.xqb_ref, bf16[768,768]{1,0:T(8,128)(2,1)S(1)} %copy-done), custom_call_target="tpu_custom_call" | custom-call | flops 1207959552 | bytes 3145728 | tf_op jit(solution)/shard_map/tower/pallas_call | solution.py:100
  65.5 0.8 collective-permute-done.5.far_ref
  66.3 0.0 copy-done.1
  66.3 0.0 copy-start.2
  66.3 1.4 copy-done.2
  67.7 0.0 copy-start.3
  67.7 0.0 copy-start.4
  67.7 0.0 copy-start.5
  67.7 5.0 %score.1 = (bf16[512,768]{1,0:T(8,128)(2,1)S(1)}, f32[512,1]{1,0:T(8,128)S(1)}, f32[24,128]{1,0:T(8,128)S(1)}) custom-call(s32[16]{0:T(128)S(1)} %fusion.33.order_ref, bf16[1024,768]{1,0:T(8,128)(2,1)S(1)} %copy-done.1, bf16[1024,768]{1,0:T(8,128)(2,1)S(1)} %copy-done.2, bf16[768,768]{1,0:T(8,128)(2,1)S(1)} %copy-done, bf16[256,768]{1,0:T(8,128)(2,1)S(1)} %bitcast.18, ...), custom_call_target="tpu_custom_call" | custom-call | flops 2214592512 | bytes 6291456 | tf_op jit(solution)/shard_map/score/pallas_call | solution.py:143
  72.7 16.2 %all_to_all.30.parts_ref = f32[16,24,128]{2,1,0:T(8,128)S(1)} all-to-all(f32[16,24,128]{2,1,0:T(8,128)S(1)} %broadcast_in_dim.92), channel_id=1, replica_groups=mesh['y'=4,'xh'=2,'c'=2,'z'=16,'xl'=2] {'y','xh','c'}, dimensions={0} | all-to-all | bytes 393216 | tf_op jit(solution)/shard_map/all_to_all | solution.py:36
  89.0 0.0 copy-done.3
  89.0 0.0 copy-done.4
  89.0 0.0 copy-done.5
  89.0 12.8 %grads.1 = (bf16[384,768]{1,0:T(8,128)(2,1)S(1)}, bf16[384,768]{1,0:T(8,128)(2,1)S(1)}, f32[8,128]{1,0:T(8,128)S(1)}) custom-call(s32[1]{0:T(128)} %bitcast.core_ref, s32[16]{0:T(128)S(1)} %fusion.33.order_ref, f32[16,24,128]{2,1,0:T(8,128)S(1)} %all_to_all.30.parts_ref, bf16[1024,768]{1,0:T(8,128)(2,1)S(1)} %copy-done.1, bf16[1024,768]{1,0:T(8,128)(2,1)S(1)} %copy-done.3, ...), custom_call_target="tpu_custom_call" | custom-call | flops 7851737088 | bytes 9437184 | tf_op jit(solution)/shard_map/grads/pallas_call | solution.py:226
  101.8 2.7 %collective-permute-start.6 = (bf16[384,768]{1,0:T(8,128)(2,1)S(1)}, bf16[384,768]{1,0:T(8,128)(2,1)S(1)}, u32[]{:S(2)}, u32[]{:S(2)}) collective-permute-start(bf16[384,768]{1,0:T(8,128)(2,1)S(1)} %get-tuple-element.32), channel_id=1, source_target_pairs={{0,32},{32,0},{1,33},{33,1},{2,34},{34,2},{3,35},{35,3},{4,36},{36... | collective-permute-start | bytes 1769480 | tf_op jit(solution)/shard_map/ppermute | solution.py:28
  104.5 1.6 collective-permute-done.6
  106.1 0.9 add_convert_fusion
  107.0 3.6 %all-to-all-start.2 = ((bf16[16,24,768]{2,1,0:T(8,128)(2,1)}), bf16[16,24,768]{2,1,0:T(8,128)(2,1)S(1)}, u32[]{:S(2)}, u32[]{:S(2)}) async-start(bf16[16,24,768]{2,1,0:T(8,128)(2,1)} %bitcast.5), calls=%async_computation.2 | async-start | bytes 1179648 | tf_op jit(solution)/shard_map/all_to_all | solution.py:36
  110.6 3.1 %collective-permute-start.7 = (f32[8,128]{1,0:T(8,128)S(1)}, f32[8,128]{1,0:T(8,128)S(1)}, u32[]{:S(2)}, u32[]{:S(2)}) collective-permute-start(f32[8,128]{1,0:T(8,128)S(1)} %get-tuple-element.33), channel_id=1, source_target_pairs={{0,1},{1,0},{2,3},{3,2},{4,5},{5,4},{6,7},{7,6},{8,9},{9,8},{10,11... | collective-permute-start | bytes 12296 | tf_op jit(solution)/shard_map/ppermute | solution.py:28
  113.8 5.2 %collective-permute-done.7 = f32[8,128]{1,0:T(8,128)S(1)} collective-permute-done((f32[8,128]{1,0:T(8,128)S(1)}, f32[8,128]{1,0:T(8,128)S(1)}, u32[]{:S(2)}, u32[]{:S(2)}) %collective-permute-start.7) | collective-permute-done | bytes 4128 | tf_op jit(solution)/shard_map/ppermute | solution.py:28
  119.0 0.5 slice.25
  120.2 0.1 maximum_bitcast_fusion
  120.3 2.0 %all-to-all-done.2 = bf16[16,24,768]{2,1,0:T(8,128)(2,1)S(1)} async-done(((bf16[16,24,768]{2,1,0:T(8,128)(2,1)}), bf16[16,24,768]{2,1,0:T(8,128)(2,1)S(1)}, u32[]{:S(2)}, u32[]{:S(2)}) %all-to-all-start.2) | async-done | bytes 589856 | tf_op jit(solution)/shard_map/all_to_all | solution.py:36
  122.3 0.1 reduce_sum.50
  122.4 0.1 reshape.284
  122.5 22.5 %all_to_all.31 = bf16[16,16,128]{2,1,0:T(8,128)(2,1)S(1)} all-to-all(bf16[16,16,128]{2,1,0:T(8,128)(2,1)S(1)} %pad_maximum_fusion), channel_id=1, replica_groups=mesh['y'=4,'xh'=2,'c'=2,'z'=16,'xl'=2] {'z'}, dimensions={0} | all-to-all | bytes 131072 | tf_op jit(solution)/shard_map/all_to_all | solution.py:36
  145.1 14.4 %all_to_all.32 = bf16[16,16,128]{2,1,0:T(8,128)(2,1)S(1)} all-to-all(bf16[16,16,128]{2,1,0:T(8,128)(2,1)S(1)} %broadcast_in_dim.95), channel_id=1, replica_groups=mesh['y'=4,'xh'=2,'c'=2,'z'=16,'xl'=2] {'z'}, dimensions={0} | all-to-all | bytes 131072 | tf_op jit(solution)/shard_map/all_to_all | solution.py:36
  159.5 0.1 broadcast_in_dim.96
  159.6 13.5 %all_to_all.33 = bf16[16,24,768]{2,1,0:T(8,128)(2,1)S(1)} all-to-all(bf16[16,24,768]{2,1,0:T(8,128)(2,1)S(1)} %broadcast_in_dim.97), channel_id=1, replica_groups=mesh['y'=4,'xh'=2,'c'=2,'z'=16,'xl'=2] {'y','xh','xl'}, dimensions={0} | all-to-all | bytes 1179648 | tf_op jit(solution)/shard_map/all_to_all | solution.py:36
  173.1 7.3 %collective-permute-start.8 = (bf16[384,768]{1,0:T(8,128)(2,1)S(1)}, bf16[384,768]{1,0:T(8,128)(2,1)S(1)}, u32[]{:S(2)}, u32[]{:S(2)}) collective-permute-start(bf16[384,768]{1,0:T(8,128)(2,1)S(1)} %bitcast.22), channel_id=1, source_target_pairs={{0,32},{32,0},{1,33},{33,1},{2,34},{34,2},{3,35},{35,3},{4,36},{36... | collective-permute-start | bytes 1769480 | tf_op jit(solution)/shard_map/ppermute | solution.py:28
  180.3 0.6 slice_reduce_fusion
  180.9 1.0 collective-permute-done.8
  181.9 0.1 broadcast_select_fusion.1
  182.1 1.6 maximum_convert_fusion
  (13 shorter events, 0.2 us)
Async XLA Ops:
  2.1 46.4 %all-to-all-start = ((bf16[16,16,768]{2,1,0:T(8,128)(2,1)}), bf16[16,16,768]{2,1,0:T(8,128)(2,1)S(1)}, u32[]{:S(2)}, u32[]{:S(2)}) async-start(bf16[16,16,768]{2,1,0:T(8,128)(2,1)} %broadcast_in_dim.84), calls=%async_computation | async-start | bytes 786432 | tf_op jit(solution)/shard_map/all_to_all | solution.py:36
  17.9 9.1 %collective-permute-start = (bf16[128,768]{1,0:T(8,128)(2,1)}, bf16[128,768]{1,0:T(8,128)(2,1)S(1)}, u32[]{:S(2)}, u32[]{:S(2)}) collective-permute-start(bf16[128,768]{1,0:T(8,128)(2,1)} %param.7), channel_id=1, source_target_pairs={{0,64},{64,0},{1,65},{65,1},{2,66},{66,2},{3,67},{67,3},{4,68},{68... | collective-permute-start | bytes 589832 | tf_op jit(solution)/shard_map/ppermute | solution.py:28
  27.0 12.0 %collective-permute-start.1 = (bf16[256,768]{1,0:T(8,128)(2,1)S(1)}, bf16[256,768]{1,0:T(8,128)(2,1)S(1)}, u32[]{:S(2)}, u32[]{:S(2)}) collective-permute-start(bf16[256,768]{1,0:T(8,128)(2,1)S(1)} %constant_dynamic-update-slice_fusion.two_ref), channel_id=1, source_target_pairs={{0,128},{128,256},{256,384},{384,0},{1,129},{129,257},{257,385},{3... | collective-permute-start | bytes 1179656 | tf_op jit(solution)/shard_map/ppermute | solution.py:32
  30.2 10.4 %collective-permute-start.2 = (bf16[256,768]{1,0:T(8,128)(2,1)S(1)}, bf16[256,768]{1,0:T(8,128)(2,1)S(1)}, u32[]{:S(2)}, u32[]{:S(2)}) collective-permute-start(bf16[256,768]{1,0:T(8,128)(2,1)S(1)} %constant_dynamic-update-slice_fusion.two_ref), channel_id=1, source_target_pairs={{0,384},{128,0},{256,128},{384,256},{1,385},{129,1},{257,129},{385... | collective-permute-start | bytes 1179656 | tf_op jit(solution)/shard_map/ppermute | solution.py:32
  33.5 14.9 %collective-permute-start.3 = (bf16[256,768]{1,0:T(8,128)(2,1)S(1)}, bf16[256,768]{1,0:T(8,128)(2,1)S(1)}, u32[]{:S(2)}, u32[]{:S(2)}) collective-permute-start(bf16[256,768]{1,0:T(8,128)(2,1)S(1)} %constant_dynamic-update-slice_fusion.two_ref), channel_id=1, source_target_pairs={{0,256},{128,384},{256,0},{384,128},{1,257},{129,385},{257,1},{385... | collective-permute-start | bytes 1179656 | tf_op jit(solution)/shard_map/ppermute | solution.py:32
  48.5 4.9 %copy-start.7 = (s32[512]{0:T(512)S(1)}, s32[512]{0:T(512)}, u32[]{:S(2)}) copy-start(s32[512]{0:T(512)} %param.10) | copy-start | bytes 6148
  48.5 8.3 %copy-start.6 = (s32[2048]{0:T(1024)S(1)}, s32[2048]{0:T(1024)}, u32[]{:S(2)}) copy-start(s32[2048]{0:T(1024)} %param.11) | copy-start | bytes 24580
  48.6 12.8 %collective-permute-start.4 = (bf16[1024,768]{1,0:T(8,128)(2,1)S(1)}, bf16[1024,768]{1,0:T(8,128)(2,1)}, u32[]{:S(2)}, u32[]{:S(2)}) collective-permute-start(bf16[1024,768]{1,0:T(8,128)(2,1)S(1)} %join.1.x_ref.xqa_ref), channel_id=1, source_target_pairs={{0,32},{32,0},{1,33},{33,1},{2,34},{34,2},{3,35},{35,3},{4,36},{36... | collective-permute-start | bytes 4718600 | tf_op jit(solution)/shard_map/ppermute | solution.py:28
  53.7 12.6 %collective-permute-start.5 = (bf16[256,768]{1,0:T(8,128)(2,1)S(1)}, bf16[256,768]{1,0:T(8,128)(2,1)S(1)}, u32[]{:S(2)}, u32[]{:S(2)}) collective-permute-start(bf16[256,768]{1,0:T(8,128)(2,1)S(1)} %bitcast.17), channel_id=1, source_target_pairs={{0,1},{1,0},{2,3},{3,2},{4,5},{5,4},{6,7},{7,6},{8,9},{9,8},{10,11... | collective-permute-start | bytes 1179656 | tf_op jit(solution)/shard_map/ppermute | solution.py:28
  57.2 1.3 copy-start
  61.4 4.9 %copy-start.1 = (bf16[1024,768]{1,0:T(8,128)(2,1)S(1)}, bf16[1024,768]{1,0:T(8,128)(2,1)}, u32[]{:S(2)}) copy-start(bf16[1024,768]{1,0:T(8,128)(2,1)} %get-tuple-element.24.eqa_ref) | copy-start | bytes 4718596
  66.3 1.4 copy-start.2
  67.7 21.3 %copy-start.3 = (bf16[1024,768]{1,0:T(8,128)(2,1)S(1)}, bf16[1024,768]{1,0:T(8,128)(2,1)}, u32[]{:S(2)}) copy-start(bf16[1024,768]{1,0:T(8,128)(2,1)} %get-tuple-element.25.eqb_ref) | copy-start | bytes 4718596
  67.7 21.3 %copy-start.4 = (f32[1024,1]{1,0:T(8,128)S(1)}, f32[1024,1]{1,0:T(8,128)}, u32[]{:S(2)}) copy-start(f32[1024,1]{1,0:T(8,128)} %get-tuple-element.27.inva_ref) | copy-start | bytes 12292
  67.7 21.3 %copy-start.5 = (f32[1024,1]{1,0:T(8,128)S(1)}, f32[1024,1]{1,0:T(8,128)}, u32[]{:S(2)}) copy-start(f32[1024,1]{1,0:T(8,128)} %get-tuple-element.28.invb_ref) | copy-start | bytes 12292
  101.8 4.3 %collective-permute-start.6 = (bf16[384,768]{1,0:T(8,128)(2,1)S(1)}, bf16[384,768]{1,0:T(8,128)(2,1)S(1)}, u32[]{:S(2)}, u32[]{:S(2)}) collective-permute-start(bf16[384,768]{1,0:T(8,128)(2,1)S(1)} %get-tuple-element.32), channel_id=1, source_target_pairs={{0,32},{32,0},{1,33},{33,1},{2,34},{34,2},{3,35},{35,3},{4,36},{36... | collective-permute-start | bytes 1769480 | tf_op jit(solution)/shard_map/ppermute | solution.py:28
  107.0 15.2 %all-to-all-start.2 = ((bf16[16,24,768]{2,1,0:T(8,128)(2,1)}), bf16[16,24,768]{2,1,0:T(8,128)(2,1)S(1)}, u32[]{:S(2)}, u32[]{:S(2)}) async-start(bf16[16,24,768]{2,1,0:T(8,128)(2,1)} %bitcast.5), calls=%async_computation.2 | async-start | bytes 1179648 | tf_op jit(solution)/shard_map/all_to_all | solution.py:36
  110.6 8.3 %collective-permute-start.7 = (f32[8,128]{1,0:T(8,128)S(1)}, f32[8,128]{1,0:T(8,128)S(1)}, u32[]{:S(2)}, u32[]{:S(2)}) collective-permute-start(f32[8,128]{1,0:T(8,128)S(1)} %get-tuple-element.33), channel_id=1, source_target_pairs={{0,1},{1,0},{2,3},{3,2},{4,5},{5,4},{6,7},{7,6},{8,9},{9,8},{10,11... | collective-permute-start | bytes 12296 | tf_op jit(solution)/shard_map/ppermute | solution.py:28
  173.1 8.9 %collective-permute-start.8 = (bf16[384,768]{1,0:T(8,128)(2,1)S(1)}, bf16[384,768]{1,0:T(8,128)(2,1)S(1)}, u32[]{:S(2)}, u32[]{:S(2)}) collective-permute-start(bf16[384,768]{1,0:T(8,128)(2,1)S(1)} %bitcast.22), channel_id=1, source_target_pairs={{0,32},{32,0},{1,33},{33,1},{2,34},{34,2},{3,35},{35,3},{4,36},{36... | collective-permute-start | bytes 1769480 | tf_op jit(solution)/shard_map/ppermute | solution.py:28

commit v5 on v4

--- a/solution.py
+++ b/solution.py
@@ -269,7 +269,7 @@
     near = gather(xi_own, "z", 16).reshape(IB // 2, D)
     far = swap(near, "xl")
     two = jnp.concatenate([xq_own, swap(xq_own, "xh")])
-    xqa = join(two, turn(two, 1), turn(two, 3), turn(two, 2), near)
+    xqa = join(two, turn(two, 1), turn(two, 3), turn(two, 2), far)
     xqb = swap(xqa, "c")
 
     q = lax.iota(jnp.int32, 16)

time: 185 us -> 180 us (0.973)
  waiting for transfers between devices: 25.5 us -> 20.7 us
    ppermute x3, waiting for transfers between devices: 11.4 us -> 7.45 us  [turn(): return lax.ppermute(x, 'y', [(i, (i + k) % 4) for i in range(4)])]
    unnamed x17 -> x21, local copies, waits for them, and re-layouts: 3.65 us -> 4.41 us
  transfers between devices with their start and end apart: 11 -> 11, of which waited for: 9 -> 6; matrix products, arithmetic and copies ran while one was open for 2% -> 2% of each run, Pallas kernels for 4% -> 2%
where the time goes in v5:
time: 180 us; the launch traced here: 179 us
  blocking collectives  64.8 us (36%)
  starting transfers between devices  56.2 us (31%)
  Pallas kernels  24.9 us (14%)
  waiting for transfers between devices  20.7 us (12%)
  local copies, waits for them, and re-layouts  6.84 us (4%)
  other arithmetic  4.04 us (2%)
    all_to_all x4, blocking collectives, exchange(): return lax.all_to_all(x, axes, 0, 0, tiled=True)  64.8 us
    ppermute x6, starting transfers between devices, swap(): return lax.ppermute(x, axis, [(0, 1), (1, 0)])  26.7 us
    all_to_all x2, starting transfers between devices, exchange(): return lax.all_to_all(x, axes, 0, 0, tiled=True)  19.3 us
    pallas_call x1, Pallas kernels, grads(): pl.pallas_call(grad_kernel, grid=(QB // CG,), in_specs=[pl.BlockSpec(memo...  12.8 us
    ppermute x6, waiting for transfers between devices, swap(): return lax.ppermute(x, axis, [(0, 1), (1, 0)])  11.2 us
    ppermute x3, starting transfers between devices, turn(): return lax.ppermute(x, 'y', [(i, (i + k) % 4) for i in range(4)])  10.1 us
    ppermute x3, waiting for transfers between devices, turn(): return lax.ppermute(x, 'y', [(i, (i + k) % 4) for i in range(4)])  7.45 us
    pallas_call x2, Pallas kernels, tower(): pl.pallas_call(tower_kernel, grid=(HALF // CH,), in_specs=[pl.BlockSpec((...  7.03 us
  transfers between devices with their start and end apart: 11, of which 6 were waited for; matrix products, arithmetic and copies ran while one was open for 2% of the time, Pallas kernels for 2%

profile of v5, /device:TPU:1, one launch (start us, length us, event | category | flops | bytes accessed | tf_op | source)
XLA Modules:
  0.0 179.0 jit_solution(4139406078132740117)
XLA Ops:
  0.6 1.5 broadcast_in_dim.84
  2.1 15.7 %all-to-all-start = ((bf16[16,16,768]{2,1,0:T(8,128)(2,1)}), bf16[16,16,768]{2,1,0:T(8,128)(2,1)S(1)}, u32[]{:S(2)}, u32[]{:S(2)}) async-start(bf16[16,16,768]{2,1,0:T(8,128)(2,1)} %broadcast_in_dim.84), calls=%async_computation | async-start | bytes 786432 | tf_op jit(solution)/shard_map/all_to_all | solution.py:36
  17.9 4.7 %collective-permute-start = (bf16[128,768]{1,0:T(8,128)(2,1)}, bf16[128,768]{1,0:T(8,128)(2,1)S(1)}, u32[]{:S(2)}, u32[]{:S(2)}) collective-permute-start(bf16[128,768]{1,0:T(8,128)(2,1)} %param.7), channel_id=1, source_target_pairs={{0,64},{64,0},{1,65},{65,1},{2,66},{66,2},{3,67},{67,3},{4,68},{68... | collective-permute-start | bytes 589832 | tf_op jit(solution)/shard_map/ppermute | solution.py:28
  22.6 1.0 constant_dynamic-update-slice_fusion.1
  23.5 3.4 %collective-permute-done = bf16[128,768]{1,0:T(8,128)(2,1)S(1)} collective-permute-done((bf16[128,768]{1,0:T(8,128)(2,1)}, bf16[128,768]{1,0:T(8,128)(2,1)S(1)}, u32[]{:S(2)}, u32[]{:S(2)}) %collective-permute-start) | collective-permute-done | bytes 196640 | tf_op jit(solution)/shard_map/ppermute | solution.py:28
  27.0 3.2 %collective-permute-start.1 = (bf16[256,768]{1,0:T(8,128)(2,1)S(1)}, bf16[256,768]{1,0:T(8,128)(2,1)S(1)}, u32[]{:S(2)}, u32[]{:S(2)}) collective-permute-start(bf16[256,768]{1,0:T(8,128)(2,1)S(1)} %constant_dynamic-update-slice_fusion.two_ref), channel_id=1, source_target_pairs={{0,128},{128,256},{256,384},{384,0},{1,129},{129,257},{257,385},{3... | collective-permute-start | bytes 1179656 | tf_op jit(solution)/shard_map/ppermute | solution.py:32
  30.2 3.4 %collective-permute-start.2 = (bf16[256,768]{1,0:T(8,128)(2,1)S(1)}, bf16[256,768]{1,0:T(8,128)(2,1)S(1)}, u32[]{:S(2)}, u32[]{:S(2)}) collective-permute-start(bf16[256,768]{1,0:T(8,128)(2,1)S(1)} %constant_dynamic-update-slice_fusion.two_ref), channel_id=1, source_target_pairs={{0,384},{128,0},{256,128},{384,256},{1,385},{129,1},{257,129},{385... | collective-permute-start | bytes 1179656 | tf_op jit(solution)/shard_map/ppermute | solution.py:32
  33.5 3.5 %collective-permute-start.3 = (bf16[256,768]{1,0:T(8,128)(2,1)S(1)}, bf16[256,768]{1,0:T(8,128)(2,1)S(1)}, u32[]{:S(2)}, u32[]{:S(2)}) collective-permute-start(bf16[256,768]{1,0:T(8,128)(2,1)S(1)} %constant_dynamic-update-slice_fusion.two_ref), channel_id=1, source_target_pairs={{0,256},{128,384},{256,0},{384,128},{1,257},{129,385},{257,1},{385... | collective-permute-start | bytes 1179656 | tf_op jit(solution)/shard_map/ppermute | solution.py:32
  37.1 0.0 all-to-all-done
  37.1 0.0 copy-start.9
  37.1 0.0 copy-start.8
  37.1 3.1 %collective-permute-start.4 = (bf16[256,768]{1,0:T(8,128)(2,1)S(1)}, bf16[256,768]{1,0:T(8,128)(2,1)S(1)}, u32[]{:S(2)}, u32[]{:S(2)}) collective-permute-start(bf16[256,768]{1,0:T(8,128)(2,1)S(1)} %bitcast.16), channel_id=1, source_target_pairs={{0,1},{1,0},{2,3},{3,2},{4,5},{5,4},{6,7},{7,6},{8,9},{9,8},{10,11... | collective-permute-start | bytes 1179656 | tf_op jit(solution)/shard_map/ppermute | solution.py:28
  40.3 0.0 copy-start
  40.3 0.8 copy-done
  41.0 0.0 collective-permute-done.1.a_ref
  41.0 0.0 collective-permute-done.2.b_ref
  41.0 7.4 %collective-permute-done.3.c_ref = bf16[256,768]{1,0:T(8,128)(2,1)S(1)} collective-permute-done((bf16[256,768]{1,0:T(8,128)(2,1)S(1)}, bf16[256,768]{1,0:T(8,128)(2,1)S(1)}, u32[]{:S(2)}, u32[]{:S(2)}) %collective-permute-start.3) | collective-permute-done | bytes 393248 | tf_op jit(solution)/shard_map/ppermute | solution.py:32
  48.5 0.0 collective-permute-done.4.after_ref.far_ref
  48.5 0.1 join.1.x_ref.xqa_ref
  48.6 5.8 %collective-permute-start.5 = (bf16[1024,768]{1,0:T(8,128)(2,1)S(1)}, bf16[1024,768]{1,0:T(8,128)(2,1)}, u32[]{:S(2)}, u32[]{:S(2)}) collective-permute-start(bf16[1024,768]{1,0:T(8,128)(2,1)S(1)} %join.1.x_ref.xqa_ref), channel_id=1, source_target_pairs={{0,32},{32,0},{1,33},{33,1},{2,34},{34,2},{3,35},{35,3},{4,36},{36... | collective-permute-start | bytes 4718600 | tf_op jit(solution)/shard_map/ppermute | solution.py:28
  54.5 0.0 copy-done.9
  54.5 0.2 select_reduce_fusion
  54.7 0.2 copy.12.logc_ref
  54.9 0.1 iota_compare_fusion.1
  55.0 0.0 copy-done.8
  55.0 0.1 select_reduce_fusion.1
  55.1 0.1 fusion.11.ids_ref
  55.2 0.0 copy-start.2
  55.2 1.3 copy-done.2
  56.5 2.9 %tower.2 = (bf16[1024,768]{1,0:T(8,128)(2,1)}, f32[1024,1]{1,0:T(8,128)}) custom-call(bf16[1024,768]{1,0:T(8,128)(2,1)S(1)} %join.1.x_ref.xqa_ref, bf16[768,768]{1,0:T(8,128)(2,1)S(1)} %copy-done.2), custom_call_target="tpu_custom_call" | custom-call | flops 1207959552 | bytes 3145728 | tf_op jit(solution)/shard_map/tower/pallas_call | solution.py:100
  59.4 0.0 copy-start.1
  59.4 0.0 copy-start.3
  59.4 0.0 collective-permute-done.5.x_ref.xqb_ref
  59.4 4.2 %tower.3 = (bf16[1024,768]{1,0:T(8,128)(2,1)}, f32[1024,1]{1,0:T(8,128)}) custom-call(bf16[1024,768]{1,0:T(8,128)(2,1)} %collective-permute-done.5.x_ref.xqb_ref, bf16[768,768]{1,0:T(8,128)(2,1)S(1)} %copy-done.2), custom_call_target="tpu_custom_call" | custom-call | flops 1207959552 | bytes 3145728 | tf_op jit(solution)/shard_map/tower/pallas_call | solution.py:100
  63.5 0.0 copy-done.1
  63.5 0.0 copy-done.3
  63.6 0.0 copy-start.4
  63.6 1.4 copy-done.4
  65.0 5.0 %score.1 = (bf16[512,768]{1,0:T(8,128)(2,1)S(1)}, f32[512,1]{1,0:T(8,128)S(1)}, f32[24,128]{1,0:T(8,128)S(1)}) custom-call(s32[16]{0:T(128)S(1)} %fusion.33.order_ref, bf16[1024,768]{1,0:T(8,128)(2,1)S(1)} %copy-done.3, bf16[1024,768]{1,0:T(8,128)(2,1)S(1)} %copy-done.4, bf16[768,768]{1,0:T(8,128)(2,1)S(1)} %copy-done.2, bf16[256,768]{1,0:T(8,128)(2,1)S(1)} %bitcast.17, ...), custom_call_target="tpu_custom_call" | custom-call | flops 2214592512 | bytes 6291456 | tf_op jit(solution)/shard_map/score/pallas_call | solution.py:143
  70.0 15.0 %all_to_all.30.parts_ref = f32[16,24,128]{2,1,0:T(8,128)S(1)} all-to-all(f32[16,24,128]{2,1,0:T(8,128)S(1)} %broadcast_in_dim.92), channel_id=1, replica_groups=mesh['y'=4,'xh'=2,'c'=2,'z'=16,'xl'=2] {'y','xh','c'}, dimensions={0} | all-to-all | bytes 393216 | tf_op jit(solution)/shard_map/all_to_all | solution.py:36
  85.0 0.0 copy-done.5
  85.0 0.0 copy-done.6
  85.0 0.0 copy-done.7
  85.0 12.8 %grads.1 = (bf16[384,768]{1,0:T(8,128)(2,1)S(1)}, bf16[384,768]{1,0:T(8,128)(2,1)S(1)}, f32[8,128]{1,0:T(8,128)S(1)}) custom-call(s32[1]{0:T(128)} %bitcast.core_ref, s32[16]{0:T(128)S(1)} %fusion.33.order_ref, f32[16,24,128]{2,1,0:T(8,128)S(1)} %all_to_all.30.parts_ref, bf16[1024,768]{1,0:T(8,128)(2,1)S(1)} %copy-done.3, bf16[1024,768]{1,0:T(8,128)(2,1)S(1)} %copy-done.5, ...), custom_call_target="tpu_custom_call" | custom-call | flops 7851737088 | bytes 9437184 | tf_op jit(solution)/shard_map/grads/pallas_call | solution.py:226
  97.8 2.7 %collective-permute-start.6 = (bf16[384,768]{1,0:T(8,128)(2,1)S(1)}, bf16[384,768]{1,0:T(8,128)(2,1)S(1)}, u32[]{:S(2)}, u32[]{:S(2)}) collective-permute-start(bf16[384,768]{1,0:T(8,128)(2,1)S(1)} %get-tuple-element.32), channel_id=1, source_target_pairs={{0,32},{32,0},{1,33},{33,1},{2,34},{34,2},{3,35},{35,3},{4,36},{36... | collective-permute-start | bytes 1769480 | tf_op jit(solution)/shard_map/ppermute | solution.py:28
  100.5 1.6 collective-permute-done.6
  102.1 0.9 add_convert_fusion
  103.1 3.6 %all-to-all-start.2 = ((bf16[16,24,768]{2,1,0:T(8,128)(2,1)}), bf16[16,24,768]{2,1,0:T(8,128)(2,1)S(1)}, u32[]{:S(2)}, u32[]{:S(2)}) async-start(bf16[16,24,768]{2,1,0:T(8,128)(2,1)} %bitcast.5), calls=%async_computation.2 | async-start | bytes 1179648 | tf_op jit(solution)/shard_map/all_to_all | solution.py:36
  106.7 3.1 %collective-permute-start.7 = (f32[8,128]{1,0:T(8,128)S(1)}, f32[8,128]{1,0:T(8,128)S(1)}, u32[]{:S(2)}, u32[]{:S(2)}) collective-permute-start(f32[8,128]{1,0:T(8,128)S(1)} %get-tuple-element.33), channel_id=1, source_target_pairs={{0,1},{1,0},{2,3},{3,2},{4,5},{5,4},{6,7},{7,6},{8,9},{9,8},{10,11... | collective-permute-start | bytes 12296 | tf_op jit(solution)/shard_map/ppermute | solution.py:28
  109.8 5.2 %collective-permute-done.7 = f32[8,128]{1,0:T(8,128)S(1)} collective-permute-done((f32[8,128]{1,0:T(8,128)S(1)}, f32[8,128]{1,0:T(8,128)S(1)}, u32[]{:S(2)}, u32[]{:S(2)}) %collective-permute-start.7) | collective-permute-done | bytes 4128 | tf_op jit(solution)/shard_map/ppermute | solution.py:28
  115.0 0.5 slice.25
  116.2 0.1 maximum_bitcast_fusion
  116.3 2.0 %all-to-all-done.2 = bf16[16,24,768]{2,1,0:T(8,128)(2,1)S(1)} async-done(((bf16[16,24,768]{2,1,0:T(8,128)(2,1)}), bf16[16,24,768]{2,1,0:T(8,128)(2,1)S(1)}, u32[]{:S(2)}, u32[]{:S(2)}) %all-to-all-start.2) | async-done | bytes 589856 | tf_op jit(solution)/shard_map/all_to_all | solution.py:36
  118.3 0.1 reduce_sum.50
  118.4 0.1 reshape.284
  118.5 21.9 %all_to_all.31 = bf16[16,16,128]{2,1,0:T(8,128)(2,1)S(1)} all-to-all(bf16[16,16,128]{2,1,0:T(8,128)(2,1)S(1)} %pad_maximum_fusion), channel_id=1, replica_groups=mesh['y'=4,'xh'=2,'c'=2,'z'=16,'xl'=2] {'z'}, dimensions={0} | all-to-all | bytes 131072 | tf_op jit(solution)/shard_map/all_to_all | solution.py:36
  140.5 14.4 %all_to_all.32 = bf16[16,16,128]{2,1,0:T(8,128)(2,1)S(1)} all-to-all(bf16[16,16,128]{2,1,0:T(8,128)(2,1)S(1)} %broadcast_in_dim.95), channel_id=1, replica_groups=mesh['y'=4,'xh'=2,'c'=2,'z'=16,'xl'=2] {'z'}, dimensions={0} | all-to-all | bytes 131072 | tf_op jit(solution)/shard_map/all_to_all | solution.py:36
  154.9 0.1 broadcast_in_dim.96
  155.0 13.5 %all_to_all.33 = bf16[16,24,768]{2,1,0:T(8,128)(2,1)S(1)} all-to-all(bf16[16,24,768]{2,1,0:T(8,128)(2,1)S(1)} %broadcast_in_dim.97), channel_id=1, replica_groups=mesh['y'=4,'xh'=2,'c'=2,'z'=16,'xl'=2] {'y','xh','xl'}, dimensions={0} | all-to-all | bytes 1179648 | tf_op jit(solution)/shard_map/all_to_all | solution.py:36
  168.5 7.3 %collective-permute-start.8 = (bf16[384,768]{1,0:T(8,128)(2,1)S(1)}, bf16[384,768]{1,0:T(8,128)(2,1)S(1)}, u32[]{:S(2)}, u32[]{:S(2)}) collective-permute-start(bf16[384,768]{1,0:T(8,128)(2,1)S(1)} %bitcast.21), channel_id=1, source_target_pairs={{0,32},{32,0},{1,33},{33,1},{2,34},{34,2},{3,35},{35,3},{4,36},{36... | collective-permute-start | bytes 1769480 | tf_op jit(solution)/shard_map/ppermute | solution.py:28
  175.7 0.6 slice_reduce_fusion
  176.3 1.0 collective-permute-done.8
  177.3 0.1 broadcast_select_fusion.1
  177.5 1.6 maximum_convert_fusion
  (16 shorter events, 0.2 us)
Async XLA Ops:
  2.1 35.0 %all-to-all-start = ((bf16[16,16,768]{2,1,0:T(8,128)(2,1)}), bf16[16,16,768]{2,1,0:T(8,128)(2,1)S(1)}, u32[]{:S(2)}, u32[]{:S(2)}) async-start(bf16[16,16,768]{2,1,0:T(8,128)(2,1)} %broadcast_in_dim.84), calls=%async_computation | async-start | bytes 786432 | tf_op jit(solution)/shard_map/all_to_all | solution.py:36
  17.9 9.1 %collective-permute-start = (bf16[128,768]{1,0:T(8,128)(2,1)}, bf16[128,768]{1,0:T(8,128)(2,1)S(1)}, u32[]{:S(2)}, u32[]{:S(2)}) collective-permute-start(bf16[128,768]{1,0:T(8,128)(2,1)} %param.7), channel_id=1, source_target_pairs={{0,64},{64,0},{1,65},{65,1},{2,66},{66,2},{3,67},{67,3},{4,68},{68... | collective-permute-start | bytes 589832 | tf_op jit(solution)/shard_map/ppermute | solution.py:28
  27.0 14.1 %collective-permute-start.1 = (bf16[256,768]{1,0:T(8,128)(2,1)S(1)}, bf16[256,768]{1,0:T(8,128)(2,1)S(1)}, u32[]{:S(2)}, u32[]{:S(2)}) collective-permute-start(bf16[256,768]{1,0:T(8,128)(2,1)S(1)} %constant_dynamic-update-slice_fusion.two_ref), channel_id=1, source_target_pairs={{0,128},{128,256},{256,384},{384,0},{1,129},{129,257},{257,385},{3... | collective-permute-start | bytes 1179656 | tf_op jit(solution)/shard_map/ppermute | solution.py:32
  30.2 10.9 %collective-permute-start.2 = (bf16[256,768]{1,0:T(8,128)(2,1)S(1)}, bf16[256,768]{1,0:T(8,128)(2,1)S(1)}, u32[]{:S(2)}, u32[]{:S(2)}) collective-permute-start(bf16[256,768]{1,0:T(8,128)(2,1)S(1)} %constant_dynamic-update-slice_fusion.two_ref), channel_id=1, source_target_pairs={{0,384},{128,0},{256,128},{384,256},{1,385},{129,1},{257,129},{385... | collective-permute-start | bytes 1179656 | tf_op jit(solution)/shard_map/ppermute | solution.py:32
  33.5 14.9 %collective-permute-start.3 = (bf16[256,768]{1,0:T(8,128)(2,1)S(1)}, bf16[256,768]{1,0:T(8,128)(2,1)S(1)}, u32[]{:S(2)}, u32[]{:S(2)}) collective-permute-start(bf16[256,768]{1,0:T(8,128)(2,1)S(1)} %constant_dynamic-update-slice_fusion.two_ref), channel_id=1, source_target_pairs={{0,256},{128,384},{256,0},{384,128},{1,257},{129,385},{257,1},{385... | collective-permute-start | bytes 1179656 | tf_op jit(solution)/shard_map/ppermute | solution.py:32
  37.1 17.4 %copy-start.9 = (s32[512]{0:T(512)S(1)}, s32[512]{0:T(512)}, u32[]{:S(2)}) copy-start(s32[512]{0:T(512)} %param.10) | copy-start | bytes 6148
  37.1 17.9 %copy-start.8 = (s32[2048]{0:T(1024)S(1)}, s32[2048]{0:T(1024)}, u32[]{:S(2)}) copy-start(s32[2048]{0:T(1024)} %param.11) | copy-start | bytes 24580
  37.1 11.4 %collective-permute-start.4 = (bf16[256,768]{1,0:T(8,128)(2,1)S(1)}, bf16[256,768]{1,0:T(8,128)(2,1)S(1)}, u32[]{:S(2)}, u32[]{:S(2)}) collective-permute-start(bf16[256,768]{1,0:T(8,128)(2,1)S(1)} %bitcast.16), channel_id=1, source_target_pairs={{0,1},{1,0},{2,3},{3,2},{4,5},{5,4},{6,7},{7,6},{8,9},{9,8},{10,11... | collective-permute-start | bytes 1179656 | tf_op jit(solution)/shard_map/ppermute | solution.py:28
  40.3 0.8 copy-start
  48.6 10.8 %collective-permute-start.5 = (bf16[1024,768]{1,0:T(8,128)(2,1)S(1)}, bf16[1024,768]{1,0:T(8,128)(2,1)}, u32[]{:S(2)}, u32[]{:S(2)}) collective-permute-start(bf16[1024,768]{1,0:T(8,128)(2,1)S(1)} %join.1.x_ref.xqa_ref), channel_id=1, source_target_pairs={{0,32},{32,0},{1,33},{33,1},{2,34},{34,2},{3,35},{35,3},{4,36},{36... | collective-permute-start | bytes 4718600 | tf_op jit(solution)/shard_map/ppermute | solution.py:28
  55.2 1.3 copy-start.2
  59.4 4.2 %copy-start.1 = (bf16[16,16,768]{2,1,0:T(8,128)(2,1)S(1)}, bf16[16,16,768]{2,1,0:T(8,128)(2,1)}, u32[]{:S(2)}) copy-start(bf16[16,16,768]{2,1,0:T(8,128)(2,1)} %copy-done) | copy-start | bytes 1179652
  59.4 4.2 %copy-start.3 = (bf16[1024,768]{1,0:T(8,128)(2,1)S(1)}, bf16[1024,768]{1,0:T(8,128)(2,1)}, u32[]{:S(2)}) copy-start(bf16[1024,768]{1,0:T(8,128)(2,1)} %get-tuple-element.24.eqa_ref) | copy-start | bytes 4718596
  63.6 1.4 copy-start.4
  65.0 20.1 %copy-start.5 = (bf16[1024,768]{1,0:T(8,128)(2,1)S(1)}, bf16[1024,768]{1,0:T(8,128)(2,1)}, u32[]{:S(2)}) copy-start(bf16[1024,768]{1,0:T(8,128)(2,1)} %get-tuple-element.25.eqb_ref) | copy-start | bytes 4718596
  65.0 20.1 %copy-start.6 = (f32[1024,1]{1,0:T(8,128)S(1)}, f32[1024,1]{1,0:T(8,128)}, u32[]{:S(2)}) copy-start(f32[1024,1]{1,0:T(8,128)} %get-tuple-element.27.inva_ref) | copy-start | bytes 12292
  65.0 20.1 %copy-start.7 = (f32[1024,1]{1,0:T(8,128)S(1)}, f32[1024,1]{1,0:T(8,128)}, u32[]{:S(2)}) copy-start(f32[1024,1]{1,0:T(8,128)} %get-tuple-element.28.invb_ref) | copy-start | bytes 12292
  97.8 4.3 %collective-permute-start.6 = (bf16[384,768]{1,0:T(8,128)(2,1)S(1)}, bf16[384,768]{1,0:T(8,128)(2,1)S(1)}, u32[]{:S(2)}, u32[]{:S(2)}) collective-permute-start(bf16[384,768]{1,0:T(8,128)(2,1)S(1)} %get-tuple-element.32), channel_id=1, source_target_pairs={{0,32},{32,0},{1,33},{33,1},{2,34},{34,2},{3,35},{35,3},{4,36},{36... | collective-permute-start | bytes 1769480 | tf_op jit(solution)/shard_map/ppermute | solution.py:28
  103.1 15.2 %all-to-all-start.2 = ((bf16[16,24,768]{2,1,0:T(8,128)(2,1)}), bf16[16,24,768]{2,1,0:T(8,128)(2,1)S(1)}, u32[]{:S(2)}, u32[]{:S(2)}) async-start(bf16[16,24,768]{2,1,0:T(8,128)(2,1)} %bitcast.5), calls=%async_computation.2 | async-start | bytes 1179648 | tf_op jit(solution)/shard_map/all_to_all | solution.py:36
  106.7 8.3 %collective-permute-start.7 = (f32[8,128]{1,0:T(8,128)S(1)}, f32[8,128]{1,0:T(8,128)S(1)}, u32[]{:S(2)}, u32[]{:S(2)}) collective-permute-start(f32[8,128]{1,0:T(8,128)S(1)} %get-tuple-element.33), channel_id=1, source_target_pairs={{0,1},{1,0},{2,3},{3,2},{4,5},{5,4},{6,7},{7,6},{8,9},{9,8},{10,11... | collective-permute-start | bytes 12296 | tf_op jit(solution)/shard_map/ppermute | solution.py:28
  168.5 8.9 %collective-permute-start.8 = (bf16[384,768]{1,0:T(8,128)(2,1)S(1)}, bf16[384,768]{1,0:T(8,128)(2,1)S(1)}, u32[]{:S(2)}, u32[]{:S(2)}) collective-permute-start(bf16[384,768]{1,0:T(8,128)(2,1)S(1)} %bitcast.21), channel_id=1, source_target_pairs={{0,32},{32,0},{1,33},{33,1},{2,34},{34,2},{3,35},{35,3},{4,36},{36... | collective-permute-start | bytes 1769480 | tf_op jit(solution)/shard_map/ppermute | solution.py:28

commit v6 on v5

--- a/solution.py
+++ b/solution.py
@@ -92,80 +92,74 @@
     )(two, a, b, c, after)
 
 
-def tower_kernel(x_ref, w_ref, e_ref, inv_ref):
-    e_ref[...], inv_ref[...] = unit_rows(x_ref[...], w_ref[...])
-
-
-def tower(x, weight):
-    return pl.pallas_call(
-        tower_kernel,
-        grid=(HALF // CH,),
-        in_specs=[pl.BlockSpec((CH, D), lambda i: (i, 0)), whole(D, D)],
-        out_specs=[pl.BlockSpec((CH, D), lambda i: (i, 0)), pl.BlockSpec((CH, 1), lambda i: (i, 0))],
-        out_shape=[pltpu.HBM((HALF, D), BF), pltpu.HBM((HALF, 1), F32)],
-        compiler_params=pltpu.CompilerParams(vmem_limit_bytes=16 << 20),
-        cost_estimate=pl.CostEstimate(flops=2 * HALF * D * D, bytes_accessed=4 * HALF * D, transcendentals=HALF),
-        name="tower",
-    )(x, weight)
-
-
-def score_kernel(order_ref, eqa_ref, eqb_ref, w_ref, near_ref, far_ref, logc_ref, ids_ref, tgt_ref,
-                 ei_ref, invi_ref, stat_ref):
-    i = pl.program_id(0)
-
-    @pl.when(i == 0)
+def score_step(base, order_ref, x_ref, w_ref, ei_ref, logc_ref, ids_ref, tgt_ref, eq_ref, inv_ref, stat_ref):
+    eq, inv_ref[...] = unit_rows(x_ref[...], w_ref[...])
+    eq_ref[...] = eq
+    scores = score_tile(ei_ref, eq, logc_ref)
+    top = jnp.max(scores, axis=0, keepdims=True)
+    lse = top + jnp.log(jnp.sum(jnp.exp(scores - top), axis=0, keepdims=True))
+    pos = jnp.sum(jnp.where(ids_ref[...] == tgt_ref[...], scores, 0.0), axis=0, keepdims=True)
+    for k in range(CH // 128):
+        row = order_ref[base + pl.program_id(0) * (CH // 128) + k]
+        part = slice(k * 128, (k + 1) * 128)
+        stat_ref[pl.ds(row, 1), :] = lse[:, part]
+        stat_ref[16:17, :] = stat_ref[16:17, :] + pos[:, part]
+
+
+def first_kernel(order_ref, x_ref, w_ref, near_ref, far_ref, logc_ref, ids_ref, tgt_ref,
+                 eq_ref, inv_ref, ei_ref, invi_ref, stat_ref):
+    @pl.when(pl.program_id(0) == 0)
     def _():
         for k, ref in enumerate((near_ref, far_ref)):
             part = slice(k * (IB // 2), (k + 1) * (IB // 2))
             ei_ref[part, :], invi_ref[part, :] = unit_rows(ref[...], w_ref[...])
         stat_ref[...] = jnp.zeros_like(stat_ref)
 
-    def run(eq):
-        scores = score_tile(ei_ref, eq, logc_ref)
-        top = jnp.max(scores, axis=0, keepdims=True)
-        lse = top + jnp.log(jnp.sum(jnp.exp(scores - top), axis=0, keepdims=True))
-        pos = jnp.sum(jnp.where(ids_ref[...] == tgt_ref[...], scores, 0.0), axis=0, keepdims=True)
-        for k in range(CH // 128):
-            part = slice(k * 128, (k + 1) * 128)
-            stat_ref[pl.ds(order_ref[i * (CH // 128) + k], 1), :] = lse[:, part]
-            stat_ref[16:17, :] = stat_ref[16:17, :] + pos[:, part]
-
-    @pl.when(i < HALF // CH)
-    def _():
-        run(eqa_ref[...])
-
-    @pl.when(i >= HALF // CH)
-    def _():
-        run(eqb_ref[...])
-
-
-def score(order, eqa, eqb, weight, near, far, logc, ids, targets):
+    score_step(0, order_ref, x_ref, w_ref, ei_ref, logc_ref, ids_ref, tgt_ref, eq_ref, inv_ref, stat_ref)
+
+
+def second_kernel(order_ref, x_ref, w_ref, ei_ref, logc_ref, ids_ref, tgt_ref, before_ref,
+                  eq_ref, inv_ref, stat_ref):
+    @pl.when(pl.program_id(0) == 0)
+    def _():
+        stat_ref[...] = before_ref[...]
+
+    score_step(8, order_ref, x_ref, w_ref, ei_ref, logc_ref, ids_ref, tgt_ref, eq_ref, inv_ref, stat_ref)
+
+
+def score_call(kernel, base, items, item_specs, item_shapes, order, x, weight, side, targets, tail, name):
+    steps = HALF // CH
     return pl.pallas_call(
-        score_kernel,
-        grid=(QB // CH,),
+        kernel,
+        grid=(steps,),
         in_specs=[
             pl.BlockSpec(memory_space=pltpu.SMEM),
-            first(CH, D),
-            second(CH, D),
+            pl.BlockSpec((CH, D), lambda i: (i, 0)),
             whole(D, D),
-            whole(IB // 2, D),
-            whole(IB // 2, D),
-            whole(IB, 1),
-            whole(IB, 1),
-            pl.BlockSpec((1, CH), lambda i: (0, i)),
-        ],
-        out_specs=[whole(IB, D), whole(IB, 1), whole(24, 128)],
+            *[whole(*x.shape) for x in items],
+            whole(IB, 1),
+            whole(IB, 1),
+            pl.BlockSpec((1, CH), lambda i: (0, i + base * steps)),
+        ]
+        + [whole(24, 128)] * len(tail),
+        out_specs=[
+            pl.BlockSpec((CH, D), lambda i: (i, 0)),
+            pl.BlockSpec((CH, 1), lambda i: (i, 0)),
+            *item_specs,
+            whole(24, 128),
+        ],
         out_shape=[
-            jax.ShapeDtypeStruct((IB, D), BF),
-            jax.ShapeDtypeStruct((IB, 1), F32),
+            jax.ShapeDtypeStruct((HALF, D), BF),
+            jax.ShapeDtypeStruct((HALF, 1), F32),
+            *item_shapes,
             jax.ShapeDtypeStruct((24, 128), F32),
         ],
         compiler_params=pltpu.CompilerParams(vmem_limit_bytes=24 << 20),
         cost_estimate=pl.CostEstimate(
-            flops=2 * IB * D * (D + QB), bytes_accessed=6 << 20, transcendentals=IB * QB
+            flops=2 * HALF * D * (D + IB), bytes_accessed=6 << 20, transcendentals=IB * HALF
         ),
-        name="score",
-    )(order, eqa, eqb, weight, near, far, logc, ids, targets)
+        name=name,
+    )(order, x, weight, *items, *side, targets, *tail)
 
 
 def grad_kernel(core_ref, order_ref, parts_ref, eqa_ref, eqb_ref, inva_ref, invb_ref, xqa_ref, xqb_ref,
@@ -285,9 +279,17 @@
     logc = jnp.sum(jnp.where(ids[:, None] == at[None, :], logs[None, :], 0.0), axis=1, keepdims=True)
     ids = (block * IB + ids)[:, None]
 
-    eqa, inva = tower(xqa, weight)
-    eqb, invb = tower(xqb, weight)
-    ei, invi, stat = score(order, eqa, eqb, weight, near, far, logc, ids, targets)
+    eqa, inva, ei, invi, stat = score_call(
+        first_kernel,
+        0,
+        (near, far),
+        [whole(IB, D), whole(IB, 1)],
+        [jax.ShapeDtypeStruct((IB, D), BF), jax.ShapeDtypeStruct((IB, 1), F32)],
+        order, xqa, weight, (logc, ids), targets, (), "score_first",
+    )
+    eqb, invb, stat = score_call(
+        second_kernel, 1, (ei,), [], [], order, xqb, weight, (logc, ids), targets, (stat,), "score_second"
+    )
     parts = gather(stat, POOL, 16)
     send, keep, loss = grads(
         core.reshape(1), order, parts, eqa, eqb, inva, invb, xqa, xqb, ei, invi, near, far, logc, ids, targets

time: 180 us -> 177 us (0.983)
  Pallas kernels: 24.9 us -> 22.6 us
    pallas_call x3 -> x2, Pallas kernels: 12 us -> 9.69 us  [score_call(): pl.pallas_call(kernel, grid=(steps,), in_specs=[pl.BlockSpec(memory_space...]
    unnamed x21 -> x13, local copies, waits for them, and re-layouts: 4.41 us -> 3.97 us
  transfers between devices with their start and end apart: 11 -> 11, of which waited for: 6 -> 6; matrix products, arithmetic and copies ran while one was open for 2% -> 2% of each run, Pallas kernels for 2% -> 3%
where the time goes in v6:
time: 177 us; the launch traced here: 176 us
  blocking collectives  64.8 us (37%)
  starting transfers between devices  56.2 us (32%)
  Pallas kernels  22.6 us (13%)
  waiting for transfers between devices  20.7 us (12%)
  local copies, waits for them, and re-layouts  6.42 us (4%)
  other arithmetic  4.04 us (2%)
    all_to_all x4, blocking collectives, exchange(): return lax.all_to_all(x, axes, 0, 0, tiled=True)  64.8 us
    ppermute x6, starting transfers between devices, swap(): return lax.ppermute(x, axis, [(0, 1), (1, 0)])  26.7 us
    all_to_all x2, starting transfers between devices, exchange(): return lax.all_to_all(x, axes, 0, 0, tiled=True)  19.3 us
    pallas_call x1, Pallas kernels, grads(): pl.pallas_call(grad_kernel, grid=(QB // CG,), in_specs=[pl.BlockSpec(memo...  12.8 us
    ppermute x6, waiting for transfers between devices, swap(): return lax.ppermute(x, axis, [(0, 1), (1, 0)])  11.2 us
    ppermute x3, starting transfers between devices, turn(): return lax.ppermute(x, 'y', [(i, (i + k) % 4) for i in range(4)])  10.1 us
    pallas_call x2, Pallas kernels, score_call(): pl.pallas_call(kernel, grid=(steps,), in_specs=[pl.BlockSpec(memory_space...  9.69 us
    ppermute x3, waiting for transfers between devices, turn(): return lax.ppermute(x, 'y', [(i, (i + k) % 4) for i in range(4)])  7.47 us
  transfers between devices with their start and end apart: 11, of which 6 were waited for; matrix products, arithmetic and copies ran while one was open for 2% of the time, Pallas kernels for 3%

profile of v6, /device:TPU:1, one launch (start us, length us, event | category | flops | bytes accessed | tf_op | source)
XLA Modules:
  0.0 176.4 jit_solution(14335766456317277178)
XLA Ops:
  0.6 1.5 broadcast_in_dim.84
  2.1 15.7 %all-to-all-start = ((bf16[16,16,768]{2,1,0:T(8,128)(2,1)}), bf16[16,16,768]{2,1,0:T(8,128)(2,1)S(1)}, u32[]{:S(2)}, u32[]{:S(2)}) async-start(bf16[16,16,768]{2,1,0:T(8,128)(2,1)} %broadcast_in_dim.84), calls=%async_computation | async-start | bytes 786432 | tf_op jit(solution)/shard_map/all_to_all | solution.py:36
  17.9 4.7 %collective-permute-start = (bf16[128,768]{1,0:T(8,128)(2,1)}, bf16[128,768]{1,0:T(8,128)(2,1)S(1)}, u32[]{:S(2)}, u32[]{:S(2)}) collective-permute-start(bf16[128,768]{1,0:T(8,128)(2,1)} %param.7), channel_id=1, source_target_pairs={{0,64},{64,0},{1,65},{65,1},{2,66},{66,2},{3,67},{67,3},{4,68},{68... | collective-permute-start | bytes 589832 | tf_op jit(solution)/shard_map/ppermute | solution.py:28
  22.6 1.0 constant_dynamic-update-slice_fusion.1
  23.5 3.4 %collective-permute-done = bf16[128,768]{1,0:T(8,128)(2,1)S(1)} collective-permute-done((bf16[128,768]{1,0:T(8,128)(2,1)}, bf16[128,768]{1,0:T(8,128)(2,1)S(1)}, u32[]{:S(2)}, u32[]{:S(2)}) %collective-permute-start) | collective-permute-done | bytes 196640 | tf_op jit(solution)/shard_map/ppermute | solution.py:28
  27.0 3.2 %collective-permute-start.1 = (bf16[256,768]{1,0:T(8,128)(2,1)S(1)}, bf16[256,768]{1,0:T(8,128)(2,1)S(1)}, u32[]{:S(2)}, u32[]{:S(2)}) collective-permute-start(bf16[256,768]{1,0:T(8,128)(2,1)S(1)} %constant_dynamic-update-slice_fusion.two_ref), channel_id=1, source_target_pairs={{0,128},{128,256},{256,384},{384,0},{1,129},{129,257},{257,385},{3... | collective-permute-start | bytes 1179656 | tf_op jit(solution)/shard_map/ppermute | solution.py:32
  30.2 3.4 %collective-permute-start.2 = (bf16[256,768]{1,0:T(8,128)(2,1)S(1)}, bf16[256,768]{1,0:T(8,128)(2,1)S(1)}, u32[]{:S(2)}, u32[]{:S(2)}) collective-permute-start(bf16[256,768]{1,0:T(8,128)(2,1)S(1)} %constant_dynamic-update-slice_fusion.two_ref), channel_id=1, source_target_pairs={{0,384},{128,0},{256,128},{384,256},{1,385},{129,1},{257,129},{385... | collective-permute-start | bytes 1179656 | tf_op jit(solution)/shard_map/ppermute | solution.py:32
  33.5 3.5 %collective-permute-start.3 = (bf16[256,768]{1,0:T(8,128)(2,1)S(1)}, bf16[256,768]{1,0:T(8,128)(2,1)S(1)}, u32[]{:S(2)}, u32[]{:S(2)}) collective-permute-start(bf16[256,768]{1,0:T(8,128)(2,1)S(1)} %constant_dynamic-update-slice_fusion.two_ref), channel_id=1, source_target_pairs={{0,256},{128,384},{256,0},{384,128},{1,257},{129,385},{257,1},{385... | collective-permute-start | bytes 1179656 | tf_op jit(solution)/shard_map/ppermute | solution.py:32
  37.1 0.0 all-to-all-done
  37.1 0.0 copy-start.5
  37.1 0.0 copy-start.4
  37.1 3.1 %collective-permute-start.4 = (bf16[256,768]{1,0:T(8,128)(2,1)S(1)}, bf16[256,768]{1,0:T(8,128)(2,1)S(1)}, u32[]{:S(2)}, u32[]{:S(2)}) collective-permute-start(bf16[256,768]{1,0:T(8,128)(2,1)S(1)} %bitcast.16), channel_id=1, source_target_pairs={{0,1},{1,0},{2,3},{3,2},{4,5},{5,4},{6,7},{7,6},{8,9},{9,8},{10,11... | collective-permute-start | bytes 1179656 | tf_op jit(solution)/shard_map/ppermute | solution.py:28
  40.3 0.0 copy-start
  40.3 0.7 copy-done
  41.0 0.0 collective-permute-done.1.a_ref
  41.0 0.0 collective-permute-done.2.b_ref
  41.0 7.5 %collective-permute-done.3.c_ref = bf16[256,768]{1,0:T(8,128)(2,1)S(1)} collective-permute-done((bf16[256,768]{1,0:T(8,128)(2,1)S(1)}, bf16[256,768]{1,0:T(8,128)(2,1)S(1)}, u32[]{:S(2)}, u32[]{:S(2)}) %collective-permute-start.3) | collective-permute-done | bytes 393248 | tf_op jit(solution)/shard_map/ppermute | solution.py:32
  48.5 0.0 collective-permute-done.4.after_ref.far_ref
  48.5 0.1 join.1.x_ref.xqa_ref
  48.6 5.8 %collective-permute-start.5 = (bf16[1024,768]{1,0:T(8,128)(2,1)S(1)}, bf16[1024,768]{1,0:T(8,128)(2,1)}, u32[]{:S(2)}, u32[]{:S(2)}) collective-permute-start(bf16[1024,768]{1,0:T(8,128)(2,1)S(1)} %join.1.x_ref.xqa_ref), channel_id=1, source_target_pairs={{0,32},{32,0},{1,33},{33,1},{2,34},{34,2},{3,35},{35,3},{4,36},{36... | collective-permute-start | bytes 4718600 | tf_op jit(solution)/shard_map/ppermute | solution.py:28
  54.5 0.0 copy-done.5
  54.5 0.2 select_reduce_fusion
  54.7 0.2 copy.10.logc_ref
  54.9 0.1 iota_compare_fusion.1
  55.0 0.0 copy-done.4
  55.0 0.1 select_reduce_fusion.1
  55.1 0.1 fusion.11.ids_ref
  55.2 0.0 copy-start.1
  55.2 1.0 copy-done.1
  56.2 0.0 copy-start.3
  56.2 1.3 copy-done.3
  57.5 5.0 %score_first.1 = (bf16[1024,768]{1,0:T(8,128)(2,1)S(1)}, f32[1024,1]{1,0:T(8,128)S(1)}, bf16[512,768]{1,0:T(8,128)(2,1)S(1)}, f32[512,1]{1,0:T(8,128)S(1)}, f32[24,128]{1,0:T(8,128)S(1)}) custom-call(s32[16]{0:T(128)S(1)} %fusion.33.order_ref, bf16[1024,768]{1,0:T(8,128)(2,1)S(1)} %join.1.x_ref.xqa_ref, bf16[768,768]{1,0:T(8,128)(2,1)S(1)} %copy-done.3, ...), custom_call_target="tpu_custom_call" | custom-call | flops 2013265920 | bytes 6291456 | tf_op jit(solution)/shard_map/score_first/pallas_call | solution.py:132
  62.5 0.0 collective-permute-done.5.x_ref.xqb_ref
  62.5 0.0 copy-start.2
  62.5 4.7 %score_second.1 = (bf16[1024,768]{1,0:T(8,128)(2,1)S(1)}, f32[1024,1]{1,0:T(8,128)S(1)}, f32[24,128]{1,0:T(8,128)S(1)}) custom-call(s32[16]{0:T(128)S(1)} %fusion.33.order_ref, bf16[1024,768]{1,0:T(8,128)(2,1)} %collective-permute-done.5.x_ref.xqb_ref, bf16[768,768]{1,0:T(8,128)(2,1)S(1)} %copy-done.3, bf16[512,768]{1,0:T(8,128)(2,1)S(1)} %get-tuple-element.25.ei_ref, ...), custom_call_target="tpu_custom_call" | custom-call | flops 2013265920 | bytes 6291456 | tf_op jit(solution)/shard_map/score_second/pallas_call | solution.py:132
  67.3 15.0 %all_to_all.30.parts_ref = f32[16,24,128]{2,1,0:T(8,128)S(1)} all-to-all(f32[16,24,128]{2,1,0:T(8,128)S(1)} %broadcast_in_dim.92), channel_id=1, replica_groups=mesh['y'=4,'xh'=2,'c'=2,'z'=16,'xl'=2] {'y','xh','c'}, dimensions={0} | all-to-all | bytes 393216 | tf_op jit(solution)/shard_map/all_to_all | solution.py:36
  82.3 0.0 copy-done.2
  82.3 12.8 %grads.1 = (bf16[384,768]{1,0:T(8,128)(2,1)S(1)}, bf16[384,768]{1,0:T(8,128)(2,1)S(1)}, f32[8,128]{1,0:T(8,128)S(1)}) custom-call(s32[1]{0:T(128)} %bitcast.core_ref, s32[16]{0:T(128)S(1)} %fusion.33.order_ref, f32[16,24,128]{2,1,0:T(8,128)S(1)} %all_to_all.30.parts_ref, bf16[1024,768]{1,0:T(8,128)(2,1)S(1)} %get-tuple-element.28.eqa_ref, ...), custom_call_target="tpu_custom_call" | custom-call | flops 7851737088 | bytes 9437184 | tf_op jit(solution)/shard_map/grads/pallas_call | solution.py:220
  95.1 2.7 %collective-permute-start.6 = (bf16[384,768]{1,0:T(8,128)(2,1)S(1)}, bf16[384,768]{1,0:T(8,128)(2,1)S(1)}, u32[]{:S(2)}, u32[]{:S(2)}) collective-permute-start(bf16[384,768]{1,0:T(8,128)(2,1)S(1)} %get-tuple-element.34), channel_id=1, source_target_pairs={{0,32},{32,0},{1,33},{33,1},{2,34},{34,2},{3,35},{35,3},{4,36},{36... | collective-permute-start | bytes 1769480 | tf_op jit(solution)/shard_map/ppermute | solution.py:28
  97.8 1.6 collective-permute-done.6
  99.4 0.9 add_convert_fusion
  100.4 3.6 %all-to-all-start.2 = ((bf16[16,24,768]{2,1,0:T(8,128)(2,1)}), bf16[16,24,768]{2,1,0:T(8,128)(2,1)S(1)}, u32[]{:S(2)}, u32[]{:S(2)}) async-start(bf16[16,24,768]{2,1,0:T(8,128)(2,1)} %bitcast.5), calls=%async_computation.2 | async-start | bytes 1179648 | tf_op jit(solution)/shard_map/all_to_all | solution.py:36
  104.0 3.1 %collective-permute-start.7 = (f32[8,128]{1,0:T(8,128)S(1)}, f32[8,128]{1,0:T(8,128)S(1)}, u32[]{:S(2)}, u32[]{:S(2)}) collective-permute-start(f32[8,128]{1,0:T(8,128)S(1)} %get-tuple-element.35), channel_id=1, source_target_pairs={{0,1},{1,0},{2,3},{3,2},{4,5},{5,4},{6,7},{7,6},{8,9},{9,8},{10,11... | collective-permute-start | bytes 12296 | tf_op jit(solution)/shard_map/ppermute | solution.py:28
  107.1 5.2 %collective-permute-done.7 = f32[8,128]{1,0:T(8,128)S(1)} collective-permute-done((f32[8,128]{1,0:T(8,128)S(1)}, f32[8,128]{1,0:T(8,128)S(1)}, u32[]{:S(2)}, u32[]{:S(2)}) %collective-permute-start.7) | collective-permute-done | bytes 4128 | tf_op jit(solution)/shard_map/ppermute | solution.py:28
  112.3 0.6 slice.25
  113.6 0.1 maximum_bitcast_fusion
  113.6 2.0 %all-to-all-done.2 = bf16[16,24,768]{2,1,0:T(8,128)(2,1)S(1)} async-done(((bf16[16,24,768]{2,1,0:T(8,128)(2,1)}), bf16[16,24,768]{2,1,0:T(8,128)(2,1)S(1)}, u32[]{:S(2)}, u32[]{:S(2)}) %all-to-all-start.2) | async-done | bytes 589856 | tf_op jit(solution)/shard_map/all_to_all | solution.py:36
  115.6 0.1 reduce_sum.50
  115.7 0.1 reshape.284
  115.9 21.9 %all_to_all.31 = bf16[16,16,128]{2,1,0:T(8,128)(2,1)S(1)} all-to-all(bf16[16,16,128]{2,1,0:T(8,128)(2,1)S(1)} %pad_maximum_fusion), channel_id=1, replica_groups=mesh['y'=4,'xh'=2,'c'=2,'z'=16,'xl'=2] {'z'}, dimensions={0} | all-to-all | bytes 131072 | tf_op jit(solution)/shard_map/all_to_all | solution.py:36
  137.8 14.4 %all_to_all.32 = bf16[16,16,128]{2,1,0:T(8,128)(2,1)S(1)} all-to-all(bf16[16,16,128]{2,1,0:T(8,128)(2,1)S(1)} %broadcast_in_dim.95), channel_id=1, replica_groups=mesh['y'=4,'xh'=2,'c'=2,'z'=16,'xl'=2] {'z'}, dimensions={0} | all-to-all | bytes 131072 | tf_op jit(solution)/shard_map/all_to_all | solution.py:36
  152.2 0.1 broadcast_in_dim.96
  152.3 13.5 %all_to_all.33 = bf16[16,24,768]{2,1,0:T(8,128)(2,1)S(1)} all-to-all(bf16[16,24,768]{2,1,0:T(8,128)(2,1)S(1)} %broadcast_in_dim.97), channel_id=1, replica_groups=mesh['y'=4,'xh'=2,'c'=2,'z'=16,'xl'=2] {'y','xh','xl'}, dimensions={0} | all-to-all | bytes 1179648 | tf_op jit(solution)/shard_map/all_to_all | solution.py:36
  165.8 7.3 %collective-permute-start.8 = (bf16[384,768]{1,0:T(8,128)(2,1)S(1)}, bf16[384,768]{1,0:T(8,128)(2,1)S(1)}, u32[]{:S(2)}, u32[]{:S(2)}) collective-permute-start(bf16[384,768]{1,0:T(8,128)(2,1)S(1)} %bitcast.22), channel_id=1, source_target_pairs={{0,32},{32,0},{1,33},{33,1},{2,34},{34,2},{3,35},{35,3},{4,36},{36... | collective-permute-start | bytes 1769480 | tf_op jit(solution)/shard_map/ppermute | solution.py:28
  173.1 0.6 slice_reduce_fusion
  173.7 1.0 collective-permute-done.8
  174.7 0.1 broadcast_select_fusion.1
  174.8 1.6 maximum_convert_fusion
  (13 shorter events, 0.2 us)
Async XLA Ops:
  2.1 35.0 %all-to-all-start = ((bf16[16,16,768]{2,1,0:T(8,128)(2,1)}), bf16[16,16,768]{2,1,0:T(8,128)(2,1)S(1)}, u32[]{:S(2)}, u32[]{:S(2)}) async-start(bf16[16,16,768]{2,1,0:T(8,128)(2,1)} %broadcast_in_dim.84), calls=%async_computation | async-start | bytes 786432 | tf_op jit(solution)/shard_map/all_to_all | solution.py:36
  17.9 9.1 %collective-permute-start = (bf16[128,768]{1,0:T(8,128)(2,1)}, bf16[128,768]{1,0:T(8,128)(2,1)S(1)}, u32[]{:S(2)}, u32[]{:S(2)}) collective-permute-start(bf16[128,768]{1,0:T(8,128)(2,1)} %param.7), channel_id=1, source_target_pairs={{0,64},{64,0},{1,65},{65,1},{2,66},{66,2},{3,67},{67,3},{4,68},{68... | collective-permute-start | bytes 589832 | tf_op jit(solution)/shard_map/ppermute | solution.py:28
  27.0 14.0 %collective-permute-start.1 = (bf16[256,768]{1,0:T(8,128)(2,1)S(1)}, bf16[256,768]{1,0:T(8,128)(2,1)S(1)}, u32[]{:S(2)}, u32[]{:S(2)}) collective-permute-start(bf16[256,768]{1,0:T(8,128)(2,1)S(1)} %constant_dynamic-update-slice_fusion.two_ref), channel_id=1, source_target_pairs={{0,128},{128,256},{256,384},{384,0},{1,129},{129,257},{257,385},{3... | collective-permute-start | bytes 1179656 | tf_op jit(solution)/shard_map/ppermute | solution.py:32
  30.2 10.8 %collective-permute-start.2 = (bf16[256,768]{1,0:T(8,128)(2,1)S(1)}, bf16[256,768]{1,0:T(8,128)(2,1)S(1)}, u32[]{:S(2)}, u32[]{:S(2)}) collective-permute-start(bf16[256,768]{1,0:T(8,128)(2,1)S(1)} %constant_dynamic-update-slice_fusion.two_ref), channel_id=1, source_target_pairs={{0,384},{128,0},{256,128},{384,256},{1,385},{129,1},{257,129},{385... | collective-permute-start | bytes 1179656 | tf_op jit(solution)/shard_map/ppermute | solution.py:32
  33.5 14.9 %collective-permute-start.3 = (bf16[256,768]{1,0:T(8,128)(2,1)S(1)}, bf16[256,768]{1,0:T(8,128)(2,1)S(1)}, u32[]{:S(2)}, u32[]{:S(2)}) collective-permute-start(bf16[256,768]{1,0:T(8,128)(2,1)S(1)} %constant_dynamic-update-slice_fusion.two_ref), channel_id=1, source_target_pairs={{0,256},{128,384},{256,0},{384,128},{1,257},{129,385},{257,1},{385... | collective-permute-start | bytes 1179656 | tf_op jit(solution)/shard_map/ppermute | solution.py:32
  37.1 17.4 %copy-start.5 = (s32[512]{0:T(512)S(1)}, s32[512]{0:T(512)}, u32[]{:S(2)}) copy-start(s32[512]{0:T(512)} %param.10) | copy-start | bytes 6148
  37.1 17.9 %copy-start.4 = (s32[2048]{0:T(1024)S(1)}, s32[2048]{0:T(1024)}, u32[]{:S(2)}) copy-start(s32[2048]{0:T(1024)} %param.11) | copy-start | bytes 24580
  37.1 11.4 %collective-permute-start.4 = (bf16[256,768]{1,0:T(8,128)(2,1)S(1)}, bf16[256,768]{1,0:T(8,128)(2,1)S(1)}, u32[]{:S(2)}, u32[]{:S(2)}) collective-permute-start(bf16[256,768]{1,0:T(8,128)(2,1)S(1)} %bitcast.16), channel_id=1, source_target_pairs={{0,1},{1,0},{2,3},{3,2},{4,5},{5,4},{6,7},{7,6},{8,9},{9,8},{10,11... | collective-permute-start | bytes 1179656 | tf_op jit(solution)/shard_map/ppermute | solution.py:28
  40.3 0.7 copy-start
  48.6 13.9 %collective-permute-start.5 = (bf16[1024,768]{1,0:T(8,128)(2,1)S(1)}, bf16[1024,768]{1,0:T(8,128)(2,1)}, u32[]{:S(2)}, u32[]{:S(2)}) collective-permute-start(bf16[1024,768]{1,0:T(8,128)(2,1)S(1)} %join.1.x_ref.xqa_ref), channel_id=1, source_target_pairs={{0,32},{32,0},{1,33},{33,1},{2,34},{34,2},{3,35},{35,3},{4,36},{36... | collective-permute-start | bytes 4718600 | tf_op jit(solution)/shard_map/ppermute | solution.py:28
  55.2 1.0 copy-start.1
  56.2 1.3 copy-start.3
  62.5 19.8 %copy-start.2 = (bf16[16,16,768]{2,1,0:T(8,128)(2,1)S(1)}, bf16[16,16,768]{2,1,0:T(8,128)(2,1)}, u32[]{:S(2)}) copy-start(bf16[16,16,768]{2,1,0:T(8,128)(2,1)} %copy-done) | copy-start | bytes 1179652
  95.1 4.3 %collective-permute-start.6 = (bf16[384,768]{1,0:T(8,128)(2,1)S(1)}, bf16[384,768]{1,0:T(8,128)(2,1)S(1)}, u32[]{:S(2)}, u32[]{:S(2)}) collective-permute-start(bf16[384,768]{1,0:T(8,128)(2,1)S(1)} %get-tuple-element.34), channel_id=1, source_target_pairs={{0,32},{32,0},{1,33},{33,1},{2,34},{34,2},{3,35},{35,3},{4,36},{36... | collective-permute-start | bytes 1769480 | tf_op jit(solution)/shard_map/ppermute | solution.py:28
  100.4 15.2 %all-to-all-start.2 = ((bf16[16,24,768]{2,1,0:T(8,128)(2,1)}), bf16[16,24,768]{2,1,0:T(8,128)(2,1)S(1)}, u32[]{:S(2)}, u32[]{:S(2)}) async-start(bf16[16,24,768]{2,1,0:T(8,128)(2,1)} %bitcast.5), calls=%async_computation.2 | async-start | bytes 1179648 | tf_op jit(solution)/shard_map/all_to_all | solution.py:36
  104.0 8.3 %collective-permute-start.7 = (f32[8,128]{1,0:T(8,128)S(1)}, f32[8,128]{1,0:T(8,128)S(1)}, u32[]{:S(2)}, u32[]{:S(2)}) collective-permute-start(f32[8,128]{1,0:T(8,128)S(1)} %get-tuple-element.35), channel_id=1, source_target_pairs={{0,1},{1,0},{2,3},{3,2},{4,5},{5,4},{6,7},{7,6},{8,9},{9,8},{10,11... | collective-permute-start | bytes 12296 | tf_op jit(solution)/shard_map/ppermute | solution.py:28
  165.8 8.9 %collective-permute-start.8 = (bf16[384,768]{1,0:T(8,128)(2,1)S(1)}, bf16[384,768]{1,0:T(8,128)(2,1)S(1)}, u32[]{:S(2)}, u32[]{:S(2)}) collective-permute-start(bf16[384,768]{1,0:T(8,128)(2,1)S(1)} %bitcast.22), channel_id=1, source_target_pairs={{0,32},{32,0},{1,33},{33,1},{2,34},{34,2},{3,35},{35,3},{4,36},{36... | collective-permute-start | bytes 1769480 | tf_op jit(solution)/shard_map/ppermute | solution.py:28

commit v7 on v6

--- a/solution.py
+++ b/solution.py
@@ -273,6 +273,7 @@
     picks = order[:, None, None] == q[None, :, None]
     targets = jnp.sum(jnp.where(picks, positives.reshape(1, 16, 128), 0), axis=1).reshape(1, QB)
     block = (y * 2 + xh) * 2 + core
+    weight, near = pltpu.with_memory_space_constraint(weight, pltpu.HBM), pltpu.with_memory_space_constraint(near, pltpu.HBM)
     at = lax.iota(jnp.int32, IB)
     ids = ((at // 16) % 16 * 2 + (xl ^ (at // 256))) * 16 + at % 16
     logs = jnp.log(counts.astype(F32))

time: 177 us -> 176 us (level)
  local copies, waits for them, and re-layouts: 6.42 us -> 3.45 us
    unnamed x13 -> x7, local copies, waits for them, and re-layouts: 3.97 us -> 0.97 us
  transfers between devices with their start and end apart: 11 -> 11, of which waited for: 6 -> 7; matrix products, arithmetic and copies ran while one was open for 2% -> 2% of each run, Pallas kernels for 3% -> 3%
where the time goes in v7:
time: 176 us; the launch traced here: 175 us
  blocking collectives  64.9 us (37%)
  starting transfers between devices  56.3 us (32%)
  Pallas kernels  23.9 us (14%)
  waiting for transfers between devices  21.2 us (12%)
  other arithmetic  4.04 us (2%)
  local copies, waits for them, and re-layouts  3.45 us (2%)
    all_to_all x4, blocking collectives, exchange(): return lax.all_to_all(x, axes, 0, 0, tiled=True)  64.9 us
    ppermute x6, starting transfers between devices, swap(): return lax.ppermute(x, axis, [(0, 1), (1, 0)])  26.8 us
    all_to_all x2, starting transfers between devices, exchange(): return lax.all_to_all(x, axes, 0, 0, tiled=True)  19.3 us
    pallas_call x1, Pallas kernels, grads(): pl.pallas_call(grad_kernel, grid=(QB // CG,), in_specs=[pl.BlockSpec(memo...  12.9 us
    ppermute x6, waiting for transfers between devices, swap(): return lax.ppermute(x, axis, [(0, 1), (1, 0)])  11.2 us
    pallas_call x2, Pallas kernels, score_call(): pl.pallas_call(kernel, grid=(steps,), in_specs=[pl.BlockSpec(memory_space...  10.9 us
    ppermute x3, starting transfers between devices, turn(): return lax.ppermute(x, 'y', [(i, (i + k) % 4) for i in range(4)])  10.1 us
    ppermute x3, waiting for transfers between devices, turn(): return lax.ppermute(x, 'y', [(i, (i + k) % 4) for i in range(4)])  8.07 us
  transfers between devices with their start and end apart: 11, of which 7 were waited for; matrix products, arithmetic and copies ran while one was open for 2% of the time, Pallas kernels for 3%

profile of v7, /device:TPU:1, one launch (start us, length us, event | category | flops | bytes accessed | tf_op | source)
XLA Modules:
  0.0 175.5 jit_solution(14107034753945515029)
XLA Ops:
  0.6 1.5 broadcast_in_dim.84
  2.1 15.7 %all-to-all-start = ((bf16[16,16,768]{2,1,0:T(8,128)(2,1)}), bf16[16,16,768]{2,1,0:T(8,128)(2,1)S(1)}, u32[]{:S(2)}, u32[]{:S(2)}) async-start(bf16[16,16,768]{2,1,0:T(8,128)(2,1)} %broadcast_in_dim.84), calls=%async_computation | async-start | bytes 786432 | tf_op jit(solution)/shard_map/all_to_all | solution.py:36
  17.9 4.7 %collective-permute-start = (bf16[128,768]{1,0:T(8,128)(2,1)}, bf16[128,768]{1,0:T(8,128)(2,1)S(1)}, u32[]{:S(2)}, u32[]{:S(2)}) collective-permute-start(bf16[128,768]{1,0:T(8,128)(2,1)} %param.7), channel_id=1, source_target_pairs={{0,64},{64,0},{1,65},{65,1},{2,66},{66,2},{3,67},{67,3},{4,68},{68... | collective-permute-start | bytes 589832 | tf_op jit(solution)/shard_map/ppermute | solution.py:28
  22.6 1.0 constant_dynamic-update-slice_fusion.1
  23.5 3.4 %collective-permute-done = bf16[128,768]{1,0:T(8,128)(2,1)S(1)} collective-permute-done((bf16[128,768]{1,0:T(8,128)(2,1)}, bf16[128,768]{1,0:T(8,128)(2,1)S(1)}, u32[]{:S(2)}, u32[]{:S(2)}) %collective-permute-start) | collective-permute-done | bytes 196640 | tf_op jit(solution)/shard_map/ppermute | solution.py:28
  27.0 3.2 %collective-permute-start.1 = (bf16[256,768]{1,0:T(8,128)(2,1)S(1)}, bf16[256,768]{1,0:T(8,128)(2,1)S(1)}, u32[]{:S(2)}, u32[]{:S(2)}) collective-permute-start(bf16[256,768]{1,0:T(8,128)(2,1)S(1)} %constant_dynamic-update-slice_fusion.two_ref), channel_id=1, source_target_pairs={{0,128},{128,256},{256,384},{384,0},{1,129},{129,257},{257,385},{3... | collective-permute-start | bytes 1179656 | tf_op jit(solution)/shard_map/ppermute | solution.py:32
  30.2 3.4 %collective-permute-start.2 = (bf16[256,768]{1,0:T(8,128)(2,1)S(1)}, bf16[256,768]{1,0:T(8,128)(2,1)S(1)}, u32[]{:S(2)}, u32[]{:S(2)}) collective-permute-start(bf16[256,768]{1,0:T(8,128)(2,1)S(1)} %constant_dynamic-update-slice_fusion.two_ref), channel_id=1, source_target_pairs={{0,384},{128,0},{256,128},{384,256},{1,385},{129,1},{257,129},{385... | collective-permute-start | bytes 1179656 | tf_op jit(solution)/shard_map/ppermute | solution.py:32
  33.5 3.5 %collective-permute-start.3 = (bf16[256,768]{1,0:T(8,128)(2,1)S(1)}, bf16[256,768]{1,0:T(8,128)(2,1)S(1)}, u32[]{:S(2)}, u32[]{:S(2)}) collective-permute-start(bf16[256,768]{1,0:T(8,128)(2,1)S(1)} %constant_dynamic-update-slice_fusion.two_ref), channel_id=1, source_target_pairs={{0,256},{128,384},{256,0},{384,128},{1,257},{129,385},{257,1},{385... | collective-permute-start | bytes 1179656 | tf_op jit(solution)/shard_map/ppermute | solution.py:32
  37.1 0.0 all-to-all-done
  37.1 0.0 copy-start
  37.1 0.0 copy-start.2
  37.1 0.0 copy-start.1
  37.1 3.3 %collective-permute-start.4 = (bf16[256,768]{1,0:T(8,128)(2,1)S(1)}, bf16[256,768]{1,0:T(8,128)(2,1)S(1)}, u32[]{:S(2)}, u32[]{:S(2)}) collective-permute-start(bf16[256,768]{1,0:T(8,128)(2,1)S(1)} %bitcast.20), channel_id=1, source_target_pairs={{0,1},{1,0},{2,3},{3,2},{4,5},{5,4},{6,7},{7,6},{8,9},{9,8},{10,11... | collective-permute-start | bytes 1179656 | tf_op jit(solution)/shard_map/ppermute | solution.py:28
  40.4 0.0 collective-permute-done.1.a_ref
  40.4 0.1 collective-permute-done.2.b_ref
  40.5 7.9 %collective-permute-done.3.c_ref = bf16[256,768]{1,0:T(8,128)(2,1)S(1)} collective-permute-done((bf16[256,768]{1,0:T(8,128)(2,1)S(1)}, bf16[256,768]{1,0:T(8,128)(2,1)S(1)}, u32[]{:S(2)}, u32[]{:S(2)}) %collective-permute-start.3) | collective-permute-done | bytes 393248 | tf_op jit(solution)/shard_map/ppermute | solution.py:32
  48.5 0.0 copy-done
  48.5 0.0 collective-permute-done.4.after_ref.far_ref
  48.5 0.1 join.1.x_ref.xqa_ref
  48.6 5.8 %collective-permute-start.5 = (bf16[1024,768]{1,0:T(8,128)(2,1)S(1)}, bf16[1024,768]{1,0:T(8,128)(2,1)}, u32[]{:S(2)}, u32[]{:S(2)}) collective-permute-start(bf16[1024,768]{1,0:T(8,128)(2,1)S(1)} %join.1.x_ref.xqa_ref), channel_id=1, source_target_pairs={{0,32},{32,0},{1,33},{33,1},{2,34},{34,2},{3,35},{35,3},{4,36},{36... | collective-permute-start | bytes 4718600 | tf_op jit(solution)/shard_map/ppermute | solution.py:28
  54.5 0.0 copy-done.2
  54.5 0.2 select_reduce_fusion
  54.7 0.2 copy.10.logc_ref
  54.9 0.1 iota_compare_fusion.1
  55.0 0.0 copy-done.1
  55.0 0.1 select_reduce_fusion.1
  55.1 0.1 fusion.11.ids_ref
  55.2 5.8 %score_first.1 = (bf16[1024,768]{1,0:T(8,128)(2,1)S(1)}, f32[1024,1]{1,0:T(8,128)S(1)}, bf16[512,768]{1,0:T(8,128)(2,1)S(1)}, f32[512,1]{1,0:T(8,128)S(1)}, f32[24,128]{1,0:T(8,128)S(1)}) custom-call(s32[16]{0:T(128)S(1)} %fusion.33.order_ref, bf16[1024,768]{1,0:T(8,128)(2,1)S(1)} %join.1.x_ref.xqa_ref, bf16[768,768]{1,0:T(8,128)(2,1)} %w_ref.3, ...), custom_call_target="tpu_custom_call" | custom-call | flops 2013265920 | bytes 6291456 | tf_op jit(solution)/shard_map/score_first/pallas_call | solution.py:132
  61.0 0.0 collective-permute-done.5.x_ref.xqb_ref
  61.1 5.1 %score_second.1 = (bf16[1024,768]{1,0:T(8,128)(2,1)S(1)}, f32[1024,1]{1,0:T(8,128)S(1)}, f32[24,128]{1,0:T(8,128)S(1)}) custom-call(s32[16]{0:T(128)S(1)} %fusion.33.order_ref, bf16[1024,768]{1,0:T(8,128)(2,1)} %collective-permute-done.5.x_ref.xqb_ref, bf16[768,768]{1,0:T(8,128)(2,1)} %w_ref.3, bf16[512,768]{1,0:T(8,128)(2,1)S(1)} %get-tuple-element.25.ei_ref, ...), custom_call_target="tpu_custom_call" | custom-call | flops 2013265920 | bytes 6291456 | tf_op jit(solution)/shard_map/score_second/pallas_call | solution.py:132
  66.2 15.0 %all_to_all.30.parts_ref = f32[16,24,128]{2,1,0:T(8,128)S(1)} all-to-all(f32[16,24,128]{2,1,0:T(8,128)S(1)} %broadcast_in_dim.92), channel_id=1, replica_groups=mesh['y'=4,'xh'=2,'c'=2,'z'=16,'xl'=2] {'y','xh','c'}, dimensions={0} | all-to-all | bytes 393216 | tf_op jit(solution)/shard_map/all_to_all | solution.py:36
  81.2 12.9 %grads.1 = (bf16[384,768]{1,0:T(8,128)(2,1)S(1)}, bf16[384,768]{1,0:T(8,128)(2,1)S(1)}, f32[8,128]{1,0:T(8,128)S(1)}) custom-call(s32[1]{0:T(128)} %bitcast.core_ref, s32[16]{0:T(128)S(1)} %fusion.33.order_ref, f32[16,24,128]{2,1,0:T(8,128)S(1)} %all_to_all.30.parts_ref, bf16[1024,768]{1,0:T(8,128)(2,1)S(1)} %get-tuple-element.28.eqa_ref, ...), custom_call_target="tpu_custom_call" | custom-call | flops 7851737088 | bytes 9437184 | tf_op jit(solution)/shard_map/grads/pallas_call | solution.py:220
  94.1 2.7 %collective-permute-start.6 = (bf16[384,768]{1,0:T(8,128)(2,1)S(1)}, bf16[384,768]{1,0:T(8,128)(2,1)S(1)}, u32[]{:S(2)}, u32[]{:S(2)}) collective-permute-start(bf16[384,768]{1,0:T(8,128)(2,1)S(1)} %get-tuple-element.34), channel_id=1, source_target_pairs={{0,32},{32,0},{1,33},{33,1},{2,34},{34,2},{3,35},{35,3},{4,36},{36... | collective-permute-start | bytes 1769480 | tf_op jit(solution)/shard_map/ppermute | solution.py:28
  96.8 1.6 collective-permute-done.6
  98.4 0.9 add_convert_fusion
  99.4 3.6 %all-to-all-start.2 = ((bf16[16,24,768]{2,1,0:T(8,128)(2,1)}), bf16[16,24,768]{2,1,0:T(8,128)(2,1)S(1)}, u32[]{:S(2)}, u32[]{:S(2)}) async-start(bf16[16,24,768]{2,1,0:T(8,128)(2,1)} %bitcast.5), calls=%async_computation.2 | async-start | bytes 1179648 | tf_op jit(solution)/shard_map/all_to_all | solution.py:36
  103.0 3.1 %collective-permute-start.7 = (f32[8,128]{1,0:T(8,128)S(1)}, f32[8,128]{1,0:T(8,128)S(1)}, u32[]{:S(2)}, u32[]{:S(2)}) collective-permute-start(f32[8,128]{1,0:T(8,128)S(1)} %get-tuple-element.35), channel_id=1, source_target_pairs={{0,1},{1,0},{2,3},{3,2},{4,5},{5,4},{6,7},{7,6},{8,9},{9,8},{10,11... | collective-permute-start | bytes 12296 | tf_op jit(solution)/shard_map/ppermute | solution.py:28
  106.1 5.2 %collective-permute-done.7 = f32[8,128]{1,0:T(8,128)S(1)} collective-permute-done((f32[8,128]{1,0:T(8,128)S(1)}, f32[8,128]{1,0:T(8,128)S(1)}, u32[]{:S(2)}, u32[]{:S(2)}) %collective-permute-start.7) | collective-permute-done | bytes 4128 | tf_op jit(solution)/shard_map/ppermute | solution.py:28
  111.3 0.6 slice.25
  112.6 0.1 maximum_bitcast_fusion
  112.7 1.9 %all-to-all-done.2 = bf16[16,24,768]{2,1,0:T(8,128)(2,1)S(1)} async-done(((bf16[16,24,768]{2,1,0:T(8,128)(2,1)}), bf16[16,24,768]{2,1,0:T(8,128)(2,1)S(1)}, u32[]{:S(2)}, u32[]{:S(2)}) %all-to-all-start.2) | async-done | bytes 589856 | tf_op jit(solution)/shard_map/all_to_all | solution.py:36
  114.6 0.1 reduce_sum.50
  114.7 0.1 reshape.284
  114.8 21.9 %all_to_all.31 = bf16[16,16,128]{2,1,0:T(8,128)(2,1)S(1)} all-to-all(bf16[16,16,128]{2,1,0:T(8,128)(2,1)S(1)} %pad_maximum_fusion), channel_id=1, replica_groups=mesh['y'=4,'xh'=2,'c'=2,'z'=16,'xl'=2] {'z'}, dimensions={0} | all-to-all | bytes 131072 | tf_op jit(solution)/shard_map/all_to_all | solution.py:36
  136.8 14.4 %all_to_all.32 = bf16[16,16,128]{2,1,0:T(8,128)(2,1)S(1)} all-to-all(bf16[16,16,128]{2,1,0:T(8,128)(2,1)S(1)} %broadcast_in_dim.95), channel_id=1, replica_groups=mesh['y'=4,'xh'=2,'c'=2,'z'=16,'xl'=2] {'z'}, dimensions={0} | all-to-all | bytes 131072 | tf_op jit(solution)/shard_map/all_to_all | solution.py:36
  151.2 0.1 broadcast_in_dim.96
  151.3 13.6 %all_to_all.33 = bf16[16,24,768]{2,1,0:T(8,128)(2,1)S(1)} all-to-all(bf16[16,24,768]{2,1,0:T(8,128)(2,1)S(1)} %broadcast_in_dim.97), channel_id=1, replica_groups=mesh['y'=4,'xh'=2,'c'=2,'z'=16,'xl'=2] {'y','xh','xl'}, dimensions={0} | all-to-all | bytes 1179648 | tf_op jit(solution)/shard_map/all_to_all | solution.py:36
  164.9 7.3 %collective-permute-start.8 = (bf16[384,768]{1,0:T(8,128)(2,1)S(1)}, bf16[384,768]{1,0:T(8,128)(2,1)S(1)}, u32[]{:S(2)}, u32[]{:S(2)}) collective-permute-start(bf16[384,768]{1,0:T(8,128)(2,1)S(1)} %bitcast.19), channel_id=1, source_target_pairs={{0,32},{32,0},{1,33},{33,1},{2,34},{34,2},{3,35},{35,3},{4,36},{36... | collective-permute-start | bytes 1769480 | tf_op jit(solution)/shard_map/ppermute | solution.py:28
  172.2 0.6 slice_reduce_fusion
  172.8 1.0 collective-permute-done.8
  173.8 0.1 broadcast_select_fusion.1
  173.9 1.6 maximum_convert_fusion
  (13 shorter events, 0.2 us)
Async XLA Ops:
  2.1 35.0 %all-to-all-start = ((bf16[16,16,768]{2,1,0:T(8,128)(2,1)}), bf16[16,16,768]{2,1,0:T(8,128)(2,1)S(1)}, u32[]{:S(2)}, u32[]{:S(2)}) async-start(bf16[16,16,768]{2,1,0:T(8,128)(2,1)} %broadcast_in_dim.84), calls=%async_computation | async-start | bytes 786432 | tf_op jit(solution)/shard_map/all_to_all | solution.py:36
  17.9 9.1 %collective-permute-start = (bf16[128,768]{1,0:T(8,128)(2,1)}, bf16[128,768]{1,0:T(8,128)(2,1)S(1)}, u32[]{:S(2)}, u32[]{:S(2)}) collective-permute-start(bf16[128,768]{1,0:T(8,128)(2,1)} %param.7), channel_id=1, source_target_pairs={{0,64},{64,0},{1,65},{65,1},{2,66},{66,2},{3,67},{67,3},{4,68},{68... | collective-permute-start | bytes 589832 | tf_op jit(solution)/shard_map/ppermute | solution.py:28
  27.0 13.4 %collective-permute-start.1 = (bf16[256,768]{1,0:T(8,128)(2,1)S(1)}, bf16[256,768]{1,0:T(8,128)(2,1)S(1)}, u32[]{:S(2)}, u32[]{:S(2)}) collective-permute-start(bf16[256,768]{1,0:T(8,128)(2,1)S(1)} %constant_dynamic-update-slice_fusion.two_ref), channel_id=1, source_target_pairs={{0,128},{128,256},{256,384},{384,0},{1,129},{129,257},{257,385},{3... | collective-permute-start | bytes 1179656 | tf_op jit(solution)/shard_map/ppermute | solution.py:32
  30.2 10.4 %collective-permute-start.2 = (bf16[256,768]{1,0:T(8,128)(2,1)S(1)}, bf16[256,768]{1,0:T(8,128)(2,1)S(1)}, u32[]{:S(2)}, u32[]{:S(2)}) collective-permute-start(bf16[256,768]{1,0:T(8,128)(2,1)S(1)} %constant_dynamic-update-slice_fusion.two_ref), channel_id=1, source_target_pairs={{0,384},{128,0},{256,128},{384,256},{1,385},{129,1},{257,129},{385... | collective-permute-start | bytes 1179656 | tf_op jit(solution)/shard_map/ppermute | solution.py:32
  33.5 14.9 %collective-permute-start.3 = (bf16[256,768]{1,0:T(8,128)(2,1)S(1)}, bf16[256,768]{1,0:T(8,128)(2,1)S(1)}, u32[]{:S(2)}, u32[]{:S(2)}) collective-permute-start(bf16[256,768]{1,0:T(8,128)(2,1)S(1)} %constant_dynamic-update-slice_fusion.two_ref), channel_id=1, source_target_pairs={{0,256},{128,384},{256,0},{384,128},{1,257},{129,385},{257,1},{385... | collective-permute-start | bytes 1179656 | tf_op jit(solution)/shard_map/ppermute | solution.py:32
  37.1 11.4 %copy-start = (bf16[16,16,768]{2,1,0:T(8,128)(2,1)}, bf16[16,16,768]{2,1,0:T(8,128)(2,1)S(1)}, u32[]{:S(2)}) copy-start(bf16[16,16,768]{2,1,0:T(8,128)(2,1)S(1)} %all-to-all-done) | copy-start | bytes 1179652
  37.1 17.3 %copy-start.2 = (s32[512]{0:T(512)S(1)}, s32[512]{0:T(512)}, u32[]{:S(2)}) copy-start(s32[512]{0:T(512)} %param.10) | copy-start | bytes 6148
  37.1 17.9 %copy-start.1 = (s32[2048]{0:T(1024)S(1)}, s32[2048]{0:T(1024)}, u32[]{:S(2)}) copy-start(s32[2048]{0:T(1024)} %param.11) | copy-start | bytes 24580
  37.1 11.3 %collective-permute-start.4 = (bf16[256,768]{1,0:T(8,128)(2,1)S(1)}, bf16[256,768]{1,0:T(8,128)(2,1)S(1)}, u32[]{:S(2)}, u32[]{:S(2)}) collective-permute-start(bf16[256,768]{1,0:T(8,128)(2,1)S(1)} %bitcast.20), channel_id=1, source_target_pairs={{0,1},{1,0},{2,3},{3,2},{4,5},{5,4},{6,7},{7,6},{8,9},{9,8},{10,11... | collective-permute-start | bytes 1179656 | tf_op jit(solution)/shard_map/ppermute | solution.py:28
  48.6 12.4 %collective-permute-start.5 = (bf16[1024,768]{1,0:T(8,128)(2,1)S(1)}, bf16[1024,768]{1,0:T(8,128)(2,1)}, u32[]{:S(2)}, u32[]{:S(2)}) collective-permute-start(bf16[1024,768]{1,0:T(8,128)(2,1)S(1)} %join.1.x_ref.xqa_ref), channel_id=1, source_target_pairs={{0,32},{32,0},{1,33},{33,1},{2,34},{34,2},{3,35},{35,3},{4,36},{36... | collective-permute-start | bytes 4718600 | tf_op jit(solution)/shard_map/ppermute | solution.py:28
  94.1 4.3 %collective-permute-start.6 = (bf16[384,768]{1,0:T(8,128)(2,1)S(1)}, bf16[384,768]{1,0:T(8,128)(2,1)S(1)}, u32[]{:S(2)}, u32[]{:S(2)}) collective-permute-start(bf16[384,768]{1,0:T(8,128)(2,1)S(1)} %get-tuple-element.34), channel_id=1, source_target_pairs={{0,32},{32,0},{1,33},{33,1},{2,34},{34,2},{3,35},{35,3},{4,36},{36... | collective-permute-start | bytes 1769480 | tf_op jit(solution)/shard_map/ppermute | solution.py:28
  99.4 15.2 %all-to-all-start.2 = ((bf16[16,24,768]{2,1,0:T(8,128)(2,1)}), bf16[16,24,768]{2,1,0:T(8,128)(2,1)S(1)}, u32[]{:S(2)}, u32[]{:S(2)}) async-start(bf16[16,24,768]{2,1,0:T(8,128)(2,1)} %bitcast.5), calls=%async_computation.2 | async-start | bytes 1179648 | tf_op jit(solution)/shard_map/all_to_all | solution.py:36
  103.0 8.3 %collective-permute-start.7 = (f32[8,128]{1,0:T(8,128)S(1)}, f32[8,128]{1,0:T(8,128)S(1)}, u32[]{:S(2)}, u32[]{:S(2)}) collective-permute-start(f32[8,128]{1,0:T(8,128)S(1)} %get-tuple-element.35), channel_id=1, source_target_pairs={{0,1},{1,0},{2,3},{3,2},{4,5},{5,4},{6,7},{7,6},{8,9},{9,8},{10,11... | collective-permute-start | bytes 12296 | tf_op jit(solution)/shard_map/ppermute | solution.py:28
  164.9 8.9 %collective-permute-start.8 = (bf16[384,768]{1,0:T(8,128)(2,1)S(1)}, bf16[384,768]{1,0:T(8,128)(2,1)S(1)}, u32[]{:S(2)}, u32[]{:S(2)}) collective-permute-start(bf16[384,768]{1,0:T(8,128)(2,1)S(1)} %bitcast.19), channel_id=1, source_target_pairs={{0,32},{32,0},{1,33},{33,1},{2,34},{34,2},{3,35},{35,3},{4,36},{36... | collective-permute-start | bytes 1769480 | tf_op jit(solution)/shard_map/ppermute | solution.py:28

commit v8 on v7

--- a/solution.py
+++ b/solution.py
@@ -57,10 +57,6 @@
     return (proj * inv).astype(BF), inv
 
 
-def score_tile(ei_ref, eq, logc_ref):
-    return 100.0 * dot(ei_ref[...], eq, ((1,), (1,))) - logc_ref[...]
-
-
 def whole(*s):
     return pl.BlockSpec(s, lambda i: (0,) * len(s))
 
@@ -95,10 +91,12 @@
 def score_step(base, order_ref, x_ref, w_ref, ei_ref, logc_ref, ids_ref, tgt_ref, eq_ref, inv_ref, stat_ref):
     eq, inv_ref[...] = unit_rows(x_ref[...], w_ref[...])
     eq_ref[...] = eq
-    scores = score_tile(ei_ref, eq, logc_ref)
-    top = jnp.max(scores, axis=0, keepdims=True)
-    lse = top + jnp.log(jnp.sum(jnp.exp(scores - top), axis=0, keepdims=True))
-    pos = jnp.sum(jnp.where(ids_ref[...] == tgt_ref[...], scores, 0.0), axis=0, keepdims=True)
+    power = dot(ei_ref[...], eq, ((1,), (1,))) * (100.0 * LOG2E) - logc_ref[...] * LOG2E
+    top = jnp.max(power, axis=0, keepdims=True)
+    total = jnp.sum(jnp.exp2(power - top), axis=0, keepdims=True)
+    lse = top * (1.0 / LOG2E) + jnp.log(total)
+    hit = ids_ref[...] == tgt_ref[...]
+    pos = jnp.sum(jnp.where(hit, power, 0.0), axis=0, keepdims=True) * (1.0 / LOG2E)
     for k in range(CH // 128):
         row = order_ref[base + pl.program_id(0) * (CH // 128) + k]
         part = slice(k * 128, (k + 1) * 128)

time: 176 us -> 176 us (level)
  no operation moved by 1% of the time
where the time goes in v8:
time: 176 us; the launch traced here: 175 us
  blocking collectives  64.9 us (37%)
  starting transfers between devices  56.3 us (32%)
  Pallas kernels  23.8 us (14%)
  waiting for transfers between devices  21.2 us (12%)
  other arithmetic  4.04 us (2%)
  local copies, waits for them, and re-layouts  3.45 us (2%)
    all_to_all x4, blocking collectives, exchange(): return lax.all_to_all(x, axes, 0, 0, tiled=True)  64.9 us
    ppermute x6, starting transfers between devices, swap(): return lax.ppermute(x, axis, [(0, 1), (1, 0)])  26.8 us
    all_to_all x2, starting transfers between devices, exchange(): return lax.all_to_all(x, axes, 0, 0, tiled=True)  19.3 us
    pallas_call x1, Pallas kernels, grads(): pl.pallas_call(grad_kernel, grid=(QB // CG,), in_specs=[pl.BlockSpec(memo...  12.9 us
    ppermute x6, waiting for transfers between devices, swap(): return lax.ppermute(x, axis, [(0, 1), (1, 0)])  11.2 us
    pallas_call x2, Pallas kernels, score_call(): pl.pallas_call(kernel, grid=(steps,), in_specs=[pl.BlockSpec(memory_space...  10.8 us
    ppermute x3, starting transfers between devices, turn(): return lax.ppermute(x, 'y', [(i, (i + k) % 4) for i in range(4)])  10.1 us
    ppermute x3, waiting for transfers between devices, turn(): return lax.ppermute(x, 'y', [(i, (i + k) % 4) for i in range(4)])  8.07 us
  transfers between devices with their start and end apart: 11, of which 7 were waited for; matrix products, arithmetic and copies ran while one was open for 2% of the time, Pallas kernels for 3%

profile of v8, /device:TPU:1, one launch (start us, length us, event | category | flops | bytes accessed | tf_op | source)
XLA Modules:
  0.0 175.4 jit_solution(16943576635423841592)
XLA Ops:
  0.6 1.5 broadcast_in_dim.84
  2.1 15.7 %all-to-all-start = ((bf16[16,16,768]{2,1,0:T(8,128)(2,1)}), bf16[16,16,768]{2,1,0:T(8,128)(2,1)S(1)}, u32[]{:S(2)}, u32[]{:S(2)}) async-start(bf16[16,16,768]{2,1,0:T(8,128)(2,1)} %broadcast_in_dim.84), calls=%async_computation | async-start | bytes 786432 | tf_op jit(solution)/shard_map/all_to_all | solution.py:36
  17.9 4.7 %collective-permute-start = (bf16[128,768]{1,0:T(8,128)(2,1)}, bf16[128,768]{1,0:T(8,128)(2,1)S(1)}, u32[]{:S(2)}, u32[]{:S(2)}) collective-permute-start(bf16[128,768]{1,0:T(8,128)(2,1)} %param.7), channel_id=1, source_target_pairs={{0,64},{64,0},{1,65},{65,1},{2,66},{66,2},{3,67},{67,3},{4,68},{68... | collective-permute-start | bytes 589832 | tf_op jit(solution)/shard_map/ppermute | solution.py:28
  22.6 1.0 constant_dynamic-update-slice_fusion.1
  23.5 3.4 %collective-permute-done = bf16[128,768]{1,0:T(8,128)(2,1)S(1)} collective-permute-done((bf16[128,768]{1,0:T(8,128)(2,1)}, bf16[128,768]{1,0:T(8,128)(2,1)S(1)}, u32[]{:S(2)}, u32[]{:S(2)}) %collective-permute-start) | collective-permute-done | bytes 196640 | tf_op jit(solution)/shard_map/ppermute | solution.py:28
  27.0 3.2 %collective-permute-start.1 = (bf16[256,768]{1,0:T(8,128)(2,1)S(1)}, bf16[256,768]{1,0:T(8,128)(2,1)S(1)}, u32[]{:S(2)}, u32[]{:S(2)}) collective-permute-start(bf16[256,768]{1,0:T(8,128)(2,1)S(1)} %constant_dynamic-update-slice_fusion.two_ref), channel_id=1, source_target_pairs={{0,128},{128,256},{256,384},{384,0},{1,129},{129,257},{257,385},{3... | collective-permute-start | bytes 1179656 | tf_op jit(solution)/shard_map/ppermute | solution.py:32
  30.2 3.4 %collective-permute-start.2 = (bf16[256,768]{1,0:T(8,128)(2,1)S(1)}, bf16[256,768]{1,0:T(8,128)(2,1)S(1)}, u32[]{:S(2)}, u32[]{:S(2)}) collective-permute-start(bf16[256,768]{1,0:T(8,128)(2,1)S(1)} %constant_dynamic-update-slice_fusion.two_ref), channel_id=1, source_target_pairs={{0,384},{128,0},{256,128},{384,256},{1,385},{129,1},{257,129},{385... | collective-permute-start | bytes 1179656 | tf_op jit(solution)/shard_map/ppermute | solution.py:32
  33.5 3.5 %collective-permute-start.3 = (bf16[256,768]{1,0:T(8,128)(2,1)S(1)}, bf16[256,768]{1,0:T(8,128)(2,1)S(1)}, u32[]{:S(2)}, u32[]{:S(2)}) collective-permute-start(bf16[256,768]{1,0:T(8,128)(2,1)S(1)} %constant_dynamic-update-slice_fusion.two_ref), channel_id=1, source_target_pairs={{0,256},{128,384},{256,0},{384,128},{1,257},{129,385},{257,1},{385... | collective-permute-start | bytes 1179656 | tf_op jit(solution)/shard_map/ppermute | solution.py:32
  37.1 0.0 all-to-all-done
  37.1 0.0 copy-start
  37.1 0.0 copy-start.2
  37.1 0.0 copy-start.1
  37.1 3.3 %collective-permute-start.4 = (bf16[256,768]{1,0:T(8,128)(2,1)S(1)}, bf16[256,768]{1,0:T(8,128)(2,1)S(1)}, u32[]{:S(2)}, u32[]{:S(2)}) collective-permute-start(bf16[256,768]{1,0:T(8,128)(2,1)S(1)} %bitcast.20), channel_id=1, source_target_pairs={{0,1},{1,0},{2,3},{3,2},{4,5},{5,4},{6,7},{7,6},{8,9},{9,8},{10,11... | collective-permute-start | bytes 1179656 | tf_op jit(solution)/shard_map/ppermute | solution.py:28
  40.4 0.0 collective-permute-done.1.a_ref
  40.4 0.1 collective-permute-done.2.b_ref
  40.5 7.9 %collective-permute-done.3.c_ref = bf16[256,768]{1,0:T(8,128)(2,1)S(1)} collective-permute-done((bf16[256,768]{1,0:T(8,128)(2,1)S(1)}, bf16[256,768]{1,0:T(8,128)(2,1)S(1)}, u32[]{:S(2)}, u32[]{:S(2)}) %collective-permute-start.3) | collective-permute-done | bytes 393248 | tf_op jit(solution)/shard_map/ppermute | solution.py:32
  48.5 0.0 copy-done
  48.5 0.0 collective-permute-done.4.after_ref.far_ref
  48.5 0.1 join.1.x_ref.xqa_ref
  48.6 5.8 %collective-permute-start.5 = (bf16[1024,768]{1,0:T(8,128)(2,1)S(1)}, bf16[1024,768]{1,0:T(8,128)(2,1)}, u32[]{:S(2)}, u32[]{:S(2)}) collective-permute-start(bf16[1024,768]{1,0:T(8,128)(2,1)S(1)} %join.1.x_ref.xqa_ref), channel_id=1, source_target_pairs={{0,32},{32,0},{1,33},{33,1},{2,34},{34,2},{3,35},{35,3},{4,36},{36... | collective-permute-start | bytes 4718600 | tf_op jit(solution)/shard_map/ppermute | solution.py:28
  54.5 0.0 copy-done.2
  54.5 0.2 select_reduce_fusion
  54.7 0.2 copy.10.logc_ref
  54.9 0.1 iota_compare_fusion.1
  55.0 0.0 copy-done.1
  55.0 0.1 select_reduce_fusion.1
  55.1 0.1 fusion.11.ids_ref
  55.2 5.8 %score_first.1 = (bf16[1024,768]{1,0:T(8,128)(2,1)S(1)}, f32[1024,1]{1,0:T(8,128)S(1)}, bf16[512,768]{1,0:T(8,128)(2,1)S(1)}, f32[512,1]{1,0:T(8,128)S(1)}, f32[24,128]{1,0:T(8,128)S(1)}) custom-call(s32[16]{0:T(128)S(1)} %fusion.33.order_ref, bf16[1024,768]{1,0:T(8,128)(2,1)S(1)} %join.1.x_ref.xqa_ref, bf16[768,768]{1,0:T(8,128)(2,1)} %w_ref.3, ...), custom_call_target="tpu_custom_call" | custom-call | flops 2013265920 | bytes 6291456 | tf_op jit(solution)/shard_map/score_first/pallas_call | solution.py:130
  61.0 0.0 collective-permute-done.5.x_ref.xqb_ref
  61.0 5.0 %score_second.1 = (bf16[1024,768]{1,0:T(8,128)(2,1)S(1)}, f32[1024,1]{1,0:T(8,128)S(1)}, f32[24,128]{1,0:T(8,128)S(1)}) custom-call(s32[16]{0:T(128)S(1)} %fusion.33.order_ref, bf16[1024,768]{1,0:T(8,128)(2,1)} %collective-permute-done.5.x_ref.xqb_ref, bf16[768,768]{1,0:T(8,128)(2,1)} %w_ref.3, bf16[512,768]{1,0:T(8,128)(2,1)S(1)} %get-tuple-element.25.ei_ref, ...), custom_call_target="tpu_custom_call" | custom-call | flops 2013265920 | bytes 6291456 | tf_op jit(solution)/shard_map/score_second/pallas_call | solution.py:130
  66.1 15.0 %all_to_all.30.parts_ref = f32[16,24,128]{2,1,0:T(8,128)S(1)} all-to-all(f32[16,24,128]{2,1,0:T(8,128)S(1)} %broadcast_in_dim.92), channel_id=1, replica_groups=mesh['y'=4,'xh'=2,'c'=2,'z'=16,'xl'=2] {'y','xh','c'}, dimensions={0} | all-to-all | bytes 393216 | tf_op jit(solution)/shard_map/all_to_all | solution.py:36
  81.1 12.9 %grads.1 = (bf16[384,768]{1,0:T(8,128)(2,1)S(1)}, bf16[384,768]{1,0:T(8,128)(2,1)S(1)}, f32[8,128]{1,0:T(8,128)S(1)}) custom-call(s32[1]{0:T(128)} %bitcast.core_ref, s32[16]{0:T(128)S(1)} %fusion.33.order_ref, f32[16,24,128]{2,1,0:T(8,128)S(1)} %all_to_all.30.parts_ref, bf16[1024,768]{1,0:T(8,128)(2,1)S(1)} %get-tuple-element.28.eqa_ref, ...), custom_call_target="tpu_custom_call" | custom-call | flops 7851737088 | bytes 9437184 | tf_op jit(solution)/shard_map/grads/pallas_call | solution.py:218
  94.0 2.7 %collective-permute-start.6 = (bf16[384,768]{1,0:T(8,128)(2,1)S(1)}, bf16[384,768]{1,0:T(8,128)(2,1)S(1)}, u32[]{:S(2)}, u32[]{:S(2)}) collective-permute-start(bf16[384,768]{1,0:T(8,128)(2,1)S(1)} %get-tuple-element.34), channel_id=1, source_target_pairs={{0,32},{32,0},{1,33},{33,1},{2,34},{34,2},{3,35},{35,3},{4,36},{36... | collective-permute-start | bytes 1769480 | tf_op jit(solution)/shard_map/ppermute | solution.py:28
  96.7 1.6 collective-permute-done.6
  98.4 0.9 add_convert_fusion
  99.3 3.6 %all-to-all-start.2 = ((bf16[16,24,768]{2,1,0:T(8,128)(2,1)}), bf16[16,24,768]{2,1,0:T(8,128)(2,1)S(1)}, u32[]{:S(2)}, u32[]{:S(2)}) async-start(bf16[16,24,768]{2,1,0:T(8,128)(2,1)} %bitcast.5), calls=%async_computation.2 | async-start | bytes 1179648 | tf_op jit(solution)/shard_map/all_to_all | solution.py:36
  102.9 3.1 %collective-permute-start.7 = (f32[8,128]{1,0:T(8,128)S(1)}, f32[8,128]{1,0:T(8,128)S(1)}, u32[]{:S(2)}, u32[]{:S(2)}) collective-permute-start(f32[8,128]{1,0:T(8,128)S(1)} %get-tuple-element.35), channel_id=1, source_target_pairs={{0,1},{1,0},{2,3},{3,2},{4,5},{5,4},{6,7},{7,6},{8,9},{9,8},{10,11... | collective-permute-start | bytes 12296 | tf_op jit(solution)/shard_map/ppermute | solution.py:28
  106.0 5.2 %collective-permute-done.7 = f32[8,128]{1,0:T(8,128)S(1)} collective-permute-done((f32[8,128]{1,0:T(8,128)S(1)}, f32[8,128]{1,0:T(8,128)S(1)}, u32[]{:S(2)}, u32[]{:S(2)}) %collective-permute-start.7) | collective-permute-done | bytes 4128 | tf_op jit(solution)/shard_map/ppermute | solution.py:28
  111.2 0.6 slice.25
  112.6 0.1 maximum_bitcast_fusion
  112.6 1.9 %all-to-all-done.2 = bf16[16,24,768]{2,1,0:T(8,128)(2,1)S(1)} async-done(((bf16[16,24,768]{2,1,0:T(8,128)(2,1)}), bf16[16,24,768]{2,1,0:T(8,128)(2,1)S(1)}, u32[]{:S(2)}, u32[]{:S(2)}) %all-to-all-start.2) | async-done | bytes 589856 | tf_op jit(solution)/shard_map/all_to_all | solution.py:36
  114.6 0.1 reduce_sum.50
  114.6 0.1 reshape.284
  114.8 21.9 %all_to_all.31 = bf16[16,16,128]{2,1,0:T(8,128)(2,1)S(1)} all-to-all(bf16[16,16,128]{2,1,0:T(8,128)(2,1)S(1)} %pad_maximum_fusion), channel_id=1, replica_groups=mesh['y'=4,'xh'=2,'c'=2,'z'=16,'xl'=2] {'z'}, dimensions={0} | all-to-all | bytes 131072 | tf_op jit(solution)/shard_map/all_to_all | solution.py:36
  136.7 14.4 %all_to_all.32 = bf16[16,16,128]{2,1,0:T(8,128)(2,1)S(1)} all-to-all(bf16[16,16,128]{2,1,0:T(8,128)(2,1)S(1)} %broadcast_in_dim.95), channel_id=1, replica_groups=mesh['y'=4,'xh'=2,'c'=2,'z'=16,'xl'=2] {'z'}, dimensions={0} | all-to-all | bytes 131072 | tf_op jit(solution)/shard_map/all_to_all | solution.py:36
  151.1 0.1 broadcast_in_dim.96
  151.2 13.6 %all_to_all.33 = bf16[16,24,768]{2,1,0:T(8,128)(2,1)S(1)} all-to-all(bf16[16,24,768]{2,1,0:T(8,128)(2,1)S(1)} %broadcast_in_dim.97), channel_id=1, replica_groups=mesh['y'=4,'xh'=2,'c'=2,'z'=16,'xl'=2] {'y','xh','xl'}, dimensions={0} | all-to-all | bytes 1179648 | tf_op jit(solution)/shard_map/all_to_all | solution.py:36
  164.8 7.3 %collective-permute-start.8 = (bf16[384,768]{1,0:T(8,128)(2,1)S(1)}, bf16[384,768]{1,0:T(8,128)(2,1)S(1)}, u32[]{:S(2)}, u32[]{:S(2)}) collective-permute-start(bf16[384,768]{1,0:T(8,128)(2,1)S(1)} %bitcast.19), channel_id=1, source_target_pairs={{0,32},{32,0},{1,33},{33,1},{2,34},{34,2},{3,35},{35,3},{4,36},{36... | collective-permute-start | bytes 1769480 | tf_op jit(solution)/shard_map/ppermute | solution.py:28
  172.1 0.6 slice_reduce_fusion
  172.7 1.0 collective-permute-done.8
  173.7 0.1 broadcast_select_fusion.1
  173.8 1.6 maximum_convert_fusion
  (13 shorter events, 0.2 us)
Async XLA Ops:
  2.1 35.0 %all-to-all-start = ((bf16[16,16,768]{2,1,0:T(8,128)(2,1)}), bf16[16,16,768]{2,1,0:T(8,128)(2,1)S(1)}, u32[]{:S(2)}, u32[]{:S(2)}) async-start(bf16[16,16,768]{2,1,0:T(8,128)(2,1)} %broadcast_in_dim.84), calls=%async_computation | async-start | bytes 786432 | tf_op jit(solution)/shard_map/all_to_all | solution.py:36
  17.9 9.1 %collective-permute-start = (bf16[128,768]{1,0:T(8,128)(2,1)}, bf16[128,768]{1,0:T(8,128)(2,1)S(1)}, u32[]{:S(2)}, u32[]{:S(2)}) collective-permute-start(bf16[128,768]{1,0:T(8,128)(2,1)} %param.7), channel_id=1, source_target_pairs={{0,64},{64,0},{1,65},{65,1},{2,66},{66,2},{3,67},{67,3},{4,68},{68... | collective-permute-start | bytes 589832 | tf_op jit(solution)/shard_map/ppermute | solution.py:28
  27.0 13.4 %collective-permute-start.1 = (bf16[256,768]{1,0:T(8,128)(2,1)S(1)}, bf16[256,768]{1,0:T(8,128)(2,1)S(1)}, u32[]{:S(2)}, u32[]{:S(2)}) collective-permute-start(bf16[256,768]{1,0:T(8,128)(2,1)S(1)} %constant_dynamic-update-slice_fusion.two_ref), channel_id=1, source_target_pairs={{0,128},{128,256},{256,384},{384,0},{1,129},{129,257},{257,385},{3... | collective-permute-start | bytes 1179656 | tf_op jit(solution)/shard_map/ppermute | solution.py:32
  30.2 10.4 %collective-permute-start.2 = (bf16[256,768]{1,0:T(8,128)(2,1)S(1)}, bf16[256,768]{1,0:T(8,128)(2,1)S(1)}, u32[]{:S(2)}, u32[]{:S(2)}) collective-permute-start(bf16[256,768]{1,0:T(8,128)(2,1)S(1)} %constant_dynamic-update-slice_fusion.two_ref), channel_id=1, source_target_pairs={{0,384},{128,0},{256,128},{384,256},{1,385},{129,1},{257,129},{385... | collective-permute-start | bytes 1179656 | tf_op jit(solution)/shard_map/ppermute | solution.py:32
  33.5 14.9 %collective-permute-start.3 = (bf16[256,768]{1,0:T(8,128)(2,1)S(1)}, bf16[256,768]{1,0:T(8,128)(2,1)S(1)}, u32[]{:S(2)}, u32[]{:S(2)}) collective-permute-start(bf16[256,768]{1,0:T(8,128)(2,1)S(1)} %constant_dynamic-update-slice_fusion.two_ref), channel_id=1, source_target_pairs={{0,256},{128,384},{256,0},{384,128},{1,257},{129,385},{257,1},{385... | collective-permute-start | bytes 1179656 | tf_op jit(solution)/shard_map/ppermute | solution.py:32
  37.1 11.4 %copy-start = (bf16[16,16,768]{2,1,0:T(8,128)(2,1)}, bf16[16,16,768]{2,1,0:T(8,128)(2,1)S(1)}, u32[]{:S(2)}) copy-start(bf16[16,16,768]{2,1,0:T(8,128)(2,1)S(1)} %all-to-all-done) | copy-start | bytes 1179652
  37.1 17.3 %copy-start.2 = (s32[512]{0:T(512)S(1)}, s32[512]{0:T(512)}, u32[]{:S(2)}) copy-start(s32[512]{0:T(512)} %param.10) | copy-start | bytes 6148
  37.1 17.9 %copy-start.1 = (s32[2048]{0:T(1024)S(1)}, s32[2048]{0:T(1024)}, u32[]{:S(2)}) copy-start(s32[2048]{0:T(1024)} %param.11) | copy-start | bytes 24580
  37.1 11.3 %collective-permute-start.4 = (bf16[256,768]{1,0:T(8,128)(2,1)S(1)}, bf16[256,768]{1,0:T(8,128)(2,1)S(1)}, u32[]{:S(2)}, u32[]{:S(2)}) collective-permute-start(bf16[256,768]{1,0:T(8,128)(2,1)S(1)} %bitcast.20), channel_id=1, source_target_pairs={{0,1},{1,0},{2,3},{3,2},{4,5},{5,4},{6,7},{7,6},{8,9},{9,8},{10,11... | collective-permute-start | bytes 1179656 | tf_op jit(solution)/shard_map/ppermute | solution.py:28
  48.6 12.4 %collective-permute-start.5 = (bf16[1024,768]{1,0:T(8,128)(2,1)S(1)}, bf16[1024,768]{1,0:T(8,128)(2,1)}, u32[]{:S(2)}, u32[]{:S(2)}) collective-permute-start(bf16[1024,768]{1,0:T(8,128)(2,1)S(1)} %join.1.x_ref.xqa_ref), channel_id=1, source_target_pairs={{0,32},{32,0},{1,33},{33,1},{2,34},{34,2},{3,35},{35,3},{4,36},{36... | collective-permute-start | bytes 4718600 | tf_op jit(solution)/shard_map/ppermute | solution.py:28
  94.0 4.3 %collective-permute-start.6 = (bf16[384,768]{1,0:T(8,128)(2,1)S(1)}, bf16[384,768]{1,0:T(8,128)(2,1)S(1)}, u32[]{:S(2)}, u32[]{:S(2)}) collective-permute-start(bf16[384,768]{1,0:T(8,128)(2,1)S(1)} %get-tuple-element.34), channel_id=1, source_target_pairs={{0,32},{32,0},{1,33},{33,1},{2,34},{34,2},{3,35},{35,3},{4,36},{36... | collective-permute-start | bytes 1769480 | tf_op jit(solution)/shard_map/ppermute | solution.py:28
  99.3 15.2 %all-to-all-start.2 = ((bf16[16,24,768]{2,1,0:T(8,128)(2,1)}), bf16[16,24,768]{2,1,0:T(8,128)(2,1)S(1)}, u32[]{:S(2)}, u32[]{:S(2)}) async-start(bf16[16,24,768]{2,1,0:T(8,128)(2,1)} %bitcast.5), calls=%async_computation.2 | async-start | bytes 1179648 | tf_op jit(solution)/shard_map/all_to_all | solution.py:36
  102.9 8.3 %collective-permute-start.7 = (f32[8,128]{1,0:T(8,128)S(1)}, f32[8,128]{1,0:T(8,128)S(1)}, u32[]{:S(2)}, u32[]{:S(2)}) collective-permute-start(f32[8,128]{1,0:T(8,128)S(1)} %get-tuple-element.35), channel_id=1, source_target_pairs={{0,1},{1,0},{2,3},{3,2},{4,5},{5,4},{6,7},{7,6},{8,9},{9,8},{10,11... | collective-permute-start | bytes 12296 | tf_op jit(solution)/shard_map/ppermute | solution.py:28
  164.8 8.9 %collective-permute-start.8 = (bf16[384,768]{1,0:T(8,128)(2,1)S(1)}, bf16[384,768]{1,0:T(8,128)(2,1)S(1)}, u32[]{:S(2)}, u32[]{:S(2)}) collective-permute-start(bf16[384,768]{1,0:T(8,128)(2,1)S(1)} %bitcast.19), channel_id=1, source_target_pairs={{0,32},{32,0},{1,33},{33,1},{2,34},{34,2},{3,35},{35,3},{4,36},{36... | collective-permute-start | bytes 1769480 | tf_op jit(solution)/shard_map/ppermute | solution.py:28
